TPU v7x, 32 devices: a whole 2x2x4 slice. The times are simulated.
32 devices in a mesh: dp: 4 (over y, x), peak: 4 (over z), mod: 2 (over core).
Axes of the slice: x: 2, y: 2, z: 4, core: 2. Of those that a mesh axis runs over, the one named last changes fastest.
Arguments:
- hidden_in: bfloat16 [2, 3072, 1024], P('mod', ('dp', 'peak')), parts along dimension 1, may hold values from -31 to 31
- value_bins: int32 [2, 3072], P('mod', ('dp', 'peak')), parts along dimension 1, may hold values from 0 to 50
- mask_flags: int32 [2, 3072], P('mod', ('dp', 'peak')), parts along dimension 1, may hold values 0 or 1
- segment_ids: int32 [2, 16, 192], P('mod', ('dp', 'peak')), parts along dimension 1, may hold values from 0 to 3, never falling along the last dimension, each value on 1 to 96 neighbouring positions
- bin_table: bfloat16 [2, 51, 1024], P('mod'), may hold values from -3 to 3
- mask_vector: bfloat16 [2, 1024], P('mod'), may hold values from -4 to 4
- qkv_weight: bfloat16 [1024, 3072], P('mod'), may hold values from -1 to 1
- out_weight: bfloat16 [1024, 1024], P('mod'), may hold values from -1.5 to 1.5
Outputs:
- update: bfloat16 [2, 3072, 1024], P('mod', ('dp', 'peak')), parts along dimension 1
There are 4 independent parts, one for each index of `dp`. A program takes and returns all parts, laid end to end along the dimension named above; an argument that names none is the same for every part. Nothing has to cross between parts.
Inputs may be any that keep to these rules, and one draw needn't show every extreme that they name: `segment_ids`: in each block of 192 tokens the segments 0 to 3 follow in order, each of 1 to 96 tokens, one of exactly 96.
All inputs are finite; a program needn't handle non-finite values. No bound on the sum of `mask_flags` on one device may be relied on, other than what follows from the above.
Results may differ from a plain program's by a relative error of at most 0.01205.
The roundings to bfloat16 on the way count: a program that leaves them out, or rounds other values in their place, can miss the bound.
Values may be sent and summed in bfloat16 or wider, within the bound.
No kernel may reach another device: no remote copies, remote signals or barrier semaphores. Data moves between devices by JAX's collectives and lax.ppermute only.
A program may use at most 128 MiB of HBM per device.

v0:
```python
import math

import jax
import jax.numpy as jnp
from jax import lax
from jax.sharding import PartitionSpec as P

H = 16
NBINS = 51
SEG_DEV = 4


def from_partner(value, axis, bit):
    mask = 2**bit
    pairs = [(source, source ^ mask) for source in range(lax.axis_size(axis))]
    return lax.ppermute(value, axis, pairs)


def attend_block(running, queries, key_block, value_block, score_bias, score_scale):
    row_max, denominator, numerator = running
    scores = (
        jnp.einsum("thd,khd->thk", queries, key_block, preferred_element_type=jnp.float32)
        * score_scale
        + score_bias
    )
    new_max = jnp.maximum(row_max, jnp.max(scores, axis=2))
    correction = jnp.exp(row_max - new_max)
    weights = jnp.exp(scores - new_max[:, :, None])
    denominator = denominator * correction + jnp.sum(weights, axis=2)
    numerator = numerator * correction[:, :, None] + jnp.einsum(
        "thk,khd->thd",
        weights.astype(jnp.bfloat16),
        value_block,
        preferred_element_type=jnp.float32,
    )
    return (new_max, denominator, numerator)


def shards(
    hidden_in, value_bins, mask_flags, segment_ids, bin_table, mask_vector, qkv_weight, out_weight
):
    tok_count = hidden_in.shape[1]
    width = hidden_in.shape[2]
    head_count = H
    head_size = width // head_count
    score_scale = float(head_size) ** (-0.5)
    selector = (value_bins[0][:, None] == jnp.arange(NBINS, dtype=jnp.int32)[None, :]).astype(
        jnp.bfloat16
    )
    bin_rows = jnp.dot(selector, bin_table[0], preferred_element_type=jnp.float32)
    chosen = jnp.where(
        mask_flags[0][:, None] == 1,
        mask_vector[0][None, :].astype(jnp.float32),
        hidden_in[0].astype(jnp.float32),
    )
    embedded = (chosen + bin_rows).astype(jnp.bfloat16)
    columns = embedded
    projected = jnp.dot(
        columns,
        lax.all_gather(qkv_weight, "mod", axis=0, tiled=True),
        preferred_element_type=jnp.float32,
    )
    projected = projected.astype(jnp.bfloat16).reshape(tok_count, head_count, 3, head_size)
    key_values = projected[:, :, 1:3, :].reshape(tok_count, 2 * width)
    seg_select = (
        segment_ids[0, 0][None, :] == jnp.arange(SEG_DEV, dtype=jnp.int32)[:, None]
    ).astype(jnp.bfloat16)
    pooled_sums = jnp.dot(seg_select, key_values, preferred_element_type=jnp.float32)
    counts = jnp.sum(seg_select.astype(jnp.float32), axis=1)
    pooled = (pooled_sums / counts[:, None]).astype(jnp.bfloat16)
    pool_bias = jnp.broadcast_to(
        jnp.log(counts).astype(jnp.bfloat16)[:, None], (SEG_DEV, head_count)
    )
    partner_kv, partner_bias = from_partner((pooled, pool_bias), "mod", 0)
    queries = projected[:, :, 0, :]
    start_state = (
        jnp.full((tok_count, head_count), -1e30, jnp.float32),
        jnp.zeros((tok_count, head_count), jnp.float32),
        jnp.zeros((tok_count, head_count, head_size), jnp.float32),
    )

    def fold_tokens(running, portion):
        row_count = portion.shape[0]
        unpacked = portion.reshape(row_count, head_count, 2, head_size)
        if row_count <= 1024:
            return attend_block(
                running, queries, unpacked[:, :, 0], unpacked[:, :, 1], 0.0, score_scale
            )
        block_size = math.gcd(row_count, 512)

        def one_step(index, state):
            sliced = lax.dynamic_slice_in_dim(unpacked, index * block_size, block_size, 0)
            return attend_block(state, queries, sliced[:, :, 0], sliced[:, :, 1], 0.0, score_scale)

        return lax.fori_loop(0, row_count // block_size, one_step, running)

    running = fold_tokens(start_state, lax.all_gather(key_values, "peak", axis=0, tiled=True))
    kv_part = lax.all_gather(partner_kv, "peak", axis=0, tiled=True)
    bias_part = lax.all_gather(partner_bias, "peak", axis=0, tiled=True)
    row_count = kv_part.shape[0]
    unpacked = kv_part.reshape(row_count, head_count, 2, head_size)
    score_bias = jnp.transpose(bias_part.astype(jnp.float32))[None, :, :]
    row_max, denominator, numerator = attend_block(
        running, queries, unpacked[:, :, 0], unpacked[:, :, 1], score_bias, score_scale
    )
    attended = (numerator / denominator[:, :, None]).astype(jnp.bfloat16).reshape(tok_count, width)
    columns = attended
    result = jnp.dot(
        columns,
        lax.all_gather(out_weight, "mod", axis=0, tiled=True),
        preferred_element_type=jnp.float32,
    )
    return result.astype(jnp.bfloat16).reshape(1, tok_count, width)


def solution(mesh):
    placed = (
        P("mod", ("dp", "peak"), None),
        P("mod", ("dp", "peak")),
        P("mod", ("dp", "peak")),
        P("mod", ("dp", "peak"), None),
        P("mod", None, None),
        P("mod", None),
        P("mod", None),
        P("mod", None),
    )
    return jax.shard_map(
        shards,
        mesh=mesh,
        in_specs=placed,
        out_specs=P("mod", ("dp", "peak"), None),
        check_vma=False,
    )
```

profile of v0, /device:TPU:0, one launch (start us, length us, event | category | flops | bytes accessed | tf_op | source)
XLA Modules:
  0.0 121.6 jit_solution(3393369843755317250)
XLA Ops:
  6.5 0.0 copy-start
  6.5 0.0 all-gather.6.cloned.1.call-start
  6.5 0.7 all-gather.6.cloned.1.call-update
  7.3 0.0 all-gather.8.cloned.1.call-start
  7.3 0.7 broadcast_in_dim.50
  8.0 0.7 compare_reduce_fusion
  8.7 19.7 %all-gather.6.cloned.1.call-done = bf16[1024,3072]{1,0:T(8,128)(2,1)} async-done(((bf16[512,3072]{1,0:T(8,128)(2,1)}), bf16[1024,3072]{1,0:T(8,128)(2,1)}) %all-gather.6.cloned.1.call-update) | async-done | bytes 6291472 | tf_op jit(solution)/shard_map/all_gather | solution.py:60
  28.4 0.0 copy-done
  28.4 4.5 %convolution_convert_fusion = bf16[192,3072]{1,0:T(8,128)(2,1)S(1)} fusion(bf16[1024,3072]{1,0:T(8,128)(2,1)} %all-gather.6.cloned.1.call-done, bf16[1,192,1024]{2,1,0:T(8,128)(2,1)} %param.8, f32[1024]{0:T(1024)S(1)} %bitcast.107, pred[192]{0:T(512)(128)(4,1)S(1)} %compare_reduce_fusion, bf16[1,51,1024]{2,1,0:T(8,128)(2,1)S(1)} %copy-done, s32[192]{0:T(256)} %bitcast.111), kind=kOutput, calls=%fused_computation.8 | convolution fusion | flops 1229399552 | bytes 7973824 | tf_op jit(solution)/shard_map/dot_general | solution.py:58
  32.9 0.0 copy-start.3
  32.9 0.7 copy.36
  33.6 0.0 copy-start.1
  33.6 0.1 slice.24
  33.7 1.3 %copy.37 = bf16[192,2048]{1,0:T(8,128)(2,1)} copy(bf16[192,2048]{0,1:T(8,128)(2,1)S(1)} %bitcast.98) | data formatting | bytes 1572864 | tf_op jit(solution)/shard_map/reshape | solution.py:64
  35.1 0.0 all-gather.8.cloned.1.call-update
  35.1 0.0 all-gather.10.cloned.1.call-start
  35.1 0.0 copy-done.3
  35.1 0.1 convert_reduce_fusion
  35.3 0.4 fusion.7
  35.6 0.2 collective-permute-start
  35.8 0.1 broadcast_in_dim.49
  35.9 0.3 collective-permute-start.1
  36.2 0.0 all-gather.10.cloned.1.call-update
  36.2 0.8 collective-permute-done.1
  37.1 11.2 %all-gather.1 = bf16[4,4,16]{2,1,0:T(4,128)(2,1)S(1)} all-gather(bf16[1,4,16]{2,1,0:T(4,128)(2,1)S(1)} %bitcast.110), channel_id=1, replica_groups=mesh['dp'=4,'peak'=4,'mod'=2] {'peak'}, dimensions={0}, use_global_device_ids=true | all-gather | bytes 640 | tf_op jit(solution)/shard_map/all_gather | solution.py:99
  48.3 0.1 copy.43
  48.4 0.0 collective-permute-done
  48.4 13.6 %all-gather = bf16[4,4,2048]{2,1,0:T(4,128)(2,1)S(1)} all-gather(bf16[1,4,2048]{2,1,0:T(4,128)(2,1)S(1)} %bitcast.105), channel_id=1, replica_groups=mesh['dp'=4,'peak'=4,'mod'=2] {'peak'}, dimensions={0}, use_global_device_ids=true | all-gather | bytes 81920 | tf_op jit(solution)/shard_map/all_gather | solution.py:98
  62.0 0.2 reshape.70
  62.1 0.8 fusion.40
  63.0 0.2 fusion.41
  63.2 0.0 copy-done.1
  63.2 37.6 %all-gather.8.cloned.1.call-done = bf16[768,2048]{1,0:T(8,128)(2,1)} async-done(((bf16[192,2048]{1,0:T(8,128)(2,1)}), bf16[768,2048]{1,0:T(8,128)(2,1)}) %all-gather.8.cloned.1.call-update) | async-done | bytes 3145744 | tf_op jit(solution)/shard_map/all_gather | solution.py:97
  100.8 3.2 %copy.38 = bf16[768,2048]{0,1:T(8,128)(2,1)S(1)} copy(bf16[768,2048]{1,0:T(8,128)(2,1)} %all-gather.8.cloned.1.call-done) | data formatting | bytes 6291456 | tf_op jit(solution)/shard_map/all_gather | solution.py:97
  104.0 2.6 %bitcast_reduce_fusion = (f32[192,16]{0,1:T(8,128)S(1)}, f32[16,768,192]{1,2,0:T(8,128)S(1)}) fusion(bf16[192,16,3,64]{0,3,2,1:T(8,128)(2,1)} %bitcast.102, bf16[768,16,2,64]{0,3,2,1:T(8,128)(2,1)S(1)} %bitcast.96), kind=kOutput, calls=%fused_computation.1 | convolution fusion | flops 306705408 | bytes 11546624 | tf_op jit(solution)/shard_map/thd,khd->thk/dot_general | solution.py:22
  106.6 0.1 fusion.28
  106.7 2.1 %fusion.1 = f32[192,16]{0,1:T(8,128)S(1)} fusion(f32[16,768,192]{1,2,0:T(8,128)S(1)} %get-tuple-element.13, f32[192,16]{0,1:T(8,128)S(1)} %get-tuple-element.11), kind=kLoop, calls=%fused_computation.3 | loop fusion | flops 7074816 | bytes 9461760 | tf_op jit(solution)/shard_map/reduce_sum | solution.py:29
  108.8 0.0 copy-start.2
  108.8 2.9 %fusion.17 = f32[192,16,64]{0,2,1:T(8,128)S(1)} fusion(f32[16,768,192]{1,2,0:T(8,128)S(1)} %get-tuple-element.13, f32[192,16]{0,1:T(8,128)S(1)} %get-tuple-element.11, bf16[768,16,2,64]{0,3,2,1:T(8,128)(2,1)S(1)} %bitcast.97, f32[192,16]{0,1:T(8,128)S(1)} %get-tuple-element.6, f32[192,16]{0,1:T(8,128)S(1)} %get-tuple-element.9), kind=kOutput, calls=%fused_computation.19 | convolution fusion | flops 309460992 | bytes 11845632 | tf_op jit(solution)/shard_map/thk,khd->thd/dot_general | solution.py:30
  111.8 0.0 copy-done.2
  111.8 0.3 fusion.20
  112.1 0.0 all-gather.10.cloned.1.call-done
  112.2 2.9 %fusion.22 = bf16[1,192,1024]{2,1,0:T(8,128)(2,1)} fusion(bf16[192,1024]{0,1:T(8,128)(2,1)S(1)} %bitcast.103, bf16[1024,1024]{1,0:T(8,128)(2,1)} %all-gather.10.cloned.1.call-done), kind=kOutput, calls=%fused_computation.24 | convolution fusion | flops 402849792 | bytes 2883584 | tf_op jit(solution)/shard_map/dot_general | solution.py:108
  (3 shorter events, 0.0 us)
Async XLA Ops:
  6.5 21.9 %copy-start = (bf16[1,51,1024]{2,1,0:T(8,128)(2,1)S(1)}, bf16[1,51,1024]{2,1,0:T(8,128)(2,1)}, u32[]{:S(2)}) copy-start(bf16[1,51,1024]{2,1,0:T(8,128)(2,1)} %param.12) | copy-start | bytes 313348
  6.5 21.9 %all-gather.6.cloned.1.call-start = ((), (), s32[]{:S(2)}) async-start(), calls=%async_computation | async-start | bytes 9437184 | tf_op jit(solution)/shard_map/all_gather | solution.py:60
  7.3 93.6 %all-gather.8.cloned.1.call-start = ((), (), s32[]{:S(2)}) async-start(), calls=%async_computation.1 | async-start | bytes 3932160 | tf_op jit(solution)/shard_map/all_gather | solution.py:97
  32.9 2.2 %copy-start.3 = (s32[1,1,192]{2,1,0:T(1,128)S(1)}, s32[1,1,192]{2,1,0:T(1,128)}, u32[]{:S(2)}) copy-start(s32[1,1,192]{2,1,0:T(1,128)} %param.11) | copy-start | bytes 2308
  33.6 29.6 %copy-start.1 = (bf16[192,3072]{0,1:T(8,128)(2,1)}, bf16[192,3072]{0,1:T(8,128)(2,1)S(1)}, u32[]{:S(2)}) copy-start(bf16[192,3072]{0,1:T(8,128)(2,1)S(1)} %copy.36) | copy-start | bytes 3538948
  35.1 77.1 %all-gather.10.cloned.1.call-start = ((), (), s32[]{:S(2)}) async-start(), calls=%async_computation.2 | async-start | bytes 3145728 | tf_op jit(solution)/shard_map/all_gather | solution.py:110
  35.6 12.7 %collective-permute-start = (bf16[4,2048]{1,0:T(4,128)(2,1)S(1)}, bf16[4,2048]{1,0:T(4,128)(2,1)S(1)}, u32[]{:S(2)}, u32[]{:S(2)}) collective-permute-start(bf16[4,2048]{1,0:T(4,128)(2,1)S(1)} %fusion.7), channel_id=1, source_target_pairs={{0,1},{1,0},{2,3},{3,2},{4,5},{5,4},{6,7},{7,6},{8,9},{9,8},{10,11... | collective-permute-start | bytes 49160 | tf_op jit(solution)/shard_map/ppermute | solution.py:16
  35.9 1.1 collective-permute-start.1
  108.8 2.9 %copy-start.2 = (bf16[16,16,1,64]{3,2,1,0:T(2,128)(2,1)S(1)}, bf16[16,16,1,64]{3,2,1,0:T(2,128)(2,1)}, u32[]{:S(2)}) copy-start(bf16[16,16,1,64]{3,2,1,0:T(2,128)(2,1)} %get-tuple-element.7) | copy-start | bytes 98308
Sparse Core Ops, SparseCore 0:
  8.9 19.4 all-gather.5
  35.2 65.5 all-gather.7
  102.4 9.3 all-gather.9
where the time goes:
time: 122 us
  waiting for transfers between devices  58.9 us (48%)
  blocking collectives  24.8 us (20%)
  matrix products  13.9 us (11%)
  between operations  13.2 us (11%)
  local copies, waits for them, and re-layouts  6.47 us (5%)
  other arithmetic  3.73 us (3%)
    all_gather x1, waiting for transfers between devices, shards(): lax.all_gather(key_values, 'peak', axis=0, tiled=True)  37.6 us
    all_gather x1, waiting for transfers between devices, shards(): lax.all_gather(qkv_weight, 'mod', axis=0, tiled=True)  19.7 us
    all_gather x1, blocking collectives, shards(): kv_part = lax.all_gather(partner_kv, 'peak', axis=0, tiled=True)  13.6 us
    all_gather x1, blocking collectives, shards(): bias_part = lax.all_gather(partner_bias, 'peak', axis=0, tiled=True)  11.2 us
    dot_general x1, matrix products, shards(): jnp.dot(columns, lax.all_gather(qkv_weight, 'mod', axis=0, tiled=True), p...  4.5 us
    dot_general x2, matrix products, attend_block(): jnp.einsum('thk,khd->thd', weights.astype(jnp.bfloat16), value_block, pre...  3.27 us
    all_gather x1, local copies, waits for them, and re-layouts, shards(): lax.all_gather(key_values, 'peak', axis=0, tiled=True)  3.18 us
    dot_general x1, matrix products, shards(): jnp.dot(columns, lax.all_gather(out_weight, 'mod', axis=0, tiled=True), p...  2.95 us
  transfers between devices with their start and end apart: 5, of which 3 were waited for; matrix products, arithmetic and copies ran while one was open for 12% of the time, Pallas kernels for 0%

commit v1 on v0

v1 whole, which is shorter than its diff:
```python
import jax
import jax.numpy as jnp
from jax import lax
from jax.experimental import pallas as pl
from jax.experimental.pallas import tpu as pltpu
from jax.sharding import PartitionSpec as P

H = 16
HD = 64
SEG_DEV = 4
PAIRS = H // 2
LANES = 128
BF16 = jnp.bfloat16
F32 = jnp.float32
VMEM_BYTES = 24 * 2**20
NEVER = -1e30


def call(kernel, outs, flops, *operands):
    spec = pl.BlockSpec(memory_space=pltpu.VMEM)
    shapes = [jax.ShapeDtypeStruct(shape, dtype) for shape, dtype in outs]
    return pl.pallas_call(
        kernel,
        out_shape=shapes,
        in_specs=[spec] * len(operands),
        out_specs=[spec] * len(shapes),
        compiler_params=pltpu.CompilerParams(vmem_limit_bytes=VMEM_BYTES),
        cost_estimate=pl.CostEstimate(flops=flops, bytes_accessed=2**20, transcendentals=0),
    )(*operands)


def contract(left, right, left_dim, right_dim):
    return lax.dot_general(
        left, right, (((left_dim,), (right_dim,)), ((), ())), preferred_element_type=F32
    )


def embed_kernel(hidden, bins, flags, segs, table, mask_row, first, second, summary):
    tokens, width = hidden.shape
    half = width // 2
    cut = tokens // 2
    mod = lax.axis_index("mod")
    one_hot = (
        lax.broadcasted_iota(jnp.int32, (table.shape[0], tokens), 0) == bins[...]
    ).astype(BF16)
    flag_rows = jnp.broadcast_to((flags[...] == 1).astype(F32), (LANES, tokens))
    flag_cols = jnp.concatenate([jnp.transpose(flag_rows)] * (half // LANES), axis=1) > 0.5
    seg_rows = lax.broadcasted_iota(jnp.int32, (2 * SEG_DEV, tokens), 0)
    picks = (lax.rem(seg_rows, SEG_DEV) == segs[...]).astype(F32)
    counts = jnp.sum(picks, axis=1, keepdims=True)
    picks = picks.astype(BF16)
    is_mean = lax.broadcasted_iota(jnp.int32, (2 * SEG_DEV, half), 0) < SEG_DEV
    for part in range(2):
        start = pl.multiple_of(lax.rem(mod + part, 2) * half, half)
        bin_rows = contract(one_hot, table[:, pl.ds(start, half)], 0, 0)
        chosen = jnp.where(
            flag_cols,
            mask_row[:, pl.ds(start, half)].astype(F32),
            hidden[:, pl.ds(start, half)].astype(F32),
        )
        embedded = (chosen + bin_rows).astype(BF16)
        columns = pl.ds(part * half, half)
        first[:, columns] = embedded[:cut]
        second[:cut, columns] = embedded[cut:]
        second[cut:, columns] = jnp.zeros((2 * SEG_DEV, half), BF16)
        sums = contract(picks, embedded, 1, 0)
        summary[:, pl.ds((1 - part) * half, half)] = jnp.where(
            is_mean, sums / counts, jnp.log(counts)
        ).astype(BF16)


def arrange_kernel(weight, arranged):
    rows = weight.shape[0]
    width = H * HD
    low = lax.broadcasted_iota(jnp.int32, (rows, LANES), 1) < HD
    for pair in range(PAIRS):
        at = pair * 3 * LANES
        query_key, value_query, key_value = [
            weight[:, at + i * LANES : at + (i + 1) * LANES] for i in range(3)
        ]
        to = pair * LANES
        arranged[:, to : to + LANES] = jnp.where(low, query_key, value_query)
        arranged[:, width + to : width + to + LANES] = jnp.where(low, key_value, query_key)
        arranged[:, 2 * width + to : 2 * width + to + LANES] = jnp.where(
            low, value_query, key_value
        )


def project(rows, weight_here, weight_there, start, stop):
    half = rows.shape[1] // 2
    return contract(rows[:, :half], weight_here[:, start:stop], 1, 0) + contract(
        rows[:, half:], weight_there[:, start:stop], 1, 0
    )


def fold(rows, summary_bias, weight_here, weight_there, turned, old, new):
    width = H * HD
    count = rows.shape[0]
    key = project(rows, weight_here, weight_there, width, 2 * width).astype(BF16)
    value = project(rows, weight_here, weight_there, 2 * width, 3 * width)
    value = jnp.transpose(value).astype(BF16)
    for pair in range(PAIRS):
        columns = slice(pair * LANES, (pair + 1) * LANES)
        scores = contract(key[:, columns], turned[pair], 1, 0)
        if summary_bias is not None:
            edge = count - summary_bias.shape[0]
            scores = jnp.concatenate([scores[:edge], scores[edge:] + summary_bias], axis=0)
        top = jnp.max(scores, axis=0, keepdims=True)
        if old is not None:
            top = jnp.maximum(top, old[0][pair : pair + 1, :])
        weights = jnp.exp(scores - top)
        total = jnp.sum(weights, axis=0, keepdims=True)
        summed = contract(value[columns, :], weights.astype(BF16), 1, 0)
        if old is not None:
            shrink = jnp.exp(old[0][pair : pair + 1, :] - top)
            total = total + shrink * old[1][pair : pair + 1, :]
            summed = summed + shrink * old[2][pair]
        new(pair, top, total, summed)


def bias_of(second):
    edge = second.shape[0] - 2 * SEG_DEV
    tail = second[edge:, :].astype(F32)
    wide = 3 * LANES
    return jnp.concatenate(
        [tail[SEG_DEV:, :wide], jnp.full((SEG_DEV, wide), NEVER, F32)], axis=0
    )


def store_state(top_ref, total_ref, summed_ref):
    def store(pair, top, total, summed):
        top_ref[pair : pair + 1, :] = top
        total_ref[pair : pair + 1, :] = total
        summed_ref[pair] = summed

    return store


def own_kernel(first, second, weight_here, weight_there, turned, top_ref, total_ref, summed_ref):
    cut = first.shape[0]
    width = H * HD
    rows = jnp.concatenate([first[...], second[...]], axis=0)
    query = project(rows[: 2 * cut], weight_here, weight_there, 0, width).astype(BF16)
    query = query.astype(F32) * (float(HD) ** -0.5)
    zeros = jnp.zeros((HD, LANES), F32)
    for pair in range(PAIRS):
        flipped = jnp.transpose(query[:, pair * LANES : (pair + 1) * LANES])
        even, odd = flipped[:HD], flipped[HD:]
        gap = jnp.zeros((HD, HD), F32)
        turned[pair] = jnp.concatenate(
            [
                jnp.concatenate([zeros, odd[:, :LANES], gap, odd[:, LANES:]], axis=1),
                jnp.concatenate([even[:, :LANES], zeros, even[:, LANES:], gap], axis=1),
            ],
            axis=0,
        ).astype(BF16)
    fold(
        rows, bias_of(second), weight_here, weight_there, turned, None,
        store_state(top_ref, total_ref, summed_ref),
    )


def both_kernel(
    first, second, weight_here, weight_there, turned, top_in, total_in, summed_in,
    top_ref, total_ref, summed_ref,
):
    rows = jnp.concatenate([first[...], second[...]], axis=0)
    fold(
        rows, bias_of(second), weight_here, weight_there, turned, (top_in, total_in, summed_in),
        store_state(top_ref, total_ref, summed_ref),
    )


def first_kernel(
    first, weight_here, weight_there, turned, top_in, total_in, summed_in,
    top_ref, total_ref, summed_ref,
):
    fold(
        first[...], None, weight_here, weight_there, turned, (top_in, total_in, summed_in),
        store_state(top_ref, total_ref, summed_ref),
    )


def last_kernel(
    second, weight_here, weight_there, turned, top_in, total_in, summed_in,
    out_here, out_there, update, attended,
):
    def finish(pair, top, total, summed):
        done = summed * (1.0 / total)
        left = jnp.concatenate([done[:HD, :LANES], done[HD:, LANES : 2 * LANES]], axis=0)
        right = jnp.concatenate(
            [done[:HD, 2 * LANES : 2 * LANES + HD], done[HD:, 2 * LANES + HD :]], axis=0
        )
        attended[pair * LANES : (pair + 1) * LANES, :] = jnp.concatenate(
            [left, right], axis=1
        ).astype(BF16)

    fold(
        second[...], bias_of(second), weight_here, weight_there, turned,
        (top_in, total_in, summed_in), finish,
    )
    half = out_here.shape[0]
    mod = lax.axis_index("mod")
    here = attended[pl.ds(pl.multiple_of(mod * half, half), half), :]
    there = attended[pl.ds(pl.multiple_of((1 - mod) * half, half), half), :]
    update[...] = (
        contract(here, out_here[...], 0, 0) + contract(there, out_there[...], 0, 0)
    ).astype(BF16)


def ring_pairs(size):
    order = [0] + list(range(1, size, 2)) + list(reversed(range(2, size, 2)))
    return [(order[i], order[(i + 1) % size]) for i in range(size)]


def swapped(value):
    return lax.ppermute(value, "mod", [(0, 1), (1, 0)])


def shards(
    hidden_in, value_bins, mask_flags, segment_ids, bin_table, mask_vector, qkv_weight, out_weight
):
    tokens, width = hidden_in.shape[1:]
    cut = tokens // 2
    size = lax.axis_size("peak")
    pairs = ring_pairs(size)
    state_shapes = [((PAIRS, 2 * tokens), F32)] * 2 + [((PAIRS, LANES, 2 * tokens), F32)]
    turned_shape = ((PAIRS, LANES, 2 * tokens), BF16)
    first, second, summary = call(
        embed_kernel,
        [((cut, width), BF16), ((cut + 2 * SEG_DEV, width), BF16), ((2 * SEG_DEV, width), BF16)],
        2**28,
        hidden_in[0], value_bins, mask_flags, segment_ids[0], bin_table[0], mask_vector,
    )
    summary = swapped(summary)
    second = lax.dynamic_update_slice(second, summary, (cut, 0))
    (arranged,) = call(arrange_kernel, [(qkv_weight.shape, BF16)], 2**28, qkv_weight)
    weights = (arranged, swapped(arranged))
    out_there = swapped(out_weight)

    turned, *state = call(
        own_kernel, [turned_shape] + state_shapes, 2**31, first, second, *weights
    )
    for step in range(1, size):
        first = lax.ppermute(first, "peak", pairs)
        second = lax.ppermute(second, "peak", pairs)
        if step < size - 1:
            state = call(
                both_kernel, state_shapes, 2**31, first, second, *weights, turned, *state
            )
    state = call(first_kernel, state_shapes, 2**30, first, *weights, turned, *state)
    (update,) = pl.pallas_call(
        last_kernel,
        out_shape=[jax.ShapeDtypeStruct((tokens, width), BF16)],
        in_specs=[pl.BlockSpec(memory_space=pltpu.VMEM)] * 9,
        out_specs=[pl.BlockSpec(memory_space=pltpu.VMEM)],
        scratch_shapes=[pltpu.VMEM((width, tokens), BF16)],
        compiler_params=pltpu.CompilerParams(vmem_limit_bytes=VMEM_BYTES),
        cost_estimate=pl.CostEstimate(flops=2**30, bytes_accessed=2**20, transcendentals=0),
    )(second, *weights, turned, *state, out_weight, out_there)
    return update[None]


def solution(mesh):
    placed = (
        P("mod", ("dp", "peak"), None),
        P("mod", ("dp", "peak")),
        P("mod", ("dp", "peak")),
        P("mod", ("dp", "peak"), None),
        P("mod", None, None),
        P("mod", None),
        P("mod", None),
        P("mod", None),
    )
    return jax.shard_map(
        shards,
        mesh=mesh,
        in_specs=placed,
        out_specs=P("mod", ("dp", "peak"), None),
        check_vma=False,
    )
```

time: 122 us -> 52.3 us (0.43)
  waiting for transfers between devices: 58.9 us -> 19.3 us
  blocking collectives: 24.8 us -> 0 us
  Pallas kernels: 0 us -> 18.2 us
  matrix products: 13.9 us -> 0 us
  between operations: 13.2 us -> 0.12 us
  starting transfers between devices: 0.59 us -> 12.6 us
  local copies, waits for them, and re-layouts: 6.47 us -> 1.92 us
  other arithmetic: 3.73 us -> 0 us
    all_gather x3 -> x0, waiting for transfers between devices: 57.3 us -> none  [the longest x1 37.6 us: shards(): lax.all_gather(key_values, 'peak', axis=0, tiled=True)]
    all_gather x2 -> x0, blocking collectives: 24.8 us -> none  [the longest x1 13.6 us: shards(): kv_part = lax.all_gather(partner_kv, 'peak', axis=0, tiled=True)]
    ppermute x2 -> x9, waiting for transfers between devices: 0.82 us -> 19.3 us  [the longest x3 10.2 us: shards(): first = lax.ppermute(first, 'peak', pairs)]
    pallas_call x0 -> x7, Pallas kernels: none -> 18.2 us  [the longest x6 14.2 us: call(): pl.pallas_call(kernel, out_shape=shapes, in_specs=[spec] * len(operands),...]
    dot_general x7 -> x0, matrix products: 13.9 us -> none  [the longest x1 4.5 us: shards(): jnp.dot(columns, lax.all_gather(qkv_weight, 'mod', axis=0, tiled=True), p...]
    ppermute x2 -> x9, starting transfers between devices: 0.51 us -> 12.6 us  [the longest x3 7.48 us: shards(): second = lax.ppermute(second, 'peak', pairs)]
    all_gather x1 -> x0, local copies, waits for them, and re-layouts: 3.18 us -> none  [shards(): lax.all_gather(key_values, 'peak', axis=0, tiled=True)]
    reduce_sum x3 -> x0, other arithmetic: 2.3 us -> none  [the longest x2 2.18 us: attend_block(): denominator = denominator * correction + jnp.sum(weights, axis=2)]
  transfers between devices with their start and end apart: 5 -> 9, of which waited for: 3 -> 4; matrix products, arithmetic and copies ran while one was open for 12% -> 0% of each run, Pallas kernels for 0% -> 25%
where the time goes in v1:
time: 52.3 us; the launch traced here: 52.2 us
  waiting for transfers between devices  19.3 us (37%)
  Pallas kernels  18.2 us (35%)
  starting transfers between devices  12.6 us (24%)
  local copies, waits for them, and re-layouts  1.92 us (4%)
    pallas_call x6, Pallas kernels, call(): pl.pallas_call(kernel, out_shape=shapes, in_specs=[spec] * len(operands),...  14.2 us
    ppermute x3, waiting for transfers between devices, shards(): first = lax.ppermute(first, 'peak', pairs)  10.2 us
    ppermute x3, starting transfers between devices, shards(): second = lax.ppermute(second, 'peak', pairs)  7.48 us
    ppermute x3, waiting for transfers between devices, swapped(): return lax.ppermute(value, 'mod', [(0, 1), (1, 0)])  4.67 us
    ppermute x3, starting transfers between devices, shards(): first = lax.ppermute(first, 'peak', pairs)  4.58 us
    ppermute x3, waiting for transfers between devices, shards(): second = lax.ppermute(second, 'peak', pairs)  4.46 us
    pallas_call x1, Pallas kernels, shards(): pl.pallas_call(last_kernel, out_shape=[jax.ShapeDtypeStruct((tokens, widt...  3.95 us
    unnamed x16, local copies, waits for them, and re-layouts  1.92 us
  transfers between devices with their start and end apart: 9, of which 4 were waited for; matrix products, arithmetic and copies ran while one was open for 0% of the time, Pallas kernels for 25%

profile of v1, /device:TPU:0, one launch (start us, length us, event | category | flops | bytes accessed | tf_op | source)
XLA Modules:
  0.0 52.2 jit_solution(16102705570334857097)
XLA Ops:
  0.0 0.0 copy-start
  0.0 1.9 %copy-done = bf16[512,3072]{1,0:T(8,128)(2,1)S(1)} copy-done((bf16[512,3072]{1,0:T(8,128)(2,1)S(1)}, bf16[512,3072]{1,0:T(8,128)(2,1)}, u32[]{:S(2)}) %copy-start) | copy-done | bytes 3145752
  1.9 0.0 copy-start.2
  1.9 0.0 copy-start.3
  1.9 0.0 copy-start.4
  1.9 0.0 copy-start.5
  1.9 0.0 copy-start.6
  1.9 0.0 copy-start.7
  1.9 0.0 copy-start.1
  1.9 1.0 %shard_map.83.weight_here = bf16[512,3072]{1,0:T(8,128)(2,1)S(1)} custom-call(bf16[512,3072]{1,0:T(8,128)(2,1)S(1)} %copy-done), custom_call_target="tpu_custom_call" | custom-call | flops 268435456 | bytes 1048576 | tf_op jit(solution)/shard_map/pallas_call | solution.py:22
  3.0 0.5 collective-permute-start.4
  3.5 0.0 copy-done.2
  3.5 0.0 copy-done.3
  3.5 0.0 copy-done.4
  3.5 0.0 copy-done.5
  3.5 0.0 copy-done.6
  3.5 0.0 copy-done.7
  3.5 0.5 %shard_map.82 = (bf16[96,1024]{1,0:T(8,128)(2,1)S(1)}, bf16[104,1024]{1,0:T(8,128)(2,1)S(1)}, bf16[8,1024]{1,0:T(8,128)(2,1)S(1)}) custom-call(bf16[192,1024]{1,0:T(8,128)(2,1)S(1)} %bitcast.4, s32[1,192]{1,0:T(1,128)S(1)} %copy-done.5, s32[1,192]{1,0:T(1,128)S(1)} %copy-done.6, s32[1,192]{1,0:T(1,128)S(1)} %bitcast.6, bf16[51,1024]{1,0:T(8,128)(2,1)S(1)} %bitcast.5, ...), custom_call_target="tpu_custom_call" | custom-call | flops 268435456 | bytes 1048576 | tf_op jit(solution)/shard_map/pallas_call | solution.py:22
  4.0 0.1 collective-permute-start
  4.1 4.7 %collective-permute-done = bf16[8,1024]{1,0:T(8,128)(2,1)S(1)} collective-permute-done((bf16[8,1024]{1,0:T(8,128)(2,1)S(1)}, bf16[8,1024]{1,0:T(8,128)(2,1)S(1)}, u32[]{:S(2)}, u32[]{:S(2)}) %collective-permute-start) | collective-permute-done | bytes 16416 | tf_op jit(solution)/shard_map/ppermute | solution.py:217
  8.8 2.9 %collective-permute-start.1 = (bf16[104,1024]{1,0:T(8,128)(2,1)S(1)}, bf16[104,1024]{1,0:T(8,128)(2,1)S(1)}, u32[]{:S(2)}, u32[]{:S(2)}) collective-permute-start(bf16[104,1024]{1,0:T(8,128)(2,1)S(1)} %constant_dynamic-update-slice_fusion.second), channel_id=1, source_target_pairs={{0,2},{2,6},{6,4},{4,0},{1,3},{3,7},{7,5},{5,1},{8,10},{10,14},{14... | collective-permute-start | bytes 638984 | tf_op jit(solution)/shard_map/ppermute | solution.py:246
  11.7 2.6 %collective-permute-start.5 = (bf16[96,1024]{1,0:T(8,128)(2,1)S(1)}, bf16[96,1024]{1,0:T(8,128)(2,1)S(1)}, u32[]{:S(2)}, u32[]{:S(2)}) collective-permute-start(bf16[96,1024]{1,0:T(8,128)(2,1)S(1)} %get-tuple-element.23.first), channel_id=1, source_target_pairs={{0,2},{2,6},{6,4},{4,0},{1,3},{3,7},{7,5},{5,1},{8,10},{10,14},{14... | collective-permute-start | bytes 589832 | tf_op jit(solution)/shard_map/ppermute | solution.py:245
  14.3 0.0 copy-done.1
  14.3 0.0 collective-permute-start.8
  14.3 4.5 %collective-permute-done.1.second = bf16[104,1024]{1,0:T(8,128)(2,1)S(1)} collective-permute-done((bf16[104,1024]{1,0:T(8,128)(2,1)S(1)}, bf16[104,1024]{1,0:T(8,128)(2,1)S(1)}, u32[]{:S(2)}, u32[]{:S(2)}) %collective-permute-start.1) | collective-permute-done | bytes 213024 | tf_op jit(solution)/shard_map/ppermute | solution.py:246
  18.8 1.2 %collective-permute-start.2 = (bf16[104,1024]{1,0:T(8,128)(2,1)S(1)}, bf16[104,1024]{1,0:T(8,128)(2,1)S(1)}, u32[]{:S(2)}, u32[]{:S(2)}) collective-permute-start(bf16[104,1024]{1,0:T(8,128)(2,1)S(1)} %collective-permute-done.1.second), channel_id=1, source_target_pairs={{0,2},{2,6},{6,4},{4,0},{1,3},{3,7},{7,5},{5,1},{8,10},{10,14},{14... | collective-permute-start | bytes 638984 | tf_op jit(solution)/shard_map/ppermute | solution.py:246
  19.9 3.1 %collective-permute-done.5.first = bf16[96,1024]{1,0:T(8,128)(2,1)S(1)} collective-permute-done((bf16[96,1024]{1,0:T(8,128)(2,1)S(1)}, bf16[96,1024]{1,0:T(8,128)(2,1)S(1)}, u32[]{:S(2)}, u32[]{:S(2)}) %collective-permute-start.5) | collective-permute-done | bytes 196640 | tf_op jit(solution)/shard_map/ppermute | solution.py:245
  23.0 1.2 %collective-permute-start.6 = (bf16[96,1024]{1,0:T(8,128)(2,1)S(1)}, bf16[96,1024]{1,0:T(8,128)(2,1)S(1)}, u32[]{:S(2)}, u32[]{:S(2)}) collective-permute-start(bf16[96,1024]{1,0:T(8,128)(2,1)S(1)} %collective-permute-done.5.first), channel_id=1, source_target_pairs={{0,2},{2,6},{6,4},{4,0},{1,3},{3,7},{7,5},{5,1},{8,10},{10,14},{14... | collective-permute-start | bytes 589832 | tf_op jit(solution)/shard_map/ppermute | solution.py:245
  24.1 7.1 %collective-permute-done.6.first = bf16[96,1024]{1,0:T(8,128)(2,1)S(1)} collective-permute-done((bf16[96,1024]{1,0:T(8,128)(2,1)S(1)}, bf16[96,1024]{1,0:T(8,128)(2,1)S(1)}, u32[]{:S(2)}, u32[]{:S(2)}) %collective-permute-start.6) | collective-permute-done | bytes 196640 | tf_op jit(solution)/shard_map/ppermute | solution.py:245
  31.3 0.8 %collective-permute-start.7 = (bf16[96,1024]{1,0:T(8,128)(2,1)S(1)}, bf16[96,1024]{1,0:T(8,128)(2,1)S(1)}, u32[]{:S(2)}, u32[]{:S(2)}) collective-permute-start(bf16[96,1024]{1,0:T(8,128)(2,1)S(1)} %collective-permute-done.6.first), channel_id=1, source_target_pairs={{0,2},{2,6},{6,4},{4,0},{1,3},{3,7},{7,5},{5,1},{8,10},{10,14},{14... | collective-permute-start | bytes 589832 | tf_op jit(solution)/shard_map/ppermute | solution.py:245
  32.1 0.0 collective-permute-done.2.second
  32.1 3.4 %collective-permute-start.3 = (bf16[104,1024]{1,0:T(8,128)(2,1)S(1)}, bf16[104,1024]{1,0:T(8,128)(2,1)S(1)}, u32[]{:S(2)}, u32[]{:S(2)}) collective-permute-start(bf16[104,1024]{1,0:T(8,128)(2,1)S(1)} %collective-permute-done.2.second), channel_id=1, source_target_pairs={{0,2},{2,6},{6,4},{4,0},{1,3},{3,7},{7,5},{5,1},{8,10},{10,14},{14... | collective-permute-start | bytes 638984 | tf_op jit(solution)/shard_map/ppermute | solution.py:246
  35.5 0.0 collective-permute-done.4.weight_there
  35.5 3.7 %shard_map.84 = (bf16[8,128,384]{2,1,0:T(8,128)(2,1)S(1)}, f32[8,384]{1,0:T(8,128)S(1)}, f32[8,384]{1,0:T(8,128)S(1)}, f32[8,128,384]{2,1,0:T(8,128)S(1)}) custom-call(bf16[96,1024]{1,0:T(8,128)(2,1)S(1)} %get-tuple-element.23.first, bf16[104,1024]{1,0:T(8,128)(2,1)S(1)} %constant_dynamic-update-slice_fusion.second, ...), custom_call_target="tpu_custom_call" | custom-call | flops 2147483648 | bytes 1048576 | tf_op jit(solution)/shard_map/pallas_call | solution.py:22
  39.2 3.3 %shard_map.85 = (f32[8,384]{1,0:T(8,128)S(1)}, f32[8,384]{1,0:T(8,128)S(1)}, f32[8,128,384]{2,1,0:T(8,128)S(1)}) custom-call(bf16[96,1024]{1,0:T(8,128)(2,1)S(1)} %collective-permute-done.5.first, bf16[104,1024]{1,0:T(8,128)(2,1)S(1)} %collective-permute-done.1.second, bf16[512,3072]{1,0:T(8,128)(2,1)S(1)} %shard_map.83.weight_here, ...), custom_call_target="tpu_custom_call" | custom-call | flops 2147483648 | bytes 1048576 | tf_op jit(solution)/shard_map/pallas_call | solution.py:22
  42.5 3.3 %shard_map.86 = (f32[8,384]{1,0:T(8,128)S(1)}, f32[8,384]{1,0:T(8,128)S(1)}, f32[8,128,384]{2,1,0:T(8,128)S(1)}) custom-call(bf16[96,1024]{1,0:T(8,128)(2,1)S(1)} %collective-permute-done.6.first, bf16[104,1024]{1,0:T(8,128)(2,1)S(1)} %collective-permute-done.2.second, bf16[512,3072]{1,0:T(8,128)(2,1)S(1)} %shard_map.83.weight_here, ...), custom_call_target="tpu_custom_call" | custom-call | flops 2147483648 | bytes 1048576 | tf_op jit(solution)/shard_map/pallas_call | solution.py:22
  45.7 0.0 collective-permute-done.7.first
  45.7 2.5 %shard_map.87 = (f32[8,384]{1,0:T(8,128)S(1)}, f32[8,384]{1,0:T(8,128)S(1)}, f32[8,128,384]{2,1,0:T(8,128)S(1)}) custom-call(bf16[96,1024]{1,0:T(8,128)(2,1)S(1)} %collective-permute-done.7.first, bf16[512,3072]{1,0:T(8,128)(2,1)S(1)} %shard_map.83.weight_here, bf16[512,3072]{1,0:T(8,128)(2,1)S(1)} %collective-permute-done.4.weight_there, ...), custom_call_target="tpu_custom_call" | custom-call | flops 1073741824 | bytes 1048576 | tf_op jit(solution)/shard_map/pallas_call | solution.py:22
  48.2 0.0 collective-permute-done.3.second
  48.2 0.0 collective-permute-done.8.out_there
  48.2 3.9 %shard_map.88 = bf16[192,1024]{1,0:T(8,128)(2,1)} custom-call(bf16[104,1024]{1,0:T(8,128)(2,1)S(1)} %collective-permute-done.3.second, bf16[512,3072]{1,0:T(8,128)(2,1)S(1)} %shard_map.83.weight_here, bf16[512,3072]{1,0:T(8,128)(2,1)S(1)} %collective-permute-done.4.weight_there, bf16[8,128,384]{2,1,0:T(8,128)(2,1)S(1)} %get-tuple-element.24.turned, ...), custom_call_target="tpu_custom_call" | custom-call | flops 1073741824 | bytes 1048576 | tf_op jit(solution)/shard_map/pallas_call | solution.py:252
  (1 shorter events, 0.0 us)
Async XLA Ops:
  0.0 1.9 %copy-start = (bf16[512,3072]{1,0:T(8,128)(2,1)S(1)}, bf16[512,3072]{1,0:T(8,128)(2,1)}, u32[]{:S(2)}) copy-start(bf16[512,3072]{1,0:T(8,128)(2,1)} %weight.1) | copy-start | bytes 9437188
  1.9 1.6 %copy-start.2 = (bf16[1,192,1024]{2,1,0:T(8,128)(2,1)S(1)}, bf16[1,192,1024]{2,1,0:T(8,128)(2,1)}, u32[]{:S(2)}) copy-start(bf16[1,192,1024]{2,1,0:T(8,128)(2,1)} %param.8) | copy-start | bytes 1179652
  1.9 1.6 %copy-start.3 = (bf16[1,51,1024]{2,1,0:T(8,128)(2,1)S(1)}, bf16[1,51,1024]{2,1,0:T(8,128)(2,1)}, u32[]{:S(2)}) copy-start(bf16[1,51,1024]{2,1,0:T(8,128)(2,1)} %param.12) | copy-start | bytes 313348
  1.9 1.6 %copy-start.4 = (bf16[1,1024]{1,0:T(2,128)(2,1)S(1)}, bf16[1,1024]{1,0:T(2,128)(2,1)}, u32[]{:S(2)}) copy-start(bf16[1,1024]{1,0:T(2,128)(2,1)} %mask_row.1) | copy-start | bytes 6148
  1.9 1.6 %copy-start.5 = (s32[1,192]{1,0:T(1,128)S(1)}, s32[1,192]{1,0:T(1,128)}, u32[]{:S(2)}) copy-start(s32[1,192]{1,0:T(1,128)} %bins.1) | copy-start | bytes 2308
  1.9 1.6 %copy-start.6 = (s32[1,192]{1,0:T(1,128)S(1)}, s32[1,192]{1,0:T(1,128)}, u32[]{:S(2)}) copy-start(s32[1,192]{1,0:T(1,128)} %flags.1) | copy-start | bytes 2308
  1.9 1.6 %copy-start.7 = (s32[1,1,192]{2,1,0:T(1,128)S(1)}, s32[1,1,192]{2,1,0:T(1,128)}, u32[]{:S(2)}) copy-start(s32[1,1,192]{2,1,0:T(1,128)} %param.11) | copy-start | bytes 2308
  1.9 12.4 %copy-start.1 = (bf16[512,1024]{1,0:T(8,128)(2,1)S(1)}, bf16[512,1024]{1,0:T(8,128)(2,1)}, u32[]{:S(2)}) copy-start(bf16[512,1024]{1,0:T(8,128)(2,1)} %out_here.1) | copy-start | bytes 3145732
  3.0 32.6 %collective-permute-start.4 = (bf16[512,3072]{1,0:T(8,128)(2,1)S(1)}, bf16[512,3072]{1,0:T(8,128)(2,1)S(1)}, u32[]{:S(2)}, u32[]{:S(2)}) collective-permute-start(bf16[512,3072]{1,0:T(8,128)(2,1)S(1)} %shard_map.83.weight_here), channel_id=1, source_target_pairs={{0,1},{1,0},{2,3},{3,2},{4,5},{5,4},{6,7},{7,6},{8,9},{9,8},{10,11... | collective-permute-start | bytes 9437192 | tf_op jit(solution)/shard_map/ppermute | solution.py:217
  4.0 4.7 %collective-permute-start = (bf16[8,1024]{1,0:T(8,128)(2,1)S(1)}, bf16[8,1024]{1,0:T(8,128)(2,1)S(1)}, u32[]{:S(2)}, u32[]{:S(2)}) collective-permute-start(bf16[8,1024]{1,0:T(8,128)(2,1)S(1)} %get-tuple-element.22), channel_id=1, source_target_pairs={{0,1},{1,0},{2,3},{3,2},{4,5},{5,4},{6,7},{7,6},{8,9},{9,8},{10,11... | collective-permute-start | bytes 49160 | tf_op jit(solution)/shard_map/ppermute | solution.py:217
  8.8 10.0 %collective-permute-start.1 = (bf16[104,1024]{1,0:T(8,128)(2,1)S(1)}, bf16[104,1024]{1,0:T(8,128)(2,1)S(1)}, u32[]{:S(2)}, u32[]{:S(2)}) collective-permute-start(bf16[104,1024]{1,0:T(8,128)(2,1)S(1)} %constant_dynamic-update-slice_fusion.second), channel_id=1, source_target_pairs={{0,2},{2,6},{6,4},{4,0},{1,3},{3,7},{7,5},{5,1},{8,10},{10,14},{14... | collective-permute-start | bytes 638984 | tf_op jit(solution)/shard_map/ppermute | solution.py:246
  11.7 11.3 %collective-permute-start.5 = (bf16[96,1024]{1,0:T(8,128)(2,1)S(1)}, bf16[96,1024]{1,0:T(8,128)(2,1)S(1)}, u32[]{:S(2)}, u32[]{:S(2)}) collective-permute-start(bf16[96,1024]{1,0:T(8,128)(2,1)S(1)} %get-tuple-element.23.first), channel_id=1, source_target_pairs={{0,2},{2,6},{6,4},{4,0},{1,3},{3,7},{7,5},{5,1},{8,10},{10,14},{14... | collective-permute-start | bytes 589832 | tf_op jit(solution)/shard_map/ppermute | solution.py:245
  14.3 33.9 %collective-permute-start.8 = (bf16[512,1024]{1,0:T(8,128)(2,1)S(1)}, bf16[512,1024]{1,0:T(8,128)(2,1)S(1)}, u32[]{:S(2)}, u32[]{:S(2)}) collective-permute-start(bf16[512,1024]{1,0:T(8,128)(2,1)S(1)} %copy-done.1), channel_id=1, source_target_pairs={{0,1},{1,0},{2,3},{3,2},{4,5},{5,4},{6,7},{7,6},{8,9},{9,8},{10,11... | collective-permute-start | bytes 3145736 | tf_op jit(solution)/shard_map/ppermute | solution.py:217
  18.8 13.3 %collective-permute-start.2 = (bf16[104,1024]{1,0:T(8,128)(2,1)S(1)}, bf16[104,1024]{1,0:T(8,128)(2,1)S(1)}, u32[]{:S(2)}, u32[]{:S(2)}) collective-permute-start(bf16[104,1024]{1,0:T(8,128)(2,1)S(1)} %collective-permute-done.1.second), channel_id=1, source_target_pairs={{0,2},{2,6},{6,4},{4,0},{1,3},{3,7},{7,5},{5,1},{8,10},{10,14},{14... | collective-permute-start | bytes 638984 | tf_op jit(solution)/shard_map/ppermute | solution.py:246
  23.0 8.3 %collective-permute-start.6 = (bf16[96,1024]{1,0:T(8,128)(2,1)S(1)}, bf16[96,1024]{1,0:T(8,128)(2,1)S(1)}, u32[]{:S(2)}, u32[]{:S(2)}) collective-permute-start(bf16[96,1024]{1,0:T(8,128)(2,1)S(1)} %collective-permute-done.5.first), channel_id=1, source_target_pairs={{0,2},{2,6},{6,4},{4,0},{1,3},{3,7},{7,5},{5,1},{8,10},{10,14},{14... | collective-permute-start | bytes 589832 | tf_op jit(solution)/shard_map/ppermute | solution.py:245
  31.3 14.4 %collective-permute-start.7 = (bf16[96,1024]{1,0:T(8,128)(2,1)S(1)}, bf16[96,1024]{1,0:T(8,128)(2,1)S(1)}, u32[]{:S(2)}, u32[]{:S(2)}) collective-permute-start(bf16[96,1024]{1,0:T(8,128)(2,1)S(1)} %collective-permute-done.6.first), channel_id=1, source_target_pairs={{0,2},{2,6},{6,4},{4,0},{1,3},{3,7},{7,5},{5,1},{8,10},{10,14},{14... | collective-permute-start | bytes 589832 | tf_op jit(solution)/shard_map/ppermute | solution.py:245
  32.1 16.1 %collective-permute-start.3 = (bf16[104,1024]{1,0:T(8,128)(2,1)S(1)}, bf16[104,1024]{1,0:T(8,128)(2,1)S(1)}, u32[]{:S(2)}, u32[]{:S(2)}) collective-permute-start(bf16[104,1024]{1,0:T(8,128)(2,1)S(1)} %collective-permute-done.2.second), channel_id=1, source_target_pairs={{0,2},{2,6},{6,4},{4,0},{1,3},{3,7},{7,5},{5,1},{8,10},{10,14},{14... | collective-permute-start | bytes 638984 | tf_op jit(solution)/shard_map/ppermute | solution.py:246

commit v2 on v1

--- a/solution.py
+++ b/solution.py
@@ -35,7 +35,17 @@
     )
 
 
-def embed_kernel(hidden, bins, flags, segs, table, mask_row, first, second, summary):
+def embed_kernel(*refs):
+    sources, (first, second), copies, done = refs[:6], refs[6:8], refs[8:14], refs[14]
+    moves = [
+        pltpu.make_async_copy(source, copy, done.at[i])
+        for i, (source, copy) in enumerate(zip(sources, copies))
+    ]
+    for move in moves:
+        move.start()
+    for move in moves:
+        move.wait()
+    hidden, bins, flags, segs, table, mask_row = copies
     tokens, width = hidden.shape
     half = width // 2
     cut = tokens // 2
@@ -60,11 +70,10 @@
         )
         embedded = (chosen + bin_rows).astype(BF16)
         columns = pl.ds(part * half, half)
-        first[:, columns] = embedded[:cut]
-        second[:cut, columns] = embedded[cut:]
-        second[cut:, columns] = jnp.zeros((2 * SEG_DEV, half), BF16)
+        first[:cut, columns] = embedded[:cut]
+        second[:, columns] = embedded[cut:]
         sums = contract(picks, embedded, 1, 0)
-        summary[:, pl.ds((1 - part) * half, half)] = jnp.where(
+        first[cut:, pl.ds((1 - part) * half, half)] = jnp.where(
             is_mean, sums / counts, jnp.log(counts)
         ).astype(BF16)
 
@@ -97,33 +106,72 @@
     width = H * HD
     count = rows.shape[0]
     key = project(rows, weight_here, weight_there, width, 2 * width).astype(BF16)
-    value = project(rows, weight_here, weight_there, 2 * width, 3 * width)
-    value = jnp.transpose(value).astype(BF16)
-    for pair in range(PAIRS):
-        columns = slice(pair * LANES, (pair + 1) * LANES)
-        scores = contract(key[:, columns], turned[pair], 1, 0)
+    low = lax.broadcasted_iota(jnp.int32, (HD, LANES), 1) < HD
+    scores, values, folded = {}, {}, {}
+
+    def score(pair):
+        found = contract(key[:, pair * LANES : (pair + 1) * LANES], turned[pair], 1, 0)
         if summary_bias is not None:
             edge = count - summary_bias.shape[0]
-            scores = jnp.concatenate([scores[:edge], scores[edge:] + summary_bias], axis=0)
-        top = jnp.max(scores, axis=0, keepdims=True)
+            found = jnp.concatenate([found[:edge], found[edge:] + summary_bias], axis=0)
+        scores[pair] = found
+
+    def value(pair):
+        start = 2 * width + pair * LANES
+        found = project(rows, weight_here, weight_there, start, start + 2 * LANES)
+        found = jnp.transpose(found).astype(BF16)
+        values[pair], values[pair + 1] = found[:LANES], found[LANES:]
+
+    def weigh(pair):
+        found = scores.pop(pair)
+        top = jnp.max(found, axis=0, keepdims=True)
         if old is not None:
             top = jnp.maximum(top, old[0][pair : pair + 1, :])
-        weights = jnp.exp(scores - top)
+        weights = jnp.exp(found - top)
         total = jnp.sum(weights, axis=0, keepdims=True)
-        summed = contract(value[columns, :], weights.astype(BF16), 1, 0)
+        shrink = None
         if old is not None:
             shrink = jnp.exp(old[0][pair : pair + 1, :] - top)
             total = total + shrink * old[1][pair : pair + 1, :]
+        folded[pair] = (weights.astype(BF16), top, total, shrink)
+
+    def attend(pair):
+        weights, top, total, shrink = folded.pop(pair)
+        product = contract(values.pop(pair), weights, 1, 0)
+        summed = jnp.concatenate(
+            [
+                product[:HD, :LANES],
+                product[HD:, LANES : 2 * LANES],
+                jnp.where(low, product[:HD, 2 * LANES :], product[HD:, 2 * LANES :]),
+            ],
+            axis=1,
+        )
+        if old is not None:
             summed = summed + shrink * old[2][pair]
         new(pair, top, total, summed)
 
-
-def bias_of(second):
-    edge = second.shape[0] - 2 * SEG_DEV
-    tail = second[edge:, :].astype(F32)
+    score(0)
+    score(1)
+    for pair in range(PAIRS):
+        if pair % 2 == 0:
+            value(pair)
+        if pair + 2 < PAIRS:
+            score(pair + 2)
+        weigh(pair)
+        if pair >= 1:
+            attend(pair - 1)
+    attend(PAIRS - 1)
+
+
+def bias_of(rows):
+    edge = rows.shape[0] - 2 * SEG_DEV
     wide = 3 * LANES
     return jnp.concatenate(
-        [tail[SEG_DEV:, :wide], jnp.full((SEG_DEV, wide), NEVER, F32)], axis=0
+        [
+            rows[edge:, :wide].astype(F32)[SEG_DEV:],
+            jnp.full((SEG_DEV, wide), NEVER, F32),
+        ],
+        axis=0,
     )
 
 
@@ -136,10 +184,12 @@
     return store
 
 
-def own_kernel(first, second, weight_here, weight_there, turned, top_ref, total_ref, summed_ref):
-    cut = first.shape[0]
+def own_kernel(
+    first, second, summary, weight_here, weight_there, turned, top_ref, total_ref, summed_ref
+):
+    cut = second.shape[0]
     width = H * HD
-    rows = jnp.concatenate([first[...], second[...]], axis=0)
+    rows = jnp.concatenate([first[:cut, :], second[...], summary[...]], axis=0)
     query = project(rows[: 2 * cut], weight_here, weight_there, 0, width).astype(BF16)
     query = query.astype(F32) * (float(HD) ** -0.5)
     zeros = jnp.zeros((HD, LANES), F32)
@@ -155,18 +205,18 @@
             axis=0,
         ).astype(BF16)
     fold(
-        rows, bias_of(second), weight_here, weight_there, turned, None,
+        rows, bias_of(summary), weight_here, weight_there, turned, None,
         store_state(top_ref, total_ref, summed_ref),
     )
 
 
 def both_kernel(
-    first, second, weight_here, weight_there, turned, top_in, total_in, summed_in,
+    first, second, summary, weight_here, weight_there, turned, top_in, total_in, summed_in,
     top_ref, total_ref, summed_ref,
 ):
-    rows = jnp.concatenate([first[...], second[...]], axis=0)
+    rows = jnp.concatenate([first[: second.shape[0], :], second[...], summary[...]], axis=0)
     fold(
-        rows, bias_of(second), weight_here, weight_there, turned, (top_in, total_in, summed_in),
+        rows, bias_of(summary), weight_here, weight_there, turned, (top_in, total_in, summed_in),
         store_state(top_ref, total_ref, summed_ref),
     )
 
@@ -176,27 +226,26 @@
     top_ref, total_ref, summed_ref,
 ):
     fold(
-        first[...], None, weight_here, weight_there, turned, (top_in, total_in, summed_in),
+        first[: first.shape[0] - 2 * SEG_DEV, :], None, weight_here, weight_there, turned, (top_in, total_in, summed_in),
         store_state(top_ref, total_ref, summed_ref),
     )
 
 
 def last_kernel(
-    second, weight_here, weight_there, turned, top_in, total_in, summed_in,
+    second, summary, weight_here, weight_there, turned, top_in, total_in, summed_in,
     out_here, out_there, update, attended,
 ):
     def finish(pair, top, total, summed):
-        done = summed * (1.0 / total)
-        left = jnp.concatenate([done[:HD, :LANES], done[HD:, LANES : 2 * LANES]], axis=0)
-        right = jnp.concatenate(
-            [done[:HD, 2 * LANES : 2 * LANES + HD], done[HD:, 2 * LANES + HD :]], axis=0
-        )
-        attended[pair * LANES : (pair + 1) * LANES, :] = jnp.concatenate(
-            [left, right], axis=1
-        ).astype(BF16)
+        done = (summed * (1.0 / total)).astype(BF16)
+        for odd in range(2):
+            at = pair * LANES + odd * HD
+            rest = 2 * LANES + odd * HD
+            attended[at : at + HD, :] = jnp.concatenate(
+                [done[:, odd * LANES : (odd + 1) * LANES], done[:, rest : rest + HD]], axis=1
+            )
 
     fold(
-        second[...], bias_of(second), weight_here, weight_there, turned,
+        jnp.concatenate([second[...], summary[...]], axis=0), bias_of(summary), weight_here, weight_there, turned,
         (top_in, total_in, summed_in), finish,
     )
     half = out_here.shape[0]
@@ -213,6 +262,10 @@
     return [(order[i], order[(i + 1) % size]) for i in range(size)]
 
 
+def after(*values):
+    return lax.optimization_barrier(values)
+
+
 def swapped(value):
     return lax.ppermute(value, "mod", [(0, 1), (1, 0)])
 
@@ -224,40 +277,59 @@
     cut = tokens // 2
     size = lax.axis_size("peak")
     pairs = ring_pairs(size)
-    state_shapes = [((PAIRS, 2 * tokens), F32)] * 2 + [((PAIRS, LANES, 2 * tokens), F32)]
+    state_shapes = [((PAIRS, 2 * tokens), F32)] * 2 + [((PAIRS, HD, 2 * tokens), F32)]
     turned_shape = ((PAIRS, LANES, 2 * tokens), BF16)
-    first, second, summary = call(
+    operands = (
+        hidden_in[0], value_bins, mask_flags, segment_ids[0], bin_table[0], mask_vector,
+    )
+    vmem = pl.BlockSpec(memory_space=pltpu.VMEM)
+    first, second = pl.pallas_call(
         embed_kernel,
-        [((cut, width), BF16), ((cut + 2 * SEG_DEV, width), BF16), ((2 * SEG_DEV, width), BF16)],
-        2**28,
-        hidden_in[0], value_bins, mask_flags, segment_ids[0], bin_table[0], mask_vector,
-    )
-    summary = swapped(summary)
-    second = lax.dynamic_update_slice(second, summary, (cut, 0))
-    (arranged,) = call(arrange_kernel, [(qkv_weight.shape, BF16)], 2**28, qkv_weight)
-    weights = (arranged, swapped(arranged))
+        out_shape=[
+            jax.ShapeDtypeStruct((rows, width), BF16) for rows in (cut + 2 * SEG_DEV, cut)
+        ],
+        in_specs=[pl.BlockSpec(memory_space=pltpu.HBM)] * len(operands),
+        out_specs=[vmem] * 2,
+        scratch_shapes=[pltpu.VMEM(operand.shape, operand.dtype) for operand in operands]
+        + [pltpu.SemaphoreType.DMA((len(operands),))],
+        compiler_params=pltpu.CompilerParams(vmem_limit_bytes=56 * 2**20),
+        cost_estimate=pl.CostEstimate(flops=2**28, bytes_accessed=2**20, transcendentals=0),
+    )(*operands)
+    weights = [
+        call(arrange_kernel, [(weight.shape, BF16)], 2**28, weight)[0]
+        for weight in (qkv_weight, swapped(qkv_weight))
+    ]
     out_there = swapped(out_weight)
 
-    turned, *state = call(
-        own_kernel, [turned_shape] + state_shapes, 2**31, first, second, *weights
-    )
-    for step in range(1, size):
-        first = lax.ppermute(first, "peak", pairs)
-        second = lax.ppermute(second, "peak", pairs)
-        if step < size - 1:
+    for step in range(size - 1):
+        next_first = lax.ppermute(first, "peak", pairs)
+        next_second = lax.ppermute(second, "peak", pairs)
+        summary = swapped(first[cut:])
+        if step == 0:
+            summary, _ = after(summary, next_first)
+            turned, *state = call(
+                own_kernel, [turned_shape] + state_shapes, 2**31,
+                first, second, summary, *weights,
+            )
+        else:
+            if step < size - 2:
+                next_first, *state = after(next_first, *state)
             state = call(
-                both_kernel, state_shapes, 2**31, first, second, *weights, turned, *state
+                both_kernel, state_shapes, 2**31,
+                first, second, summary, *weights, turned, *state,
             )
+        first, second = next_first, next_second
+    summary = swapped(first[cut:])
     state = call(first_kernel, state_shapes, 2**30, first, *weights, turned, *state)
     (update,) = pl.pallas_call(
         last_kernel,
         out_shape=[jax.ShapeDtypeStruct((tokens, width), BF16)],
-        in_specs=[pl.BlockSpec(memory_space=pltpu.VMEM)] * 9,
+        in_specs=[pl.BlockSpec(memory_space=pltpu.VMEM)] * 10,
         out_specs=[pl.BlockSpec(memory_space=pltpu.VMEM)],
         scratch_shapes=[pltpu.VMEM((width, tokens), BF16)],
         compiler_params=pltpu.CompilerParams(vmem_limit_bytes=VMEM_BYTES),
         cost_estimate=pl.CostEstimate(flops=2**30, bytes_accessed=2**20, transcendentals=0),
-    )(second, *weights, turned, *state, out_weight, out_there)
+    )(second, summary, *weights, turned, *state, out_weight, out_there)
     return update[None]
 
 

time: 52.3 us -> 40.6 us (0.78)
  waiting for transfers between devices: 19.3 us -> 5.34 us
  starting transfers between devices: 12.6 us -> 14.7 us
  local copies, waits for them, and re-layouts: 1.92 us -> 2.63 us
  Pallas kernels: 18.2 us -> 17.5 us
    ppermute x6, waiting for transfers between devices: 14.7 us -> 5.32 us  [the longest x3 4.15 us: shards(): next_second = lax.ppermute(second, 'peak', pairs)]
    ppermute x3 -> x6, waiting for transfers between devices: 4.67 us -> 0.02 us  [swapped(): return lax.ppermute(value, 'mod', [(0, 1), (1, 0)])]
    pallas_call x6, Pallas kernels: 14.2 us -> 11.8 us  [call(): pl.pallas_call(kernel, out_shape=shapes, in_specs=[spec] * len(operands),...]
    pallas_call x0 -> x1, Pallas kernels: none -> 2.35 us  [shards(): pl.pallas_call(embed_kernel, out_shape=[jax.ShapeDtypeStruct((rows, width...]
    ppermute x3 -> x6, starting transfers between devices: 0.58 us -> 1.66 us  [swapped(): return lax.ppermute(value, 'mod', [(0, 1), (1, 0)])]
    ppermute x6, starting transfers between devices: 12.1 us -> 13.1 us  [the longest x3 8.54 us: shards(): next_first = lax.ppermute(first, 'peak', pairs)]
    slice x0 -> x4, local copies, waits for them, and re-layouts: none -> 0.73 us  [shards(): summary = swapped(first[cut:])]
    pallas_call x1, Pallas kernels: 3.95 us -> 3.38 us  [shards(): pl.pallas_call(last_kernel, out_shape=[jax.ShapeDtypeStruct((tokens, widt...]
  transfers between devices with their start and end apart: 9 -> 12, of which waited for: 4 -> 3; matrix products, arithmetic and copies ran while one was open for 0% -> 2% of each run, Pallas kernels for 25% -> 35%
where the time goes in v2:
time: 40.6 us; the launch traced here: 40.4 us
  Pallas kernels  17.5 us (43%)
  starting transfers between devices  14.7 us (36%)
  waiting for transfers between devices  5.34 us (13%)
  local copies, waits for them, and re-layouts  2.63 us (6%)
    pallas_call x6, Pallas kernels, call(): pl.pallas_call(kernel, out_shape=shapes, in_specs=[spec] * len(operands),...  11.8 us
    ppermute x3, starting transfers between devices, shards(): next_first = lax.ppermute(first, 'peak', pairs)  8.54 us
    ppermute x3, starting transfers between devices, shards(): next_second = lax.ppermute(second, 'peak', pairs)  4.53 us
    ppermute x3, waiting for transfers between devices, shards(): next_second = lax.ppermute(second, 'peak', pairs)  4.15 us
    pallas_call x1, Pallas kernels, shards(): pl.pallas_call(last_kernel, out_shape=[jax.ShapeDtypeStruct((tokens, widt...  3.38 us
    pallas_call x1, Pallas kernels, shards(): pl.pallas_call(embed_kernel, out_shape=[jax.ShapeDtypeStruct((rows, width...  2.35 us
    unnamed x8, local copies, waits for them, and re-layouts  1.9 us
    ppermute x6, starting transfers between devices, swapped(): return lax.ppermute(value, 'mod', [(0, 1), (1, 0)])  1.66 us
  transfers between devices with their start and end apart: 12, of which 3 were waited for; matrix products, arithmetic and copies ran while one was open for 2% of the time, Pallas kernels for 35%

profile of v2, /device:TPU:0, one launch (start us, length us, event | category | flops | bytes accessed | tf_op | source)
XLA Modules:
  0.0 40.4 jit_solution(8655005029553221383)
XLA Ops:
  0.0 0.5 %collective-permute-start.6 = (bf16[512,3072]{1,0:T(8,128)(2,1)}, bf16[512,3072]{1,0:T(8,128)(2,1)S(1)}, u32[]{:S(2)}, u32[]{:S(2)}) collective-permute-start(bf16[512,3072]{1,0:T(8,128)(2,1)} %weight.1), channel_id=1, source_target_pairs={{0,1},{1,0},{2,3},{3,2},{4,5},{5,4},{6,7},{7,6},{8,9},{9,8},{10,11... | collective-permute-start | bytes 9437192 | tf_op jit(solution)/shard_map/ppermute | solution.py:270
  0.5 2.3 %shard_map.82 = (bf16[104,1024]{1,0:T(8,128)(2,1)}, bf16[96,1024]{1,0:T(8,128)(2,1)}) custom-call(bf16[192,1024]{1,0:T(8,128)(2,1)} %bitcast.4, s32[1,192]{1,0:T(1,128)} %refs_1_.1, s32[1,192]{1,0:T(1,128)} %refs_2_.1, s32[1,192]{1,0:T(1,128)} %bitcast.6, bf16[51,1024]{1,0:T(8,128)(2,1)} %bitcast.5, bf16[1,1024]{1,0:T(2,128)(2,1)} %refs_5_.1), custom_call_target="tpu_custom_call" | custom-call | flops 268435456 | bytes 1048576 | tf_op jit(solution)/shard_map/pallas_call | solution.py:286
  2.8 2.6 %collective-permute-start = (bf16[96,1024]{1,0:T(8,128)(2,1)}, bf16[96,1024]{1,0:T(8,128)(2,1)S(1)}, u32[]{:S(2)}, u32[]{:S(2)}) collective-permute-start(bf16[96,1024]{1,0:T(8,128)(2,1)} %get-tuple-element.25.second), channel_id=1, source_target_pairs={{0,2},{2,6},{6,4},{4,0},{1,3},{3,7},{7,5},{5,1},{8,10},{10,14},{14... | collective-permute-start | bytes 589832 | tf_op jit(solution)/shard_map/ppermute | solution.py:306
  5.4 0.2 collective-permute-start.11
  5.7 2.6 %collective-permute-start.3 = (bf16[104,1024]{1,0:T(8,128)(2,1)}, bf16[104,1024]{1,0:T(8,128)(2,1)S(1)}, u32[]{:S(2)}, u32[]{:S(2)}) collective-permute-start(bf16[104,1024]{1,0:T(8,128)(2,1)} %get-tuple-element.26.first), channel_id=1, source_target_pairs={{0,2},{2,6},{6,4},{4,0},{1,3},{3,7},{7,5},{5,1},{8,10},{10,14},{14... | collective-permute-start | bytes 638984 | tf_op jit(solution)/shard_map/ppermute | solution.py:305
  8.3 4.1 %collective-permute-done.second = bf16[96,1024]{1,0:T(8,128)(2,1)S(1)} collective-permute-done((bf16[96,1024]{1,0:T(8,128)(2,1)}, bf16[96,1024]{1,0:T(8,128)(2,1)S(1)}, u32[]{:S(2)}, u32[]{:S(2)}) %collective-permute-start) | collective-permute-done | bytes 196640 | tf_op jit(solution)/shard_map/ppermute | solution.py:306
  12.4 1.1 %collective-permute-start.1 = (bf16[96,1024]{1,0:T(8,128)(2,1)S(1)}, bf16[96,1024]{1,0:T(8,128)(2,1)S(1)}, u32[]{:S(2)}, u32[]{:S(2)}) collective-permute-start(bf16[96,1024]{1,0:T(8,128)(2,1)S(1)} %collective-permute-done.second), channel_id=1, source_target_pairs={{0,2},{2,6},{6,4},{4,0},{1,3},{3,7},{7,5},{5,1},{8,10},{10,14},{14... | collective-permute-start | bytes 589832 | tf_op jit(solution)/shard_map/ppermute | solution.py:306
  13.6 0.7 %slice.12 = bf16[8,1024]{1,0:T(8,128)(2,1)S(1)} slice(bf16[104,1024]{1,0:T(8,128)(2,1)} %get-tuple-element.26.first), slice={[96:104], [0:1024]} | slice | bytes 32768 | tf_op jit(solution)/shard_map/slice | solution.py:307
  14.3 0.0 collective-permute-start.5
  14.3 0.0 copy-start
  14.3 1.9 %copy-done = bf16[512,3072]{1,0:T(8,128)(2,1)S(1)} copy-done((bf16[512,3072]{1,0:T(8,128)(2,1)S(1)}, bf16[512,3072]{1,0:T(8,128)(2,1)}, u32[]{:S(2)}) %copy-start) | copy-done | bytes 3145752
  16.2 1.0 %shard_map.83.weight_here = bf16[512,3072]{1,0:T(8,128)(2,1)S(1)} custom-call(bf16[512,3072]{1,0:T(8,128)(2,1)S(1)} %copy-done), custom_call_target="tpu_custom_call" | custom-call | flops 268435456 | bytes 1048576 | tf_op jit(solution)/shard_map/pallas_call | solution.py:22
  17.2 0.0 collective-permute-done.5.summary
  17.2 0.0 collective-permute-done.3.first
  17.2 0.0 copy-start.2
  17.2 0.0 copy-start.3
  17.2 0.6 %collective-permute-start.10 = (bf16[8,1024]{1,0:T(8,128)(2,1)S(1)}, bf16[8,1024]{1,0:T(8,128)(2,1)S(1)}, u32[]{:S(2)}, u32[]{:S(2)}) collective-permute-start(bf16[8,1024]{1,0:T(8,128)(2,1)S(1)} %slice.17), channel_id=1, source_target_pairs={{0,1},{1,0},{2,3},{3,2},{4,5},{5,4},{6,7},{7,6},{8,9},{9,8},{10,11... | collective-permute-start | bytes 49160 | tf_op jit(solution)/shard_map/ppermute | solution.py:270
  17.8 3.3 %collective-permute-start.4 = (bf16[104,1024]{1,0:T(8,128)(2,1)S(1)}, bf16[104,1024]{1,0:T(8,128)(2,1)S(1)}, u32[]{:S(2)}, u32[]{:S(2)}) collective-permute-start(bf16[104,1024]{1,0:T(8,128)(2,1)S(1)} %collective-permute-done.3.first), channel_id=1, source_target_pairs={{0,2},{2,6},{6,4},{4,0},{1,3},{3,7},{7,5},{5,1},{8,10},{10,14},{14... | collective-permute-start | bytes 638984 | tf_op jit(solution)/shard_map/ppermute | solution.py:305
  21.1 0.0 collective-permute-done.1.second
  21.1 0.8 %collective-permute-start.2 = (bf16[96,1024]{1,0:T(8,128)(2,1)S(1)}, bf16[96,1024]{1,0:T(8,128)(2,1)S(1)}, u32[]{:S(2)}, u32[]{:S(2)}) collective-permute-start(bf16[96,1024]{1,0:T(8,128)(2,1)S(1)} %collective-permute-done.1.second), channel_id=1, source_target_pairs={{0,2},{2,6},{6,4},{4,0},{1,3},{3,7},{7,5},{5,1},{8,10},{10,14},{14... | collective-permute-start | bytes 589832 | tf_op jit(solution)/shard_map/ppermute | solution.py:306
  21.9 0.0 collective-permute-done.6.weight
  21.9 1.0 %shard_map.84.weight_there = bf16[512,3072]{1,0:T(8,128)(2,1)S(1)} custom-call(bf16[512,3072]{1,0:T(8,128)(2,1)S(1)} %collective-permute-done.6.weight), custom_call_target="tpu_custom_call" | custom-call | flops 268435456 | bytes 1048576 | tf_op jit(solution)/shard_map/pallas_call | solution.py:22
  22.9 0.0 copy-done.2
  22.9 0.0 copy-done.3
  22.9 2.9 %shard_map.85 = (bf16[8,128,384]{2,1,0:T(8,128)(2,1)S(1)}, f32[8,384]{1,0:T(8,128)S(1)}, f32[8,384]{1,0:T(8,128)S(1)}, f32[8,64,384]{2,1,0:T(8,128)S(1)}) custom-call(bf16[104,1024]{1,0:T(8,128)(2,1)S(1)} %copy-done.2, bf16[96,1024]{1,0:T(8,128)(2,1)S(1)} %copy-done.3, bf16[8,1024]{1,0:T(8,128)(2,1)S(1)} %collective-permute-done.5.summary, ...), custom_call_target="tpu_custom_call" | custom-call | flops 2147483648 | bytes 1048576 | tf_op jit(solution)/shard_map/pallas_call | solution.py:22
  25.9 1.0 %collective-permute-done.4.first = bf16[104,1024]{1,0:T(8,128)(2,1)S(1)} collective-permute-done((bf16[104,1024]{1,0:T(8,128)(2,1)S(1)}, bf16[104,1024]{1,0:T(8,128)(2,1)S(1)}, u32[]{:S(2)}, u32[]{:S(2)}) %collective-permute-start.4) | collective-permute-done | bytes 213024 | tf_op jit(solution)/shard_map/ppermute | solution.py:305
  26.8 2.7 %collective-permute-start.7 = (bf16[104,1024]{1,0:T(8,128)(2,1)S(1)}, bf16[104,1024]{1,0:T(8,128)(2,1)S(1)}, u32[]{:S(2)}, u32[]{:S(2)}) collective-permute-start(bf16[104,1024]{1,0:T(8,128)(2,1)S(1)} %collective-permute-done.4.first), channel_id=1, source_target_pairs={{0,2},{2,6},{6,4},{4,0},{1,3},{3,7},{7,5},{5,1},{8,10},{10,14},{14... | collective-permute-start | bytes 638984 | tf_op jit(solution)/shard_map/ppermute | solution.py:305
  29.5 0.0 collective-permute-start.9
  29.5 0.0 collective-permute-done.10.summary
  29.5 2.5 %shard_map.86 = (f32[8,384]{1,0:T(8,128)S(1)}, f32[8,384]{1,0:T(8,128)S(1)}, f32[8,64,384]{2,1,0:T(8,128)S(1)}) custom-call(bf16[104,1024]{1,0:T(8,128)(2,1)S(1)} %collective-permute-done.3.first, bf16[96,1024]{1,0:T(8,128)(2,1)S(1)} %collective-permute-done.second, bf16[8,1024]{1,0:T(8,128)(2,1)S(1)} %collective-permute-done.10.summary, ...), custom_call_target="tpu_custom_call" | custom-call | flops 2147483648 | bytes 1048576 | tf_op jit(solution)/shard_map/pallas_call | solution.py:22
  32.0 0.0 collective-permute-done.9.summary
  32.0 2.5 %shard_map.87 = (f32[8,384]{1,0:T(8,128)S(1)}, f32[8,384]{1,0:T(8,128)S(1)}, f32[8,64,384]{2,1,0:T(8,128)S(1)}) custom-call(bf16[104,1024]{1,0:T(8,128)(2,1)S(1)} %collective-permute-done.4.first, bf16[96,1024]{1,0:T(8,128)(2,1)S(1)} %collective-permute-done.1.second, bf16[8,1024]{1,0:T(8,128)(2,1)S(1)} %collective-permute-done.9.summary, ...), custom_call_target="tpu_custom_call" | custom-call | flops 2147483648 | bytes 1048576 | tf_op jit(solution)/shard_map/pallas_call | solution.py:22
  34.5 0.2 collective-permute-done.7.first
  34.7 0.4 collective-permute-start.8
  35.1 0.0 copy-start.1
  35.1 1.9 %shard_map.88 = (f32[8,384]{1,0:T(8,128)S(1)}, f32[8,384]{1,0:T(8,128)S(1)}, f32[8,64,384]{2,1,0:T(8,128)S(1)}) custom-call(bf16[104,1024]{1,0:T(8,128)(2,1)S(1)} %collective-permute-done.7.first, bf16[512,3072]{1,0:T(8,128)(2,1)S(1)} %shard_map.83.weight_here, bf16[512,3072]{1,0:T(8,128)(2,1)S(1)} %shard_map.84.weight_there, ...), custom_call_target="tpu_custom_call" | custom-call | flops 1073741824 | bytes 1048576 | tf_op jit(solution)/shard_map/pallas_call | solution.py:22
  37.0 0.0 collective-permute-done.2.second
  37.0 0.0 collective-permute-done.11.out_there
  37.0 0.0 collective-permute-done.8.summary
  37.0 0.0 copy-done.1
  37.0 3.4 %shard_map.89 = bf16[192,1024]{1,0:T(8,128)(2,1)} custom-call(bf16[96,1024]{1,0:T(8,128)(2,1)S(1)} %collective-permute-done.2.second, bf16[8,1024]{1,0:T(8,128)(2,1)S(1)} %collective-permute-done.8.summary, bf16[512,3072]{1,0:T(8,128)(2,1)S(1)} %shard_map.83.weight_here, bf16[512,3072]{1,0:T(8,128)(2,1)S(1)} %shard_map.84.weight_there, ...), custom_call_target="tpu_custom_call" | custom-call | flops 1073741824 | bytes 1048576 | tf_op jit(solution)/shard_map/pallas_call | solution.py:324
  (3 shorter events, 0.0 us)
Async XLA Ops:
  0.0 21.9 %collective-permute-start.6 = (bf16[512,3072]{1,0:T(8,128)(2,1)}, bf16[512,3072]{1,0:T(8,128)(2,1)S(1)}, u32[]{:S(2)}, u32[]{:S(2)}) collective-permute-start(bf16[512,3072]{1,0:T(8,128)(2,1)} %weight.1), channel_id=1, source_target_pairs={{0,1},{1,0},{2,3},{3,2},{4,5},{5,4},{6,7},{7,6},{8,9},{9,8},{10,11... | collective-permute-start | bytes 9437192 | tf_op jit(solution)/shard_map/ppermute | solution.py:270
  2.8 9.6 %collective-permute-start = (bf16[96,1024]{1,0:T(8,128)(2,1)}, bf16[96,1024]{1,0:T(8,128)(2,1)S(1)}, u32[]{:S(2)}, u32[]{:S(2)}) collective-permute-start(bf16[96,1024]{1,0:T(8,128)(2,1)} %get-tuple-element.25.second), channel_id=1, source_target_pairs={{0,2},{2,6},{6,4},{4,0},{1,3},{3,7},{7,5},{5,1},{8,10},{10,14},{14... | collective-permute-start | bytes 589832 | tf_op jit(solution)/shard_map/ppermute | solution.py:306
  5.4 31.6 %collective-permute-start.11 = (bf16[512,1024]{1,0:T(8,128)(2,1)}, bf16[512,1024]{1,0:T(8,128)(2,1)S(1)}, u32[]{:S(2)}, u32[]{:S(2)}) collective-permute-start(bf16[512,1024]{1,0:T(8,128)(2,1)} %out_here.1), channel_id=1, source_target_pairs={{0,1},{1,0},{2,3},{3,2},{4,5},{5,4},{6,7},{7,6},{8,9},{9,8},{10,11... | collective-permute-start | bytes 3145736 | tf_op jit(solution)/shard_map/ppermute | solution.py:270
  5.7 11.5 %collective-permute-start.3 = (bf16[104,1024]{1,0:T(8,128)(2,1)}, bf16[104,1024]{1,0:T(8,128)(2,1)S(1)}, u32[]{:S(2)}, u32[]{:S(2)}) collective-permute-start(bf16[104,1024]{1,0:T(8,128)(2,1)} %get-tuple-element.26.first), channel_id=1, source_target_pairs={{0,2},{2,6},{6,4},{4,0},{1,3},{3,7},{7,5},{5,1},{8,10},{10,14},{14... | collective-permute-start | bytes 638984 | tf_op jit(solution)/shard_map/ppermute | solution.py:305
  12.4 8.7 %collective-permute-start.1 = (bf16[96,1024]{1,0:T(8,128)(2,1)S(1)}, bf16[96,1024]{1,0:T(8,128)(2,1)S(1)}, u32[]{:S(2)}, u32[]{:S(2)}) collective-permute-start(bf16[96,1024]{1,0:T(8,128)(2,1)S(1)} %collective-permute-done.second), channel_id=1, source_target_pairs={{0,2},{2,6},{6,4},{4,0},{1,3},{3,7},{7,5},{5,1},{8,10},{10,14},{14... | collective-permute-start | bytes 589832 | tf_op jit(solution)/shard_map/ppermute | solution.py:306
  14.3 2.9 %collective-permute-start.5 = (bf16[8,1024]{1,0:T(8,128)(2,1)S(1)}, bf16[8,1024]{1,0:T(8,128)(2,1)S(1)}, u32[]{:S(2)}, u32[]{:S(2)}) collective-permute-start(bf16[8,1024]{1,0:T(8,128)(2,1)S(1)} %slice.12), channel_id=1, source_target_pairs={{0,1},{1,0},{2,3},{3,2},{4,5},{5,4},{6,7},{7,6},{8,9},{9,8},{10,11... | collective-permute-start | bytes 49160 | tf_op jit(solution)/shard_map/ppermute | solution.py:270
  14.3 1.9 %copy-start = (bf16[512,3072]{1,0:T(8,128)(2,1)S(1)}, bf16[512,3072]{1,0:T(8,128)(2,1)}, u32[]{:S(2)}) copy-start(bf16[512,3072]{1,0:T(8,128)(2,1)} %weight.1) | copy-start | bytes 9437188
  17.2 5.7 %copy-start.2 = (bf16[104,1024]{1,0:T(8,128)(2,1)S(1)}, bf16[104,1024]{1,0:T(8,128)(2,1)}, u32[]{:S(2)}) copy-start(bf16[104,1024]{1,0:T(8,128)(2,1)} %get-tuple-element.26.first) | copy-start | bytes 638980
  17.2 5.7 %copy-start.3 = (bf16[96,1024]{1,0:T(8,128)(2,1)S(1)}, bf16[96,1024]{1,0:T(8,128)(2,1)}, u32[]{:S(2)}) copy-start(bf16[96,1024]{1,0:T(8,128)(2,1)} %get-tuple-element.25.second) | copy-start | bytes 589828
  17.2 12.3 %collective-permute-start.10 = (bf16[8,1024]{1,0:T(8,128)(2,1)S(1)}, bf16[8,1024]{1,0:T(8,128)(2,1)S(1)}, u32[]{:S(2)}, u32[]{:S(2)}) collective-permute-start(bf16[8,1024]{1,0:T(8,128)(2,1)S(1)} %slice.17), channel_id=1, source_target_pairs={{0,1},{1,0},{2,3},{3,2},{4,5},{5,4},{6,7},{7,6},{8,9},{9,8},{10,11... | collective-permute-start | bytes 49160 | tf_op jit(solution)/shard_map/ppermute | solution.py:270
  17.8 9.0 %collective-permute-start.4 = (bf16[104,1024]{1,0:T(8,128)(2,1)S(1)}, bf16[104,1024]{1,0:T(8,128)(2,1)S(1)}, u32[]{:S(2)}, u32[]{:S(2)}) collective-permute-start(bf16[104,1024]{1,0:T(8,128)(2,1)S(1)} %collective-permute-done.3.first), channel_id=1, source_target_pairs={{0,2},{2,6},{6,4},{4,0},{1,3},{3,7},{7,5},{5,1},{8,10},{10,14},{14... | collective-permute-start | bytes 638984 | tf_op jit(solution)/shard_map/ppermute | solution.py:305
  21.1 15.9 %collective-permute-start.2 = (bf16[96,1024]{1,0:T(8,128)(2,1)S(1)}, bf16[96,1024]{1,0:T(8,128)(2,1)S(1)}, u32[]{:S(2)}, u32[]{:S(2)}) collective-permute-start(bf16[96,1024]{1,0:T(8,128)(2,1)S(1)} %collective-permute-done.1.second), channel_id=1, source_target_pairs={{0,2},{2,6},{6,4},{4,0},{1,3},{3,7},{7,5},{5,1},{8,10},{10,14},{14... | collective-permute-start | bytes 589832 | tf_op jit(solution)/shard_map/ppermute | solution.py:306
  26.8 7.9 %collective-permute-start.7 = (bf16[104,1024]{1,0:T(8,128)(2,1)S(1)}, bf16[104,1024]{1,0:T(8,128)(2,1)S(1)}, u32[]{:S(2)}, u32[]{:S(2)}) collective-permute-start(bf16[104,1024]{1,0:T(8,128)(2,1)S(1)} %collective-permute-done.4.first), channel_id=1, source_target_pairs={{0,2},{2,6},{6,4},{4,0},{1,3},{3,7},{7,5},{5,1},{8,10},{10,14},{14... | collective-permute-start | bytes 638984 | tf_op jit(solution)/shard_map/ppermute | solution.py:305
  29.5 2.5 %collective-permute-start.9 = (bf16[8,1024]{1,0:T(8,128)(2,1)S(1)}, bf16[8,1024]{1,0:T(8,128)(2,1)S(1)}, u32[]{:S(2)}, u32[]{:S(2)}) collective-permute-start(bf16[8,1024]{1,0:T(8,128)(2,1)S(1)} %slice.14), channel_id=1, source_target_pairs={{0,1},{1,0},{2,3},{3,2},{4,5},{5,4},{6,7},{7,6},{8,9},{9,8},{10,11... | collective-permute-start | bytes 49160 | tf_op jit(solution)/shard_map/ppermute | solution.py:270
  34.7 2.3 %collective-permute-start.8 = (bf16[8,1024]{1,0:T(8,128)(2,1)S(1)}, bf16[8,1024]{1,0:T(8,128)(2,1)S(1)}, u32[]{:S(2)}, u32[]{:S(2)}) collective-permute-start(bf16[8,1024]{1,0:T(8,128)(2,1)S(1)} %slice.16), channel_id=1, source_target_pairs={{0,1},{1,0},{2,3},{3,2},{4,5},{5,4},{6,7},{7,6},{8,9},{9,8},{10,11... | collective-permute-start | bytes 49160 | tf_op jit(solution)/shard_map/ppermute | solution.py:270
  35.1 1.9 %copy-start.1 = (bf16[512,1024]{1,0:T(8,128)(2,1)S(1)}, bf16[512,1024]{1,0:T(8,128)(2,1)}, u32[]{:S(2)}) copy-start(bf16[512,1024]{1,0:T(8,128)(2,1)} %out_here.1) | copy-start | bytes 3145732

commit v3 on v2

--- a/solution.py
+++ b/solution.py
@@ -14,6 +14,7 @@
 F32 = jnp.float32
 VMEM_BYTES = 24 * 2**20
 NEVER = -1e30
+COST = (2**28, 2**28)
 
 
 def call(kernel, outs, flops, *operands):
@@ -25,7 +26,7 @@
         in_specs=[spec] * len(operands),
         out_specs=[spec] * len(shapes),
         compiler_params=pltpu.CompilerParams(vmem_limit_bytes=VMEM_BYTES),
-        cost_estimate=pl.CostEstimate(flops=flops, bytes_accessed=2**20, transcendentals=0),
+        cost_estimate=pl.CostEstimate(flops=flops, bytes_accessed=2**10, transcendentals=0),
     )(*operands)
 
 
@@ -36,7 +37,7 @@
 
 
 def embed_kernel(*refs):
-    sources, (first, second), copies, done = refs[:6], refs[6:8], refs[8:14], refs[14]
+    sources, (first, second, summary), copies, done = refs[:6], refs[6:9], refs[9:15], refs[15]
     moves = [
         pltpu.make_async_copy(source, copy, done.at[i])
         for i, (source, copy) in enumerate(zip(sources, copies))
@@ -73,9 +74,9 @@
         first[:cut, columns] = embedded[:cut]
         second[:, columns] = embedded[cut:]
         sums = contract(picks, embedded, 1, 0)
-        first[cut:, pl.ds((1 - part) * half, half)] = jnp.where(
-            is_mean, sums / counts, jnp.log(counts)
-        ).astype(BF16)
+        crossed = pl.ds((1 - part) * half, half)
+        summary[:, crossed] = jnp.where(is_mean, sums / counts, jnp.log(counts)).astype(BF16)
+        first[cut:, crossed] = summary[:, crossed]
 
 
 def arrange_kernel(weight, arranged):
@@ -185,11 +186,14 @@
 
 
 def own_kernel(
-    first, second, summary, weight_here, weight_there, turned, top_ref, total_ref, summed_ref
+    first, second, arrived, summary, weight_here, weight_there,
+    turned, top_ref, total_ref, summed_ref,
 ):
     cut = second.shape[0]
     width = H * HD
-    rows = jnp.concatenate([first[:cut, :], second[...], summary[...]], axis=0)
+    rows = jnp.concatenate(
+        [first[:cut, :], second[...], arrived[:cut, :], summary[...]], axis=0
+    )
     query = project(rows[: 2 * cut], weight_here, weight_there, 0, width).astype(BF16)
     query = query.astype(F32) * (float(HD) ** -0.5)
     zeros = jnp.zeros((HD, LANES), F32)
@@ -210,23 +214,14 @@
     )
 
 
-def both_kernel(
-    first, second, summary, weight_here, weight_there, turned, top_in, total_in, summed_in,
+def middle_kernel(
+    second, first, summary, weight_here, weight_there, turned, top_in, total_in, summed_in,
     top_ref, total_ref, summed_ref,
 ):
-    rows = jnp.concatenate([first[: second.shape[0], :], second[...], summary[...]], axis=0)
+    cut = second.shape[0]
+    rows = jnp.concatenate([second[...], first[:cut, :], summary[...]], axis=0)
     fold(
         rows, bias_of(summary), weight_here, weight_there, turned, (top_in, total_in, summed_in),
-        store_state(top_ref, total_ref, summed_ref),
-    )
-
-
-def first_kernel(
-    first, weight_here, weight_there, turned, top_in, total_in, summed_in,
-    top_ref, total_ref, summed_ref,
-):
-    fold(
-        first[: first.shape[0] - 2 * SEG_DEV, :], None, weight_here, weight_there, turned, (top_in, total_in, summed_in),
         store_state(top_ref, total_ref, summed_ref),
     )
 
@@ -282,45 +277,45 @@
     operands = (
         hidden_in[0], value_bins, mask_flags, segment_ids[0], bin_table[0], mask_vector,
     )
+    operands = [pltpu.with_memory_space_constraint(operand, pltpu.HBM) for operand in operands]
     vmem = pl.BlockSpec(memory_space=pltpu.VMEM)
-    first, second = pl.pallas_call(
+    first, second, summary = pl.pallas_call(
         embed_kernel,
         out_shape=[
-            jax.ShapeDtypeStruct((rows, width), BF16) for rows in (cut + 2 * SEG_DEV, cut)
+            jax.ShapeDtypeStruct((rows, width), BF16) for rows in (cut + 2 * SEG_DEV, cut, 2 * SEG_DEV)
         ],
         in_specs=[pl.BlockSpec(memory_space=pltpu.HBM)] * len(operands),
-        out_specs=[vmem] * 2,
+        out_specs=[vmem] * 3,
         scratch_shapes=[pltpu.VMEM(operand.shape, operand.dtype) for operand in operands]
         + [pltpu.SemaphoreType.DMA((len(operands),))],
-        compiler_params=pltpu.CompilerParams(vmem_limit_bytes=56 * 2**20),
-        cost_estimate=pl.CostEstimate(flops=2**28, bytes_accessed=2**20, transcendentals=0),
+        compiler_params=pltpu.CompilerParams(vmem_limit_bytes=VMEM_BYTES),
+        cost_estimate=pl.CostEstimate(flops=2**20, bytes_accessed=2**10, transcendentals=0),
     )(*operands)
     weights = [
-        call(arrange_kernel, [(weight.shape, BF16)], 2**28, weight)[0]
+        call(arrange_kernel, [(weight.shape, BF16)], 2**20, weight)[0]
         for weight in (qkv_weight, swapped(qkv_weight))
     ]
     out_there = swapped(out_weight)
 
+    summary = swapped(summary)
     for step in range(size - 1):
         next_first = lax.ppermute(first, "peak", pairs)
         next_second = lax.ppermute(second, "peak", pairs)
-        summary = swapped(first[cut:])
         if step == 0:
-            summary, _ = after(summary, next_first)
+            next_first, summary, *weights = after(next_first, summary, *weights)
             turned, *state = call(
-                own_kernel, [turned_shape] + state_shapes, 2**31,
-                first, second, summary, *weights,
+                own_kernel, [turned_shape] + state_shapes, COST[0],
+                first, second, next_first, summary, *weights,
             )
         else:
-            if step < size - 2:
-                next_first, *state = after(next_first, *state)
             state = call(
-                both_kernel, state_shapes, 2**31,
-                first, second, summary, *weights, turned, *state,
+                middle_kernel, state_shapes, COST[1],
+                second, next_first, summary, *weights, turned, *state,
             )
+        if step < size - 2:
+            next_second, *state = after(next_second, *state)
         first, second = next_first, next_second
-    summary = swapped(first[cut:])
-    state = call(first_kernel, state_shapes, 2**30, first, *weights, turned, *state)
+        summary = swapped(first[cut:])
     (update,) = pl.pallas_call(
         last_kernel,
         out_shape=[jax.ShapeDtypeStruct((tokens, width), BF16)],
@@ -328,7 +323,7 @@
         out_specs=[pl.BlockSpec(memory_space=pltpu.VMEM)],
         scratch_shapes=[pltpu.VMEM((width, tokens), BF16)],
         compiler_params=pltpu.CompilerParams(vmem_limit_bytes=VMEM_BYTES),
-        cost_estimate=pl.CostEstimate(flops=2**30, bytes_accessed=2**20, transcendentals=0),
+        cost_estimate=pl.CostEstimate(flops=2**20, bytes_accessed=2**10, transcendentals=0),
     )(second, summary, *weights, turned, *state, out_weight, out_there)
     return update[None]
 

time: 40.6 us -> 37.2 us (0.916)
  Pallas kernels: 17.5 us -> 16 us
  waiting for transfers between devices: 5.34 us -> 4.02 us
  local copies, waits for them, and re-layouts: 2.63 us -> 1.9 us
    ppermute x3, starting transfers between devices: 4.53 us -> 8.57 us  [shards(): next_second = lax.ppermute(second, 'peak', pairs)]
    ppermute x3, starting transfers between devices: 8.54 us -> 5.92 us  [shards(): next_first = lax.ppermute(first, 'peak', pairs)]
    ppermute x3, waiting for transfers between devices: 4.15 us -> 1.63 us  [shards(): next_second = lax.ppermute(second, 'peak', pairs)]
    ppermute x3, waiting for transfers between devices: 1.17 us -> 2.37 us  [shards(): next_first = lax.ppermute(first, 'peak', pairs)]
    ppermute x6, starting transfers between devices: 1.66 us -> 0.52 us  [swapped(): return lax.ppermute(value, 'mod', [(0, 1), (1, 0)])]
    pallas_call x6 -> x5, Pallas kernels: 11.8 us -> 11 us  [call(): pl.pallas_call(kernel, out_shape=shapes, in_specs=[spec] * len(operands),...]
    slice x4 -> x3, local copies, waits for them, and re-layouts: 0.73 us -> 0.01 us  [shards(): summary = swapped(first[cut:])]
    pallas_call x1, Pallas kernels: 2.35 us -> 1.67 us  [shards(): pl.pallas_call(embed_kernel, out_shape=[jax.ShapeDtypeStruct((rows, width...]
  transfers between devices with their start and end apart: 12 -> 12, of which waited for: 3 -> 4; matrix products, arithmetic and copies ran while one was open for 2% -> 0% of each run, Pallas kernels for 35% -> 34%
where the time goes in v3:
time: 37.2 us; the launch traced here: 37 us
  Pallas kernels  16 us (43%)
  starting transfers between devices  15 us (40%)
  waiting for transfers between devices  4.02 us (11%)
  local copies, waits for them, and re-layouts  1.9 us (5%)
    pallas_call x5, Pallas kernels, call(): pl.pallas_call(kernel, out_shape=shapes, in_specs=[spec] * len(operands),...  11 us
    ppermute x3, starting transfers between devices, shards(): next_second = lax.ppermute(second, 'peak', pairs)  8.57 us
    ppermute x3, starting transfers between devices, shards(): next_first = lax.ppermute(first, 'peak', pairs)  5.92 us
    pallas_call x1, Pallas kernels, shards(): pl.pallas_call(last_kernel, out_shape=[jax.ShapeDtypeStruct((tokens, widt...  3.39 us
    ppermute x3, waiting for transfers between devices, shards(): next_first = lax.ppermute(first, 'peak', pairs)  2.37 us
    unnamed x4, local copies, waits for them, and re-layouts  1.89 us
    pallas_call x1, Pallas kernels, shards(): pl.pallas_call(embed_kernel, out_shape=[jax.ShapeDtypeStruct((rows, width...  1.67 us
    ppermute x3, waiting for transfers between devices, shards(): next_second = lax.ppermute(second, 'peak', pairs)  1.63 us
  transfers between devices with their start and end apart: 12, of which 4 were waited for; matrix products, arithmetic and copies ran while one was open for 0% of the time, Pallas kernels for 34%

profile of v3, /device:TPU:0, one launch (start us, length us, event | category | flops | bytes accessed | tf_op | source)
XLA Modules:
  0.0 37.0 jit_solution(6745073904190760703)
XLA Ops:
  0.0 0.5 %collective-permute-start.3 = (bf16[512,3072]{1,0:T(8,128)(2,1)}, bf16[512,3072]{1,0:T(8,128)(2,1)S(1)}, u32[]{:S(2)}, u32[]{:S(2)}) collective-permute-start(bf16[512,3072]{1,0:T(8,128)(2,1)} %weight.1), channel_id=1, source_target_pairs={{0,1},{1,0},{2,3},{3,2},{4,5},{5,4},{6,7},{7,6},{8,9},{9,8},{10,11... | collective-permute-start | bytes 9437192 | tf_op jit(solution)/shard_map/ppermute | solution.py:265
  0.5 0.1 collective-permute-start.11
  0.5 1.7 %shard_map.82 = (bf16[104,1024]{1,0:T(8,128)(2,1)S(1)}, bf16[96,1024]{1,0:T(8,128)(2,1)S(1)}, bf16[8,1024]{1,0:T(8,128)(2,1)S(1)}) custom-call(bf16[192,1024]{1,0:T(8,128)(2,1)} %bitcast.4, s32[1,192]{1,0:T(1,128)} %refs_1_.1, s32[1,192]{1,0:T(1,128)} %refs_2_.1, s32[1,192]{1,0:T(1,128)} %bitcast.6, bf16[51,1024]{1,0:T(8,128)(2,1)} %bitcast.5, ...), custom_call_target="tpu_custom_call" | custom-call | flops 1048576 | bytes 1024 | tf_op jit(solution)/shard_map/pallas_call | solution.py:282
  2.2 3.1 %collective-permute-start.1 = (bf16[104,1024]{1,0:T(8,128)(2,1)S(1)}, bf16[104,1024]{1,0:T(8,128)(2,1)S(1)}, u32[]{:S(2)}, u32[]{:S(2)}) collective-permute-start(bf16[104,1024]{1,0:T(8,128)(2,1)S(1)} %get-tuple-element.31.first), channel_id=1, source_target_pairs={{0,2},{2,6},{6,4},{4,0},{1,3},{3,7},{7,5},{5,1},{8,10},{10,14},{14... | collective-permute-start | bytes 638984 | tf_op jit(solution)/shard_map/ppermute | solution.py:302
  5.3 2.6 %collective-permute-start = (bf16[96,1024]{1,0:T(8,128)(2,1)S(1)}, bf16[96,1024]{1,0:T(8,128)(2,1)S(1)}, u32[]{:S(2)}, u32[]{:S(2)}) collective-permute-start(bf16[96,1024]{1,0:T(8,128)(2,1)S(1)} %get-tuple-element.30.second), channel_id=1, source_target_pairs={{0,2},{2,6},{6,4},{4,0},{1,3},{3,7},{7,5},{5,1},{8,10},{10,14},{14... | collective-permute-start | bytes 589832 | tf_op jit(solution)/shard_map/ppermute | solution.py:303
  7.8 0.0 collective-permute-start.2
  7.8 0.0 copy-start
  7.9 1.9 %copy-done = bf16[512,3072]{1,0:T(8,128)(2,1)S(1)} copy-done((bf16[512,3072]{1,0:T(8,128)(2,1)S(1)}, bf16[512,3072]{1,0:T(8,128)(2,1)}, u32[]{:S(2)}) %copy-start) | copy-done | bytes 3145752
  9.7 1.0 %shard_map.83.weight_here = bf16[512,3072]{1,0:T(8,128)(2,1)S(1)} custom-call(bf16[512,3072]{1,0:T(8,128)(2,1)S(1)} %copy-done), custom_call_target="tpu_custom_call" | custom-call | flops 1048576 | bytes 1024 | tf_op jit(solution)/shard_map/pallas_call | solution.py:23
  10.8 0.0 collective-permute-done.3.weight
  10.8 1.0 %shard_map.84.weight_there = bf16[512,3072]{1,0:T(8,128)(2,1)S(1)} custom-call(bf16[512,3072]{1,0:T(8,128)(2,1)S(1)} %collective-permute-done.3.weight), custom_call_target="tpu_custom_call" | custom-call | flops 1048576 | bytes 1024 | tf_op jit(solution)/shard_map/pallas_call | solution.py:23
  11.8 0.0 collective-permute-done.2.summary
  11.8 0.5 %collective-permute-done.1.arrived = bf16[104,1024]{1,0:T(8,128)(2,1)S(1)} collective-permute-done((bf16[104,1024]{1,0:T(8,128)(2,1)S(1)}, bf16[104,1024]{1,0:T(8,128)(2,1)S(1)}, u32[]{:S(2)}, u32[]{:S(2)}) %collective-permute-start.1) | collective-permute-done | bytes 213024 | tf_op jit(solution)/shard_map/ppermute | solution.py:302
  12.3 1.2 %collective-permute-start.5 = (bf16[104,1024]{1,0:T(8,128)(2,1)S(1)}, bf16[104,1024]{1,0:T(8,128)(2,1)S(1)}, u32[]{:S(2)}, u32[]{:S(2)}) collective-permute-start(bf16[104,1024]{1,0:T(8,128)(2,1)S(1)} %collective-permute-done.1.arrived), channel_id=1, source_target_pairs={{0,2},{2,6},{6,4},{4,0},{1,3},{3,7},{7,5},{5,1},{8,10},{10,14},{14... | collective-permute-start | bytes 638984 | tf_op jit(solution)/shard_map/ppermute | solution.py:302
  13.5 3.9 %shard_map.85 = (bf16[8,128,384]{2,1,0:T(8,128)(2,1)S(1)}, f32[8,384]{1,0:T(8,128)S(1)}, f32[8,384]{1,0:T(8,128)S(1)}, f32[8,64,384]{2,1,0:T(8,128)S(1)}) custom-call(bf16[104,1024]{1,0:T(8,128)(2,1)S(1)} %get-tuple-element.31.first, bf16[96,1024]{1,0:T(8,128)(2,1)S(1)} %get-tuple-element.30.second, bf16[104,1024]{1,0:T(8,128)(2,1)S(1)} %collective-permute-done.1.arrived, ...), custom_call_target="tpu_custom_call" | custom-call | flops 268435456 | bytes 1024 | tf_op jit(solution)/shard_map/pallas_call | solution.py:23
  17.4 0.0 collective-permute-done.second
  17.4 3.4 %collective-permute-start.4 = (bf16[96,1024]{1,0:T(8,128)(2,1)S(1)}, bf16[96,1024]{1,0:T(8,128)(2,1)S(1)}, u32[]{:S(2)}, u32[]{:S(2)}) collective-permute-start(bf16[96,1024]{1,0:T(8,128)(2,1)S(1)} %collective-permute-done.second), channel_id=1, source_target_pairs={{0,2},{2,6},{6,4},{4,0},{1,3},{3,7},{7,5},{5,1},{8,10},{10,14},{14... | collective-permute-start | bytes 589832 | tf_op jit(solution)/shard_map/ppermute | solution.py:303
  20.9 0.0 collective-permute-start.6
  20.9 0.0 collective-permute-done.5.first
  20.9 1.7 %collective-permute-start.8 = (bf16[104,1024]{1,0:T(8,128)(2,1)S(1)}, bf16[104,1024]{1,0:T(8,128)(2,1)S(1)}, u32[]{:S(2)}, u32[]{:S(2)}) collective-permute-start(bf16[104,1024]{1,0:T(8,128)(2,1)S(1)} %collective-permute-done.5.first), channel_id=1, source_target_pairs={{0,2},{2,6},{6,4},{4,0},{1,3},{3,7},{7,5},{5,1},{8,10},{10,14},{14... | collective-permute-start | bytes 638984 | tf_op jit(solution)/shard_map/ppermute | solution.py:302
  22.6 0.0 collective-permute-done.6.summary
  22.6 2.5 %shard_map.86 = (f32[8,384]{1,0:T(8,128)S(1)}, f32[8,384]{1,0:T(8,128)S(1)}, f32[8,64,384]{2,1,0:T(8,128)S(1)}) custom-call(bf16[96,1024]{1,0:T(8,128)(2,1)S(1)} %collective-permute-done.second, bf16[104,1024]{1,0:T(8,128)(2,1)S(1)} %collective-permute-done.5.first, bf16[8,1024]{1,0:T(8,128)(2,1)S(1)} %collective-permute-done.6.summary, ...), custom_call_target="tpu_custom_call" | custom-call | flops 268435456 | bytes 1024 | tf_op jit(solution)/shard_map/pallas_call | solution.py:23
  25.1 1.1 %collective-permute-done.4.second = bf16[96,1024]{1,0:T(8,128)(2,1)S(1)} collective-permute-done((bf16[96,1024]{1,0:T(8,128)(2,1)S(1)}, bf16[96,1024]{1,0:T(8,128)(2,1)S(1)}, u32[]{:S(2)}, u32[]{:S(2)}) %collective-permute-start.4) | collective-permute-done | bytes 196640 | tf_op jit(solution)/shard_map/ppermute | solution.py:303
  26.2 2.6 %collective-permute-start.7 = (bf16[96,1024]{1,0:T(8,128)(2,1)S(1)}, bf16[96,1024]{1,0:T(8,128)(2,1)S(1)}, u32[]{:S(2)}, u32[]{:S(2)}) collective-permute-start(bf16[96,1024]{1,0:T(8,128)(2,1)S(1)} %collective-permute-done.4.second), channel_id=1, source_target_pairs={{0,2},{2,6},{6,4},{4,0},{1,3},{3,7},{7,5},{5,1},{8,10},{10,14},{14... | collective-permute-start | bytes 589832 | tf_op jit(solution)/shard_map/ppermute | solution.py:303
  28.7 0.0 collective-permute-start.10
  28.7 1.8 %collective-permute-done.8.first = bf16[104,1024]{1,0:T(8,128)(2,1)S(1)} collective-permute-done((bf16[104,1024]{1,0:T(8,128)(2,1)S(1)}, bf16[104,1024]{1,0:T(8,128)(2,1)S(1)}, u32[]{:S(2)}, u32[]{:S(2)}) %collective-permute-start.8) | collective-permute-done | bytes 213024 | tf_op jit(solution)/shard_map/ppermute | solution.py:302
  30.6 0.0 copy-start.1
  30.6 0.0 collective-permute-start.9
  30.6 0.0 collective-permute-done.10.summary
  30.6 2.5 %shard_map.87 = (f32[8,384]{1,0:T(8,128)S(1)}, f32[8,384]{1,0:T(8,128)S(1)}, f32[8,64,384]{2,1,0:T(8,128)S(1)}) custom-call(bf16[96,1024]{1,0:T(8,128)(2,1)S(1)} %collective-permute-done.4.second, bf16[104,1024]{1,0:T(8,128)(2,1)S(1)} %collective-permute-done.8.first, bf16[8,1024]{1,0:T(8,128)(2,1)S(1)} %collective-permute-done.10.summary, ...), custom_call_target="tpu_custom_call" | custom-call | flops 268435456 | bytes 1024 | tf_op jit(solution)/shard_map/pallas_call | solution.py:23
  33.1 0.0 collective-permute-done.11.out_there
  33.1 0.6 %collective-permute-done.7.second = bf16[96,1024]{1,0:T(8,128)(2,1)S(1)} collective-permute-done((bf16[96,1024]{1,0:T(8,128)(2,1)S(1)}, bf16[96,1024]{1,0:T(8,128)(2,1)S(1)}, u32[]{:S(2)}, u32[]{:S(2)}) %collective-permute-start.7) | collective-permute-done | bytes 196640 | tf_op jit(solution)/shard_map/ppermute | solution.py:303
  33.7 0.0 collective-permute-done.9.summary
  33.7 0.0 copy-done.1
  33.7 3.4 %shard_map.88 = bf16[192,1024]{1,0:T(8,128)(2,1)} custom-call(bf16[96,1024]{1,0:T(8,128)(2,1)S(1)} %collective-permute-done.7.second, bf16[8,1024]{1,0:T(8,128)(2,1)S(1)} %collective-permute-done.9.summary, bf16[512,3072]{1,0:T(8,128)(2,1)S(1)} %shard_map.83.weight_here, bf16[512,3072]{1,0:T(8,128)(2,1)S(1)} %shard_map.84.weight_there, ...), custom_call_target="tpu_custom_call" | custom-call | flops 1048576 | bytes 1024 | tf_op jit(solution)/shard_map/pallas_call | solution.py:319
  (3 shorter events, 0.0 us)
Async XLA Ops:
  0.0 10.8 %collective-permute-start.3 = (bf16[512,3072]{1,0:T(8,128)(2,1)}, bf16[512,3072]{1,0:T(8,128)(2,1)S(1)}, u32[]{:S(2)}, u32[]{:S(2)}) collective-permute-start(bf16[512,3072]{1,0:T(8,128)(2,1)} %weight.1), channel_id=1, source_target_pairs={{0,1},{1,0},{2,3},{3,2},{4,5},{5,4},{6,7},{7,6},{8,9},{9,8},{10,11... | collective-permute-start | bytes 9437192 | tf_op jit(solution)/shard_map/ppermute | solution.py:265
  0.5 32.6 %collective-permute-start.11 = (bf16[512,1024]{1,0:T(8,128)(2,1)}, bf16[512,1024]{1,0:T(8,128)(2,1)S(1)}, u32[]{:S(2)}, u32[]{:S(2)}) collective-permute-start(bf16[512,1024]{1,0:T(8,128)(2,1)} %out_here.1), channel_id=1, source_target_pairs={{0,1},{1,0},{2,3},{3,2},{4,5},{5,4},{6,7},{7,6},{8,9},{9,8},{10,11... | collective-permute-start | bytes 3145736 | tf_op jit(solution)/shard_map/ppermute | solution.py:265
  2.2 10.1 %collective-permute-start.1 = (bf16[104,1024]{1,0:T(8,128)(2,1)S(1)}, bf16[104,1024]{1,0:T(8,128)(2,1)S(1)}, u32[]{:S(2)}, u32[]{:S(2)}) collective-permute-start(bf16[104,1024]{1,0:T(8,128)(2,1)S(1)} %get-tuple-element.31.first), channel_id=1, source_target_pairs={{0,2},{2,6},{6,4},{4,0},{1,3},{3,7},{7,5},{5,1},{8,10},{10,14},{14... | collective-permute-start | bytes 638984 | tf_op jit(solution)/shard_map/ppermute | solution.py:302
  5.3 12.2 %collective-permute-start = (bf16[96,1024]{1,0:T(8,128)(2,1)S(1)}, bf16[96,1024]{1,0:T(8,128)(2,1)S(1)}, u32[]{:S(2)}, u32[]{:S(2)}) collective-permute-start(bf16[96,1024]{1,0:T(8,128)(2,1)S(1)} %get-tuple-element.30.second), channel_id=1, source_target_pairs={{0,2},{2,6},{6,4},{4,0},{1,3},{3,7},{7,5},{5,1},{8,10},{10,14},{14... | collective-permute-start | bytes 589832 | tf_op jit(solution)/shard_map/ppermute | solution.py:303
  7.8 3.9 %collective-permute-start.2 = (bf16[8,1024]{1,0:T(8,128)(2,1)S(1)}, bf16[8,1024]{1,0:T(8,128)(2,1)S(1)}, u32[]{:S(2)}, u32[]{:S(2)}) collective-permute-start(bf16[8,1024]{1,0:T(8,128)(2,1)S(1)} %get-tuple-element.32), channel_id=1, source_target_pairs={{0,1},{1,0},{2,3},{3,2},{4,5},{5,4},{6,7},{7,6},{8,9},{9,8},{10,11... | collective-permute-start | bytes 49160 | tf_op jit(solution)/shard_map/ppermute | solution.py:265
  7.8 1.9 %copy-start = (bf16[512,3072]{1,0:T(8,128)(2,1)S(1)}, bf16[512,3072]{1,0:T(8,128)(2,1)}, u32[]{:S(2)}) copy-start(bf16[512,3072]{1,0:T(8,128)(2,1)} %weight.1) | copy-start | bytes 9437188
  12.3 8.5 %collective-permute-start.5 = (bf16[104,1024]{1,0:T(8,128)(2,1)S(1)}, bf16[104,1024]{1,0:T(8,128)(2,1)S(1)}, u32[]{:S(2)}, u32[]{:S(2)}) collective-permute-start(bf16[104,1024]{1,0:T(8,128)(2,1)S(1)} %collective-permute-done.1.arrived), channel_id=1, source_target_pairs={{0,2},{2,6},{6,4},{4,0},{1,3},{3,7},{7,5},{5,1},{8,10},{10,14},{14... | collective-permute-start | bytes 638984 | tf_op jit(solution)/shard_map/ppermute | solution.py:302
  17.4 8.7 %collective-permute-start.4 = (bf16[96,1024]{1,0:T(8,128)(2,1)S(1)}, bf16[96,1024]{1,0:T(8,128)(2,1)S(1)}, u32[]{:S(2)}, u32[]{:S(2)}) collective-permute-start(bf16[96,1024]{1,0:T(8,128)(2,1)S(1)} %collective-permute-done.second), channel_id=1, source_target_pairs={{0,2},{2,6},{6,4},{4,0},{1,3},{3,7},{7,5},{5,1},{8,10},{10,14},{14... | collective-permute-start | bytes 589832 | tf_op jit(solution)/shard_map/ppermute | solution.py:303
  20.9 1.7 %collective-permute-start.6 = (bf16[8,1024]{1,0:T(8,128)(2,1)S(1)}, bf16[8,1024]{1,0:T(8,128)(2,1)S(1)}, u32[]{:S(2)}, u32[]{:S(2)}) collective-permute-start(bf16[8,1024]{1,0:T(8,128)(2,1)S(1)} %slice.9), channel_id=1, source_target_pairs={{0,1},{1,0},{2,3},{3,2},{4,5},{5,4},{6,7},{7,6},{8,9},{9,8},{10,11... | collective-permute-start | bytes 49160 | tf_op jit(solution)/shard_map/ppermute | solution.py:265
  20.9 9.7 %collective-permute-start.8 = (bf16[104,1024]{1,0:T(8,128)(2,1)S(1)}, bf16[104,1024]{1,0:T(8,128)(2,1)S(1)}, u32[]{:S(2)}, u32[]{:S(2)}) collective-permute-start(bf16[104,1024]{1,0:T(8,128)(2,1)S(1)} %collective-permute-done.5.first), channel_id=1, source_target_pairs={{0,2},{2,6},{6,4},{4,0},{1,3},{3,7},{7,5},{5,1},{8,10},{10,14},{14... | collective-permute-start | bytes 638984 | tf_op jit(solution)/shard_map/ppermute | solution.py:302
  26.2 7.5 %collective-permute-start.7 = (bf16[96,1024]{1,0:T(8,128)(2,1)S(1)}, bf16[96,1024]{1,0:T(8,128)(2,1)S(1)}, u32[]{:S(2)}, u32[]{:S(2)}) collective-permute-start(bf16[96,1024]{1,0:T(8,128)(2,1)S(1)} %collective-permute-done.4.second), channel_id=1, source_target_pairs={{0,2},{2,6},{6,4},{4,0},{1,3},{3,7},{7,5},{5,1},{8,10},{10,14},{14... | collective-permute-start | bytes 589832 | tf_op jit(solution)/shard_map/ppermute | solution.py:303
  28.7 1.9 %collective-permute-start.10 = (bf16[8,1024]{1,0:T(8,128)(2,1)S(1)}, bf16[8,1024]{1,0:T(8,128)(2,1)S(1)}, u32[]{:S(2)}, u32[]{:S(2)}) collective-permute-start(bf16[8,1024]{1,0:T(8,128)(2,1)S(1)} %slice.13), channel_id=1, source_target_pairs={{0,1},{1,0},{2,3},{3,2},{4,5},{5,4},{6,7},{7,6},{8,9},{9,8},{10,11... | collective-permute-start | bytes 49160 | tf_op jit(solution)/shard_map/ppermute | solution.py:265
  30.6 3.1 %copy-start.1 = (bf16[512,1024]{1,0:T(8,128)(2,1)S(1)}, bf16[512,1024]{1,0:T(8,128)(2,1)}, u32[]{:S(2)}) copy-start(bf16[512,1024]{1,0:T(8,128)(2,1)} %out_here.1) | copy-start | bytes 3145732
  30.6 3.1 %collective-permute-start.9 = (bf16[8,1024]{1,0:T(8,128)(2,1)S(1)}, bf16[8,1024]{1,0:T(8,128)(2,1)S(1)}, u32[]{:S(2)}, u32[]{:S(2)}) collective-permute-start(bf16[8,1024]{1,0:T(8,128)(2,1)S(1)} %slice.12), channel_id=1, source_target_pairs={{0,1},{1,0},{2,3},{3,2},{4,5},{5,4},{6,7},{7,6},{8,9},{9,8},{10,11... | collective-permute-start | bytes 49160 | tf_op jit(solution)/shard_map/ppermute | solution.py:265

commit v4 on v3

--- a/solution.py
+++ b/solution.py
@@ -44,7 +44,7 @@
     ]
     for move in moves:
         move.start()
-    for move in moves:
+    for move in moves[1:]:
         move.wait()
     hidden, bins, flags, segs, table, mask_row = copies
     tokens, width = hidden.shape
@@ -61,9 +61,10 @@
     counts = jnp.sum(picks, axis=1, keepdims=True)
     picks = picks.astype(BF16)
     is_mean = lax.broadcasted_iota(jnp.int32, (2 * SEG_DEV, half), 0) < SEG_DEV
-    for part in range(2):
-        start = pl.multiple_of(lax.rem(mod + part, 2) * half, half)
-        bin_rows = contract(one_hot, table[:, pl.ds(start, half)], 0, 0)
+    starts = [pl.multiple_of(lax.rem(mod + part, 2) * half, half) for part in range(2)]
+    bin_parts = [contract(one_hot, table[:, pl.ds(start, half)], 0, 0) for start in starts]
+    moves[0].wait()
+    for part, (start, bin_rows) in enumerate(zip(starts, bin_parts)):
         chosen = jnp.where(
             flag_cols,
             mask_row[:, pl.ds(start, half)].astype(F32),
@@ -106,9 +107,11 @@
 def fold(rows, summary_bias, weight_here, weight_there, turned, old, new):
     width = H * HD
     count = rows.shape[0]
-    key = project(rows, weight_here, weight_there, width, 2 * width).astype(BF16)
+    key_value = project(rows, weight_here, weight_there, width, 3 * width)
+    key = key_value[:, :width].astype(BF16)
+    value = jnp.transpose(key_value[:, width:]).astype(BF16)
     low = lax.broadcasted_iota(jnp.int32, (HD, LANES), 1) < HD
-    scores, values, folded = {}, {}, {}
+    scores, folded = {}, {}
 
     def score(pair):
         found = contract(key[:, pair * LANES : (pair + 1) * LANES], turned[pair], 1, 0)
@@ -116,12 +119,6 @@
             edge = count - summary_bias.shape[0]
             found = jnp.concatenate([found[:edge], found[edge:] + summary_bias], axis=0)
         scores[pair] = found
-
-    def value(pair):
-        start = 2 * width + pair * LANES
-        found = project(rows, weight_here, weight_there, start, start + 2 * LANES)
-        found = jnp.transpose(found).astype(BF16)
-        values[pair], values[pair + 1] = found[:LANES], found[LANES:]
 
     def weigh(pair):
         found = scores.pop(pair)
@@ -138,7 +135,7 @@
 
     def attend(pair):
         weights, top, total, shrink = folded.pop(pair)
-        product = contract(values.pop(pair), weights, 1, 0)
+        product = contract(value[pair * LANES : (pair + 1) * LANES], weights, 1, 0)
         summed = jnp.concatenate(
             [
                 product[:HD, :LANES],
@@ -154,8 +151,6 @@
     score(0)
     score(1)
     for pair in range(PAIRS):
-        if pair % 2 == 0:
-            value(pair)
         if pair + 2 < PAIRS:
             score(pair + 2)
         weigh(pair)

time: 37.2 us -> 36.4 us (0.978)
  Pallas kernels: 16 us -> 14 us
  waiting for transfers between devices: 4.02 us -> 5.63 us
    ppermute x3, waiting for transfers between devices: 2.37 us -> 3.9 us  [shards(): next_first = lax.ppermute(first, 'peak', pairs)]
    pallas_call x5, Pallas kernels: 11 us -> 9.47 us  [call(): pl.pallas_call(kernel, out_shape=shapes, in_specs=[spec] * len(operands),...]
    pallas_call x1, Pallas kernels: 3.39 us -> 2.83 us  [shards(): pl.pallas_call(last_kernel, out_shape=[jax.ShapeDtypeStruct((tokens, widt...]
    ppermute x3, starting transfers between devices: 5.92 us -> 5.46 us  [shards(): next_first = lax.ppermute(first, 'peak', pairs)]
  transfers between devices with their start and end apart: 12 -> 12, of which waited for: 4 -> 5; matrix products, arithmetic and copies ran while one was open for 0% -> 0% of each run, Pallas kernels for 34% -> 31%
where the time goes in v4:
time: 36.4 us; the launch traced here: 36.3 us
  starting transfers between devices  14.7 us (40%)
  Pallas kernels  14 us (38%)
  waiting for transfers between devices  5.63 us (15%)
  local copies, waits for them, and re-layouts  1.9 us (5%)
    pallas_call x5, Pallas kernels, call(): pl.pallas_call(kernel, out_shape=shapes, in_specs=[spec] * len(operands),...  9.47 us
    ppermute x3, starting transfers between devices, shards(): next_second = lax.ppermute(second, 'peak', pairs)  8.72 us
    ppermute x3, starting transfers between devices, shards(): next_first = lax.ppermute(first, 'peak', pairs)  5.46 us
    ppermute x3, waiting for transfers between devices, shards(): next_first = lax.ppermute(first, 'peak', pairs)  3.9 us
    pallas_call x1, Pallas kernels, shards(): pl.pallas_call(last_kernel, out_shape=[jax.ShapeDtypeStruct((tokens, widt...  2.83 us
    unnamed x4, local copies, waits for them, and re-layouts  1.89 us
    ppermute x3, waiting for transfers between devices, shards(): next_second = lax.ppermute(second, 'peak', pairs)  1.72 us
    pallas_call x1, Pallas kernels, shards(): pl.pallas_call(embed_kernel, out_shape=[jax.ShapeDtypeStruct((rows, width...  1.65 us
  transfers between devices with their start and end apart: 12, of which 5 were waited for; matrix products, arithmetic and copies ran while one was open for 0% of the time, Pallas kernels for 31%

profile of v4, /device:TPU:0, one launch (start us, length us, event | category | flops | bytes accessed | tf_op | source)
XLA Modules:
  0.0 36.3 jit_solution(2794529076562791601)
XLA Ops:
  0.0 0.5 %collective-permute-start.3 = (bf16[512,3072]{1,0:T(8,128)(2,1)}, bf16[512,3072]{1,0:T(8,128)(2,1)S(1)}, u32[]{:S(2)}, u32[]{:S(2)}) collective-permute-start(bf16[512,3072]{1,0:T(8,128)(2,1)} %weight.1), channel_id=1, source_target_pairs={{0,1},{1,0},{2,3},{3,2},{4,5},{5,4},{6,7},{7,6},{8,9},{9,8},{10,11... | collective-permute-start | bytes 9437192 | tf_op jit(solution)/shard_map/ppermute | solution.py:260
  0.5 0.1 collective-permute-start.11
  0.5 1.6 %shard_map.82 = (bf16[104,1024]{1,0:T(8,128)(2,1)S(1)}, bf16[96,1024]{1,0:T(8,128)(2,1)S(1)}, bf16[8,1024]{1,0:T(8,128)(2,1)S(1)}) custom-call(bf16[192,1024]{1,0:T(8,128)(2,1)} %bitcast.4, s32[1,192]{1,0:T(1,128)} %refs_1_.1, s32[1,192]{1,0:T(1,128)} %refs_2_.1, s32[1,192]{1,0:T(1,128)} %bitcast.6, bf16[51,1024]{1,0:T(8,128)(2,1)} %bitcast.5, ...), custom_call_target="tpu_custom_call" | custom-call | flops 1048576 | bytes 1024 | tf_op jit(solution)/shard_map/pallas_call | solution.py:277
  2.2 3.1 %collective-permute-start.1 = (bf16[104,1024]{1,0:T(8,128)(2,1)S(1)}, bf16[104,1024]{1,0:T(8,128)(2,1)S(1)}, u32[]{:S(2)}, u32[]{:S(2)}) collective-permute-start(bf16[104,1024]{1,0:T(8,128)(2,1)S(1)} %get-tuple-element.31.first), channel_id=1, source_target_pairs={{0,2},{2,6},{6,4},{4,0},{1,3},{3,7},{7,5},{5,1},{8,10},{10,14},{14... | collective-permute-start | bytes 638984 | tf_op jit(solution)/shard_map/ppermute | solution.py:297
  5.2 2.6 %collective-permute-start = (bf16[96,1024]{1,0:T(8,128)(2,1)S(1)}, bf16[96,1024]{1,0:T(8,128)(2,1)S(1)}, u32[]{:S(2)}, u32[]{:S(2)}) collective-permute-start(bf16[96,1024]{1,0:T(8,128)(2,1)S(1)} %get-tuple-element.30.second), channel_id=1, source_target_pairs={{0,2},{2,6},{6,4},{4,0},{1,3},{3,7},{7,5},{5,1},{8,10},{10,14},{14... | collective-permute-start | bytes 589832 | tf_op jit(solution)/shard_map/ppermute | solution.py:298
  7.8 0.0 collective-permute-start.2
  7.8 0.0 copy-start
  7.8 1.9 %copy-done = bf16[512,3072]{1,0:T(8,128)(2,1)S(1)} copy-done((bf16[512,3072]{1,0:T(8,128)(2,1)S(1)}, bf16[512,3072]{1,0:T(8,128)(2,1)}, u32[]{:S(2)}) %copy-start) | copy-done | bytes 3145752
  9.7 1.0 %shard_map.83.weight_here = bf16[512,3072]{1,0:T(8,128)(2,1)S(1)} custom-call(bf16[512,3072]{1,0:T(8,128)(2,1)S(1)} %copy-done), custom_call_target="tpu_custom_call" | custom-call | flops 1048576 | bytes 1024 | tf_op jit(solution)/shard_map/pallas_call | solution.py:23
  10.7 0.0 collective-permute-done.3.weight
  10.8 1.0 %shard_map.84.weight_there = bf16[512,3072]{1,0:T(8,128)(2,1)S(1)} custom-call(bf16[512,3072]{1,0:T(8,128)(2,1)S(1)} %collective-permute-done.3.weight), custom_call_target="tpu_custom_call" | custom-call | flops 1048576 | bytes 1024 | tf_op jit(solution)/shard_map/pallas_call | solution.py:23
  11.8 0.0 collective-permute-done.2.summary
  11.8 0.5 %collective-permute-done.1.arrived = bf16[104,1024]{1,0:T(8,128)(2,1)S(1)} collective-permute-done((bf16[104,1024]{1,0:T(8,128)(2,1)S(1)}, bf16[104,1024]{1,0:T(8,128)(2,1)S(1)}, u32[]{:S(2)}, u32[]{:S(2)}) %collective-permute-start.1) | collective-permute-done | bytes 213024 | tf_op jit(solution)/shard_map/ppermute | solution.py:297
  12.3 1.2 %collective-permute-start.5 = (bf16[104,1024]{1,0:T(8,128)(2,1)S(1)}, bf16[104,1024]{1,0:T(8,128)(2,1)S(1)}, u32[]{:S(2)}, u32[]{:S(2)}) collective-permute-start(bf16[104,1024]{1,0:T(8,128)(2,1)S(1)} %collective-permute-done.1.arrived), channel_id=1, source_target_pairs={{0,2},{2,6},{6,4},{4,0},{1,3},{3,7},{7,5},{5,1},{8,10},{10,14},{14... | collective-permute-start | bytes 638984 | tf_op jit(solution)/shard_map/ppermute | solution.py:297
  13.5 3.4 %shard_map.85 = (bf16[8,128,384]{2,1,0:T(8,128)(2,1)S(1)}, f32[8,384]{1,0:T(8,128)S(1)}, f32[8,384]{1,0:T(8,128)S(1)}, f32[8,64,384]{2,1,0:T(8,128)S(1)}) custom-call(bf16[104,1024]{1,0:T(8,128)(2,1)S(1)} %get-tuple-element.31.first, bf16[96,1024]{1,0:T(8,128)(2,1)S(1)} %get-tuple-element.30.second, bf16[104,1024]{1,0:T(8,128)(2,1)S(1)} %collective-permute-done.1.arrived, ...), custom_call_target="tpu_custom_call" | custom-call | flops 268435456 | bytes 1024 | tf_op jit(solution)/shard_map/pallas_call | solution.py:23
  16.9 0.0 collective-permute-done.second
  16.9 3.4 %collective-permute-start.4 = (bf16[96,1024]{1,0:T(8,128)(2,1)S(1)}, bf16[96,1024]{1,0:T(8,128)(2,1)S(1)}, u32[]{:S(2)}, u32[]{:S(2)}) collective-permute-start(bf16[96,1024]{1,0:T(8,128)(2,1)S(1)} %collective-permute-done.second), channel_id=1, source_target_pairs={{0,2},{2,6},{6,4},{4,0},{1,3},{3,7},{7,5},{5,1},{8,10},{10,14},{14... | collective-permute-start | bytes 589832 | tf_op jit(solution)/shard_map/ppermute | solution.py:298
  20.3 0.0 collective-permute-start.6
  20.3 1.0 %collective-permute-done.5.first = bf16[104,1024]{1,0:T(8,128)(2,1)S(1)} collective-permute-done((bf16[104,1024]{1,0:T(8,128)(2,1)S(1)}, bf16[104,1024]{1,0:T(8,128)(2,1)S(1)}, u32[]{:S(2)}, u32[]{:S(2)}) %collective-permute-start.5) | collective-permute-done | bytes 213024 | tf_op jit(solution)/shard_map/ppermute | solution.py:297
  21.3 1.2 %collective-permute-start.8 = (bf16[104,1024]{1,0:T(8,128)(2,1)S(1)}, bf16[104,1024]{1,0:T(8,128)(2,1)S(1)}, u32[]{:S(2)}, u32[]{:S(2)}) collective-permute-start(bf16[104,1024]{1,0:T(8,128)(2,1)S(1)} %collective-permute-done.5.first), channel_id=1, source_target_pairs={{0,2},{2,6},{6,4},{4,0},{1,3},{3,7},{7,5},{5,1},{8,10},{10,14},{14... | collective-permute-start | bytes 638984 | tf_op jit(solution)/shard_map/ppermute | solution.py:297
  22.6 0.0 collective-permute-done.6.summary
  22.6 2.0 %shard_map.86 = (f32[8,384]{1,0:T(8,128)S(1)}, f32[8,384]{1,0:T(8,128)S(1)}, f32[8,64,384]{2,1,0:T(8,128)S(1)}) custom-call(bf16[96,1024]{1,0:T(8,128)(2,1)S(1)} %collective-permute-done.second, bf16[104,1024]{1,0:T(8,128)(2,1)S(1)} %collective-permute-done.5.first, bf16[8,1024]{1,0:T(8,128)(2,1)S(1)} %collective-permute-done.6.summary, ...), custom_call_target="tpu_custom_call" | custom-call | flops 268435456 | bytes 1024 | tf_op jit(solution)/shard_map/pallas_call | solution.py:23
  24.6 0.7 %collective-permute-done.4.second = bf16[96,1024]{1,0:T(8,128)(2,1)S(1)} collective-permute-done((bf16[96,1024]{1,0:T(8,128)(2,1)S(1)}, bf16[96,1024]{1,0:T(8,128)(2,1)S(1)}, u32[]{:S(2)}, u32[]{:S(2)}) %collective-permute-start.4) | collective-permute-done | bytes 196640 | tf_op jit(solution)/shard_map/ppermute | solution.py:298
  25.3 2.7 %collective-permute-start.7 = (bf16[96,1024]{1,0:T(8,128)(2,1)S(1)}, bf16[96,1024]{1,0:T(8,128)(2,1)S(1)}, u32[]{:S(2)}, u32[]{:S(2)}) collective-permute-start(bf16[96,1024]{1,0:T(8,128)(2,1)S(1)} %collective-permute-done.4.second), channel_id=1, source_target_pairs={{0,2},{2,6},{6,4},{4,0},{1,3},{3,7},{7,5},{5,1},{8,10},{10,14},{14... | collective-permute-start | bytes 589832 | tf_op jit(solution)/shard_map/ppermute | solution.py:298
  28.0 0.0 collective-permute-start.10
  28.0 2.4 %collective-permute-done.8.first = bf16[104,1024]{1,0:T(8,128)(2,1)S(1)} collective-permute-done((bf16[104,1024]{1,0:T(8,128)(2,1)S(1)}, bf16[104,1024]{1,0:T(8,128)(2,1)S(1)}, u32[]{:S(2)}, u32[]{:S(2)}) %collective-permute-start.8) | collective-permute-done | bytes 213024 | tf_op jit(solution)/shard_map/ppermute | solution.py:297
  30.4 0.0 copy-start.1
  30.4 0.0 collective-permute-start.9
  30.4 0.0 collective-permute-done.10.summary
  30.4 2.0 %shard_map.87 = (f32[8,384]{1,0:T(8,128)S(1)}, f32[8,384]{1,0:T(8,128)S(1)}, f32[8,64,384]{2,1,0:T(8,128)S(1)}) custom-call(bf16[96,1024]{1,0:T(8,128)(2,1)S(1)} %collective-permute-done.4.second, bf16[104,1024]{1,0:T(8,128)(2,1)S(1)} %collective-permute-done.8.first, bf16[8,1024]{1,0:T(8,128)(2,1)S(1)} %collective-permute-done.10.summary, ...), custom_call_target="tpu_custom_call" | custom-call | flops 268435456 | bytes 1024 | tf_op jit(solution)/shard_map/pallas_call | solution.py:23
  32.5 0.0 collective-permute-done.11.out_there
  32.5 1.0 %collective-permute-done.7.second = bf16[96,1024]{1,0:T(8,128)(2,1)S(1)} collective-permute-done((bf16[96,1024]{1,0:T(8,128)(2,1)S(1)}, bf16[96,1024]{1,0:T(8,128)(2,1)S(1)}, u32[]{:S(2)}, u32[]{:S(2)}) %collective-permute-start.7) | collective-permute-done | bytes 196640 | tf_op jit(solution)/shard_map/ppermute | solution.py:298
  33.4 0.0 collective-permute-done.9.summary
  33.4 0.0 copy-done.1
  33.5 2.8 %shard_map.88 = bf16[192,1024]{1,0:T(8,128)(2,1)} custom-call(bf16[96,1024]{1,0:T(8,128)(2,1)S(1)} %collective-permute-done.7.second, bf16[8,1024]{1,0:T(8,128)(2,1)S(1)} %collective-permute-done.9.summary, bf16[512,3072]{1,0:T(8,128)(2,1)S(1)} %shard_map.83.weight_here, bf16[512,3072]{1,0:T(8,128)(2,1)S(1)} %shard_map.84.weight_there, ...), custom_call_target="tpu_custom_call" | custom-call | flops 1048576 | bytes 1024 | tf_op jit(solution)/shard_map/pallas_call | solution.py:314
  (3 shorter events, 0.0 us)
Async XLA Ops:
  0.0 10.7 %collective-permute-start.3 = (bf16[512,3072]{1,0:T(8,128)(2,1)}, bf16[512,3072]{1,0:T(8,128)(2,1)S(1)}, u32[]{:S(2)}, u32[]{:S(2)}) collective-permute-start(bf16[512,3072]{1,0:T(8,128)(2,1)} %weight.1), channel_id=1, source_target_pairs={{0,1},{1,0},{2,3},{3,2},{4,5},{5,4},{6,7},{7,6},{8,9},{9,8},{10,11... | collective-permute-start | bytes 9437192 | tf_op jit(solution)/shard_map/ppermute | solution.py:260
  0.5 32.0 %collective-permute-start.11 = (bf16[512,1024]{1,0:T(8,128)(2,1)}, bf16[512,1024]{1,0:T(8,128)(2,1)S(1)}, u32[]{:S(2)}, u32[]{:S(2)}) collective-permute-start(bf16[512,1024]{1,0:T(8,128)(2,1)} %out_here.1), channel_id=1, source_target_pairs={{0,1},{1,0},{2,3},{3,2},{4,5},{5,4},{6,7},{7,6},{8,9},{9,8},{10,11... | collective-permute-start | bytes 3145736 | tf_op jit(solution)/shard_map/ppermute | solution.py:260
  2.2 10.2 %collective-permute-start.1 = (bf16[104,1024]{1,0:T(8,128)(2,1)S(1)}, bf16[104,1024]{1,0:T(8,128)(2,1)S(1)}, u32[]{:S(2)}, u32[]{:S(2)}) collective-permute-start(bf16[104,1024]{1,0:T(8,128)(2,1)S(1)} %get-tuple-element.31.first), channel_id=1, source_target_pairs={{0,2},{2,6},{6,4},{4,0},{1,3},{3,7},{7,5},{5,1},{8,10},{10,14},{14... | collective-permute-start | bytes 638984 | tf_op jit(solution)/shard_map/ppermute | solution.py:297
  5.2 11.6 %collective-permute-start = (bf16[96,1024]{1,0:T(8,128)(2,1)S(1)}, bf16[96,1024]{1,0:T(8,128)(2,1)S(1)}, u32[]{:S(2)}, u32[]{:S(2)}) collective-permute-start(bf16[96,1024]{1,0:T(8,128)(2,1)S(1)} %get-tuple-element.30.second), channel_id=1, source_target_pairs={{0,2},{2,6},{6,4},{4,0},{1,3},{3,7},{7,5},{5,1},{8,10},{10,14},{14... | collective-permute-start | bytes 589832 | tf_op jit(solution)/shard_map/ppermute | solution.py:298
  7.8 3.9 %collective-permute-start.2 = (bf16[8,1024]{1,0:T(8,128)(2,1)S(1)}, bf16[8,1024]{1,0:T(8,128)(2,1)S(1)}, u32[]{:S(2)}, u32[]{:S(2)}) collective-permute-start(bf16[8,1024]{1,0:T(8,128)(2,1)S(1)} %get-tuple-element.32), channel_id=1, source_target_pairs={{0,1},{1,0},{2,3},{3,2},{4,5},{5,4},{6,7},{7,6},{8,9},{9,8},{10,11... | collective-permute-start | bytes 49160 | tf_op jit(solution)/shard_map/ppermute | solution.py:260
  7.8 1.9 %copy-start = (bf16[512,3072]{1,0:T(8,128)(2,1)S(1)}, bf16[512,3072]{1,0:T(8,128)(2,1)}, u32[]{:S(2)}) copy-start(bf16[512,3072]{1,0:T(8,128)(2,1)} %weight.1) | copy-start | bytes 9437188
  12.3 9.0 %collective-permute-start.5 = (bf16[104,1024]{1,0:T(8,128)(2,1)S(1)}, bf16[104,1024]{1,0:T(8,128)(2,1)S(1)}, u32[]{:S(2)}, u32[]{:S(2)}) collective-permute-start(bf16[104,1024]{1,0:T(8,128)(2,1)S(1)} %collective-permute-done.1.arrived), channel_id=1, source_target_pairs={{0,2},{2,6},{6,4},{4,0},{1,3},{3,7},{7,5},{5,1},{8,10},{10,14},{14... | collective-permute-start | bytes 638984 | tf_op jit(solution)/shard_map/ppermute | solution.py:297
  16.9 8.4 %collective-permute-start.4 = (bf16[96,1024]{1,0:T(8,128)(2,1)S(1)}, bf16[96,1024]{1,0:T(8,128)(2,1)S(1)}, u32[]{:S(2)}, u32[]{:S(2)}) collective-permute-start(bf16[96,1024]{1,0:T(8,128)(2,1)S(1)} %collective-permute-done.second), channel_id=1, source_target_pairs={{0,2},{2,6},{6,4},{4,0},{1,3},{3,7},{7,5},{5,1},{8,10},{10,14},{14... | collective-permute-start | bytes 589832 | tf_op jit(solution)/shard_map/ppermute | solution.py:298
  20.3 2.2 %collective-permute-start.6 = (bf16[8,1024]{1,0:T(8,128)(2,1)S(1)}, bf16[8,1024]{1,0:T(8,128)(2,1)S(1)}, u32[]{:S(2)}, u32[]{:S(2)}) collective-permute-start(bf16[8,1024]{1,0:T(8,128)(2,1)S(1)} %slice.9), channel_id=1, source_target_pairs={{0,1},{1,0},{2,3},{3,2},{4,5},{5,4},{6,7},{7,6},{8,9},{9,8},{10,11... | collective-permute-start | bytes 49160 | tf_op jit(solution)/shard_map/ppermute | solution.py:260
  21.3 9.1 %collective-permute-start.8 = (bf16[104,1024]{1,0:T(8,128)(2,1)S(1)}, bf16[104,1024]{1,0:T(8,128)(2,1)S(1)}, u32[]{:S(2)}, u32[]{:S(2)}) collective-permute-start(bf16[104,1024]{1,0:T(8,128)(2,1)S(1)} %collective-permute-done.5.first), channel_id=1, source_target_pairs={{0,2},{2,6},{6,4},{4,0},{1,3},{3,7},{7,5},{5,1},{8,10},{10,14},{14... | collective-permute-start | bytes 638984 | tf_op jit(solution)/shard_map/ppermute | solution.py:297
  25.3 8.1 %collective-permute-start.7 = (bf16[96,1024]{1,0:T(8,128)(2,1)S(1)}, bf16[96,1024]{1,0:T(8,128)(2,1)S(1)}, u32[]{:S(2)}, u32[]{:S(2)}) collective-permute-start(bf16[96,1024]{1,0:T(8,128)(2,1)S(1)} %collective-permute-done.4.second), channel_id=1, source_target_pairs={{0,2},{2,6},{6,4},{4,0},{1,3},{3,7},{7,5},{5,1},{8,10},{10,14},{14... | collective-permute-start | bytes 589832 | tf_op jit(solution)/shard_map/ppermute | solution.py:298
  28.0 2.4 %collective-permute-start.10 = (bf16[8,1024]{1,0:T(8,128)(2,1)S(1)}, bf16[8,1024]{1,0:T(8,128)(2,1)S(1)}, u32[]{:S(2)}, u32[]{:S(2)}) collective-permute-start(bf16[8,1024]{1,0:T(8,128)(2,1)S(1)} %slice.13), channel_id=1, source_target_pairs={{0,1},{1,0},{2,3},{3,2},{4,5},{5,4},{6,7},{7,6},{8,9},{9,8},{10,11... | collective-permute-start | bytes 49160 | tf_op jit(solution)/shard_map/ppermute | solution.py:260
  30.4 3.0 %copy-start.1 = (bf16[512,1024]{1,0:T(8,128)(2,1)S(1)}, bf16[512,1024]{1,0:T(8,128)(2,1)}, u32[]{:S(2)}) copy-start(bf16[512,1024]{1,0:T(8,128)(2,1)} %out_here.1) | copy-start | bytes 3145732
  30.4 3.0 %collective-permute-start.9 = (bf16[8,1024]{1,0:T(8,128)(2,1)S(1)}, bf16[8,1024]{1,0:T(8,128)(2,1)S(1)}, u32[]{:S(2)}, u32[]{:S(2)}) collective-permute-start(bf16[8,1024]{1,0:T(8,128)(2,1)S(1)} %slice.12), channel_id=1, source_target_pairs={{0,1},{1,0},{2,3},{3,2},{4,5},{5,4},{6,7},{7,6},{8,9},{9,8},{10,11... | collective-permute-start | bytes 49160 | tf_op jit(solution)/shard_map/ppermute | solution.py:260

commit v5 on v4

--- a/solution.py
+++ b/solution.py
@@ -63,6 +63,7 @@
     is_mean = lax.broadcasted_iota(jnp.int32, (2 * SEG_DEV, half), 0) < SEG_DEV
     starts = [pl.multiple_of(lax.rem(mod + part, 2) * half, half) for part in range(2)]
     bin_parts = [contract(one_hot, table[:, pl.ds(start, half)], 0, 0) for start in starts]
+    means = []
     moves[0].wait()
     for part, (start, bin_rows) in enumerate(zip(starts, bin_parts)):
         chosen = jnp.where(
@@ -72,12 +73,17 @@
         )
         embedded = (chosen + bin_rows).astype(BF16)
         columns = pl.ds(part * half, half)
-        first[:cut, columns] = embedded[:cut]
+        for tile in range(half // LANES):
+            at = (part * (half // LANES) + tile) * cut
+            first[at : at + cut, :] = embedded[:cut, tile * LANES : (tile + 1) * LANES]
         second[:, columns] = embedded[cut:]
-        sums = contract(picks, embedded, 1, 0)
-        crossed = pl.ds((1 - part) * half, half)
-        summary[:, crossed] = jnp.where(is_mean, sums / counts, jnp.log(counts)).astype(BF16)
-        first[cut:, crossed] = summary[:, crossed]
+        means.append(contract(picks, embedded, 1, 0) / counts)
+    both = jnp.where(is_mean, means[1], means[0])
+    bias = jnp.broadcast_to(jnp.log(counts), (2 * SEG_DEV, LANES))
+    tiles = [both[:, at : at + LANES] for at in range(0, half, LANES)]
+    packed = jnp.concatenate(tiles + [bias], axis=0).astype(BF16)
+    summary[...] = packed
+    first[first.shape[0] - packed.shape[0] :, :] = packed
 
 
 def arrange_kernel(weight, arranged):
@@ -159,16 +165,20 @@
     attend(PAIRS - 1)
 
 
-def bias_of(rows):
-    edge = rows.shape[0] - 2 * SEG_DEV
-    wide = 3 * LANES
-    return jnp.concatenate(
-        [
-            rows[edge:, :wide].astype(F32)[SEG_DEV:],
-            jnp.full((SEG_DEV, wide), NEVER, F32),
-        ],
-        axis=0,
-    )
+def tokens_of(first, width):
+    count = width // LANES
+    cut = (first.shape[0] - (count // 2 + 1) * 2 * SEG_DEV) // count
+    return jnp.concatenate([first[tile * cut : (tile + 1) * cut, :] for tile in range(count)], axis=1)
+
+
+def summaries_of(packed):
+    rows = 2 * SEG_DEV
+    tiles = packed[...].astype(F32)
+    tiles = [tiles[at : at + rows] for at in range(0, packed.shape[0], rows)]
+    turned = [jnp.concatenate([tile[SEG_DEV:], tile[:SEG_DEV]], axis=0) for tile in tiles[:-1]]
+    means = jnp.concatenate(tiles[:-1] + turned, axis=1).astype(BF16)
+    is_key = lax.broadcasted_iota(jnp.int32, (rows, 3 * LANES), 0) < SEG_DEV
+    return means, jnp.where(is_key, jnp.concatenate([tiles[-1]] * 3, axis=1), NEVER)
 
 
 def store_state(top_ref, total_ref, summed_ref):
@@ -184,10 +194,10 @@
     first, second, arrived, summary, weight_here, weight_there,
     turned, top_ref, total_ref, summed_ref,
 ):
-    cut = second.shape[0]
-    width = H * HD
+    cut, width = second.shape
+    means, bias = summaries_of(summary)
     rows = jnp.concatenate(
-        [first[:cut, :], second[...], arrived[:cut, :], summary[...]], axis=0
+        [tokens_of(first, width), second[...], tokens_of(arrived, width), means], axis=0
     )
     query = project(rows[: 2 * cut], weight_here, weight_there, 0, width).astype(BF16)
     query = query.astype(F32) * (float(HD) ** -0.5)
@@ -204,7 +214,7 @@
             axis=0,
         ).astype(BF16)
     fold(
-        rows, bias_of(summary), weight_here, weight_there, turned, None,
+        rows, bias, weight_here, weight_there, turned, None,
         store_state(top_ref, total_ref, summed_ref),
     )
 
@@ -213,10 +223,10 @@
     second, first, summary, weight_here, weight_there, turned, top_in, total_in, summed_in,
     top_ref, total_ref, summed_ref,
 ):
-    cut = second.shape[0]
-    rows = jnp.concatenate([second[...], first[:cut, :], summary[...]], axis=0)
+    means, bias = summaries_of(summary)
+    rows = jnp.concatenate([second[...], tokens_of(first, second.shape[1]), means], axis=0)
     fold(
-        rows, bias_of(summary), weight_here, weight_there, turned, (top_in, total_in, summed_in),
+        rows, bias, weight_here, weight_there, turned, (top_in, total_in, summed_in),
         store_state(top_ref, total_ref, summed_ref),
     )
 
@@ -234,8 +244,9 @@
                 [done[:, odd * LANES : (odd + 1) * LANES], done[:, rest : rest + HD]], axis=1
             )
 
+    means, bias = summaries_of(summary)
     fold(
-        jnp.concatenate([second[...], summary[...]], axis=0), bias_of(summary), weight_here, weight_there, turned,
+        jnp.concatenate([second[...], means], axis=0), bias, weight_here, weight_there, turned,
         (top_in, total_in, summed_in), finish,
     )
     half = out_here.shape[0]
@@ -265,6 +276,7 @@
 ):
     tokens, width = hidden_in.shape[1:]
     cut = tokens // 2
+    extra = (width // LANES // 2 + 1) * 2 * SEG_DEV
     size = lax.axis_size("peak")
     pairs = ring_pairs(size)
     state_shapes = [((PAIRS, 2 * tokens), F32)] * 2 + [((PAIRS, HD, 2 * tokens), F32)]
@@ -277,7 +289,9 @@
     first, second, summary = pl.pallas_call(
         embed_kernel,
         out_shape=[
-            jax.ShapeDtypeStruct((rows, width), BF16) for rows in (cut + 2 * SEG_DEV, cut, 2 * SEG_DEV)
+            jax.ShapeDtypeStruct((cut * width // LANES + extra, LANES), BF16),
+            jax.ShapeDtypeStruct((tokens - cut, width), BF16),
+            jax.ShapeDtypeStruct((extra, LANES), BF16),
         ],
         in_specs=[pl.BlockSpec(memory_space=pltpu.HBM)] * len(operands),
         out_specs=[vmem] * 3,
@@ -310,7 +324,7 @@
         if step < size - 2:
             next_second, *state = after(next_second, *state)
         first, second = next_first, next_second
-        summary = swapped(first[cut:])
+        summary = swapped(first[first.shape[0] - extra :])
     (update,) = pl.pallas_call(
         last_kernel,
         out_shape=[jax.ShapeDtypeStruct((tokens, width), BF16)],

time: 36.4 us -> 36.1 us (level)
    ppermute x3, waiting for transfers between devices: 3.9 us -> 3.22 us  [shards(): next_first = lax.ppermute(first, 'peak', pairs)]
    ppermute x3, waiting for transfers between devices: 1.72 us -> 2.1 us  [shards(): next_second = lax.ppermute(second, 'peak', pairs)]
where the time goes in v5:
time: 36.1 us; the launch traced here: 36 us
  starting transfers between devices  14.6 us (40%)
  Pallas kernels  14 us (39%)
  waiting for transfers between devices  5.34 us (15%)
  local copies, waits for them, and re-layouts  1.9 us (5%)
    pallas_call x5, Pallas kernels, call(): pl.pallas_call(kernel, out_shape=shapes, in_specs=[spec] * len(operands),...  9.51 us
    ppermute x3, starting transfers between devices, shards(): next_second = lax.ppermute(second, 'peak', pairs)  8.55 us
    ppermute x3, starting transfers between devices, shards(): next_first = lax.ppermute(first, 'peak', pairs)  5.57 us
    ppermute x3, waiting for transfers between devices, shards(): next_first = lax.ppermute(first, 'peak', pairs)  3.22 us
    pallas_call x1, Pallas kernels, shards(): pl.pallas_call(last_kernel, out_shape=[jax.ShapeDtypeStruct((tokens, widt...  2.86 us
    ppermute x3, waiting for transfers between devices, shards(): next_second = lax.ppermute(second, 'peak', pairs)  2.1 us
    unnamed x4, local copies, waits for them, and re-layouts  1.89 us
    pallas_call x1, Pallas kernels, shards(): pl.pallas_call(embed_kernel, out_shape=[jax.ShapeDtypeStruct((cut * width...  1.64 us
  transfers between devices with their start and end apart: 12, of which 5 were waited for; matrix products, arithmetic and copies ran while one was open for 0% of the time, Pallas kernels for 31%

profile of v5, /device:TPU:0, one launch (start us, length us, event | category | flops | bytes accessed | tf_op | source)
XLA Modules:
  0.0 36.0 jit_solution(4650033858501902859)
XLA Ops:
  0.0 0.5 %collective-permute-start.3 = (bf16[512,3072]{1,0:T(8,128)(2,1)}, bf16[512,3072]{1,0:T(8,128)(2,1)S(1)}, u32[]{:S(2)}, u32[]{:S(2)}) collective-permute-start(bf16[512,3072]{1,0:T(8,128)(2,1)} %weight.1), channel_id=1, source_target_pairs={{0,1},{1,0},{2,3},{3,2},{4,5},{5,4},{6,7},{7,6},{8,9},{9,8},{10,11... | collective-permute-start | bytes 9437192 | tf_op jit(solution)/shard_map/ppermute | solution.py:271
  0.5 0.1 collective-permute-start.11
  0.5 1.6 %shard_map.82 = (bf16[808,128]{1,0:T(8,128)(2,1)S(1)}, bf16[96,1024]{1,0:T(8,128)(2,1)S(1)}, bf16[40,128]{1,0:T(8,128)(2,1)S(1)}) custom-call(bf16[192,1024]{1,0:T(8,128)(2,1)} %bitcast.4, s32[1,192]{1,0:T(1,128)} %refs_1_.1, s32[1,192]{1,0:T(1,128)} %refs_2_.1, s32[1,192]{1,0:T(1,128)} %bitcast.6, bf16[51,1024]{1,0:T(8,128)(2,1)} %bitcast.5, ...), custom_call_target="tpu_custom_call" | custom-call | flops 1048576 | bytes 1024 | tf_op jit(solution)/shard_map/pallas_call | solution.py:289
  2.2 3.1 %collective-permute-start.1 = (bf16[808,128]{1,0:T(8,128)(2,1)S(1)}, bf16[808,128]{1,0:T(8,128)(2,1)S(1)}, u32[]{:S(2)}, u32[]{:S(2)}) collective-permute-start(bf16[808,128]{1,0:T(8,128)(2,1)S(1)} %get-tuple-element.31.first), channel_id=1, source_target_pairs={{0,2},{2,6},{6,4},{4,0},{1,3},{3,7},{7,5},{5,1},{8,10},{10,14},{14... | collective-permute-start | bytes 620552 | tf_op jit(solution)/shard_map/ppermute | solution.py:311
  5.2 2.6 %collective-permute-start = (bf16[96,1024]{1,0:T(8,128)(2,1)S(1)}, bf16[96,1024]{1,0:T(8,128)(2,1)S(1)}, u32[]{:S(2)}, u32[]{:S(2)}) collective-permute-start(bf16[96,1024]{1,0:T(8,128)(2,1)S(1)} %get-tuple-element.30.second), channel_id=1, source_target_pairs={{0,2},{2,6},{6,4},{4,0},{1,3},{3,7},{7,5},{5,1},{8,10},{10,14},{14... | collective-permute-start | bytes 589832 | tf_op jit(solution)/shard_map/ppermute | solution.py:312
  7.8 0.0 collective-permute-start.2
  7.8 0.0 copy-start
  7.8 1.9 %copy-done = bf16[512,3072]{1,0:T(8,128)(2,1)S(1)} copy-done((bf16[512,3072]{1,0:T(8,128)(2,1)S(1)}, bf16[512,3072]{1,0:T(8,128)(2,1)}, u32[]{:S(2)}) %copy-start) | copy-done | bytes 3145752
  9.7 1.0 %shard_map.83.weight_here = bf16[512,3072]{1,0:T(8,128)(2,1)S(1)} custom-call(bf16[512,3072]{1,0:T(8,128)(2,1)S(1)} %copy-done), custom_call_target="tpu_custom_call" | custom-call | flops 1048576 | bytes 1024 | tf_op jit(solution)/shard_map/pallas_call | solution.py:23
  10.7 0.0 collective-permute-done.3.weight
  10.7 1.0 %shard_map.84.weight_there = bf16[512,3072]{1,0:T(8,128)(2,1)S(1)} custom-call(bf16[512,3072]{1,0:T(8,128)(2,1)S(1)} %collective-permute-done.3.weight), custom_call_target="tpu_custom_call" | custom-call | flops 1048576 | bytes 1024 | tf_op jit(solution)/shard_map/pallas_call | solution.py:23
  11.8 0.0 collective-permute-done.2.summary
  11.8 0.4 %collective-permute-done.1.arrived = bf16[808,128]{1,0:T(8,128)(2,1)S(1)} collective-permute-done((bf16[808,128]{1,0:T(8,128)(2,1)S(1)}, bf16[808,128]{1,0:T(8,128)(2,1)S(1)}, u32[]{:S(2)}, u32[]{:S(2)}) %collective-permute-start.1) | collective-permute-done | bytes 206880 | tf_op jit(solution)/shard_map/ppermute | solution.py:311
  12.2 1.2 %collective-permute-start.5 = (bf16[808,128]{1,0:T(8,128)(2,1)S(1)}, bf16[808,128]{1,0:T(8,128)(2,1)S(1)}, u32[]{:S(2)}, u32[]{:S(2)}) collective-permute-start(bf16[808,128]{1,0:T(8,128)(2,1)S(1)} %collective-permute-done.1.arrived), channel_id=1, source_target_pairs={{0,2},{2,6},{6,4},{4,0},{1,3},{3,7},{7,5},{5,1},{8,10},{10,14},{14... | collective-permute-start | bytes 620552 | tf_op jit(solution)/shard_map/ppermute | solution.py:311
  13.3 3.4 %shard_map.85 = (bf16[8,128,384]{2,1,0:T(8,128)(2,1)S(1)}, f32[8,384]{1,0:T(8,128)S(1)}, f32[8,384]{1,0:T(8,128)S(1)}, f32[8,64,384]{2,1,0:T(8,128)S(1)}) custom-call(bf16[808,128]{1,0:T(8,128)(2,1)S(1)} %get-tuple-element.31.first, bf16[96,1024]{1,0:T(8,128)(2,1)S(1)} %get-tuple-element.30.second, bf16[808,128]{1,0:T(8,128)(2,1)S(1)} %collective-permute-done.1.arrived, ...), custom_call_target="tpu_custom_call" | custom-call | flops 268435456 | bytes 1024 | tf_op jit(solution)/shard_map/pallas_call | solution.py:23
  16.8 0.0 collective-permute-done.second
  16.8 3.4 %collective-permute-start.4 = (bf16[96,1024]{1,0:T(8,128)(2,1)S(1)}, bf16[96,1024]{1,0:T(8,128)(2,1)S(1)}, u32[]{:S(2)}, u32[]{:S(2)}) collective-permute-start(bf16[96,1024]{1,0:T(8,128)(2,1)S(1)} %collective-permute-done.second), channel_id=1, source_target_pairs={{0,2},{2,6},{6,4},{4,0},{1,3},{3,7},{7,5},{5,1},{8,10},{10,14},{14... | collective-permute-start | bytes 589832 | tf_op jit(solution)/shard_map/ppermute | solution.py:312
  20.2 0.0 collective-permute-start.6
  20.2 0.7 %collective-permute-done.5.first = bf16[808,128]{1,0:T(8,128)(2,1)S(1)} collective-permute-done((bf16[808,128]{1,0:T(8,128)(2,1)S(1)}, bf16[808,128]{1,0:T(8,128)(2,1)S(1)}, u32[]{:S(2)}, u32[]{:S(2)}) %collective-permute-start.5) | collective-permute-done | bytes 206880 | tf_op jit(solution)/shard_map/ppermute | solution.py:311
  21.0 1.3 %collective-permute-start.8 = (bf16[808,128]{1,0:T(8,128)(2,1)S(1)}, bf16[808,128]{1,0:T(8,128)(2,1)S(1)}, u32[]{:S(2)}, u32[]{:S(2)}) collective-permute-start(bf16[808,128]{1,0:T(8,128)(2,1)S(1)} %collective-permute-done.5.first), channel_id=1, source_target_pairs={{0,2},{2,6},{6,4},{4,0},{1,3},{3,7},{7,5},{5,1},{8,10},{10,14},{14... | collective-permute-start | bytes 620552 | tf_op jit(solution)/shard_map/ppermute | solution.py:311
  22.3 0.0 collective-permute-done.6.summary
  22.3 2.0 %shard_map.86 = (f32[8,384]{1,0:T(8,128)S(1)}, f32[8,384]{1,0:T(8,128)S(1)}, f32[8,64,384]{2,1,0:T(8,128)S(1)}) custom-call(bf16[96,1024]{1,0:T(8,128)(2,1)S(1)} %collective-permute-done.second, bf16[808,128]{1,0:T(8,128)(2,1)S(1)} %collective-permute-done.5.first, bf16[40,128]{1,0:T(8,128)(2,1)S(1)} %collective-permute-done.6.summary, ...), custom_call_target="tpu_custom_call" | custom-call | flops 268435456 | bytes 1024 | tf_op jit(solution)/shard_map/pallas_call | solution.py:23
  24.3 0.9 %collective-permute-done.4.second = bf16[96,1024]{1,0:T(8,128)(2,1)S(1)} collective-permute-done((bf16[96,1024]{1,0:T(8,128)(2,1)S(1)}, bf16[96,1024]{1,0:T(8,128)(2,1)S(1)}, u32[]{:S(2)}, u32[]{:S(2)}) %collective-permute-start.4) | collective-permute-done | bytes 196640 | tf_op jit(solution)/shard_map/ppermute | solution.py:312
  25.3 2.5 %collective-permute-start.7 = (bf16[96,1024]{1,0:T(8,128)(2,1)S(1)}, bf16[96,1024]{1,0:T(8,128)(2,1)S(1)}, u32[]{:S(2)}, u32[]{:S(2)}) collective-permute-start(bf16[96,1024]{1,0:T(8,128)(2,1)S(1)} %collective-permute-done.4.second), channel_id=1, source_target_pairs={{0,2},{2,6},{6,4},{4,0},{1,3},{3,7},{7,5},{5,1},{8,10},{10,14},{14... | collective-permute-start | bytes 589832 | tf_op jit(solution)/shard_map/ppermute | solution.py:312
  27.8 0.0 collective-permute-start.10
  27.8 2.1 %collective-permute-done.8.first = bf16[808,128]{1,0:T(8,128)(2,1)S(1)} collective-permute-done((bf16[808,128]{1,0:T(8,128)(2,1)S(1)}, bf16[808,128]{1,0:T(8,128)(2,1)S(1)}, u32[]{:S(2)}, u32[]{:S(2)}) %collective-permute-start.8) | collective-permute-done | bytes 206880 | tf_op jit(solution)/shard_map/ppermute | solution.py:311
  29.9 0.0 copy-start.1
  29.9 0.0 collective-permute-start.9
  29.9 0.0 collective-permute-done.10.summary
  29.9 2.0 %shard_map.87 = (f32[8,384]{1,0:T(8,128)S(1)}, f32[8,384]{1,0:T(8,128)S(1)}, f32[8,64,384]{2,1,0:T(8,128)S(1)}) custom-call(bf16[96,1024]{1,0:T(8,128)(2,1)S(1)} %collective-permute-done.4.second, bf16[808,128]{1,0:T(8,128)(2,1)S(1)} %collective-permute-done.8.first, bf16[40,128]{1,0:T(8,128)(2,1)S(1)} %collective-permute-done.10.summary, ...), custom_call_target="tpu_custom_call" | custom-call | flops 268435456 | bytes 1024 | tf_op jit(solution)/shard_map/pallas_call | solution.py:23
  31.9 0.0 collective-permute-done.11.out_there
  32.0 1.2 %collective-permute-done.7.second = bf16[96,1024]{1,0:T(8,128)(2,1)S(1)} collective-permute-done((bf16[96,1024]{1,0:T(8,128)(2,1)S(1)}, bf16[96,1024]{1,0:T(8,128)(2,1)S(1)}, u32[]{:S(2)}, u32[]{:S(2)}) %collective-permute-start.7) | collective-permute-done | bytes 196640 | tf_op jit(solution)/shard_map/ppermute | solution.py:312
  33.1 0.0 collective-permute-done.9.summary
  33.1 0.0 copy-done.1
  33.1 2.9 %shard_map.88 = bf16[192,1024]{1,0:T(8,128)(2,1)} custom-call(bf16[96,1024]{1,0:T(8,128)(2,1)S(1)} %collective-permute-done.7.second, bf16[40,128]{1,0:T(8,128)(2,1)S(1)} %collective-permute-done.9.summary, bf16[512,3072]{1,0:T(8,128)(2,1)S(1)} %shard_map.83.weight_here, bf16[512,3072]{1,0:T(8,128)(2,1)S(1)} %shard_map.84.weight_there, ...), custom_call_target="tpu_custom_call" | custom-call | flops 1048576 | bytes 1024 | tf_op jit(solution)/shard_map/pallas_call | solution.py:328
  (3 shorter events, 0.0 us)
Async XLA Ops:
  0.0 10.7 %collective-permute-start.3 = (bf16[512,3072]{1,0:T(8,128)(2,1)}, bf16[512,3072]{1,0:T(8,128)(2,1)S(1)}, u32[]{:S(2)}, u32[]{:S(2)}) collective-permute-start(bf16[512,3072]{1,0:T(8,128)(2,1)} %weight.1), channel_id=1, source_target_pairs={{0,1},{1,0},{2,3},{3,2},{4,5},{5,4},{6,7},{7,6},{8,9},{9,8},{10,11... | collective-permute-start | bytes 9437192 | tf_op jit(solution)/shard_map/ppermute | solution.py:271
  0.5 31.5 %collective-permute-start.11 = (bf16[512,1024]{1,0:T(8,128)(2,1)}, bf16[512,1024]{1,0:T(8,128)(2,1)S(1)}, u32[]{:S(2)}, u32[]{:S(2)}) collective-permute-start(bf16[512,1024]{1,0:T(8,128)(2,1)} %out_here.1), channel_id=1, source_target_pairs={{0,1},{1,0},{2,3},{3,2},{4,5},{5,4},{6,7},{7,6},{8,9},{9,8},{10,11... | collective-permute-start | bytes 3145736 | tf_op jit(solution)/shard_map/ppermute | solution.py:271
  2.2 10.0 %collective-permute-start.1 = (bf16[808,128]{1,0:T(8,128)(2,1)S(1)}, bf16[808,128]{1,0:T(8,128)(2,1)S(1)}, u32[]{:S(2)}, u32[]{:S(2)}) collective-permute-start(bf16[808,128]{1,0:T(8,128)(2,1)S(1)} %get-tuple-element.31.first), channel_id=1, source_target_pairs={{0,2},{2,6},{6,4},{4,0},{1,3},{3,7},{7,5},{5,1},{8,10},{10,14},{14... | collective-permute-start | bytes 620552 | tf_op jit(solution)/shard_map/ppermute | solution.py:311
  5.2 11.5 %collective-permute-start = (bf16[96,1024]{1,0:T(8,128)(2,1)S(1)}, bf16[96,1024]{1,0:T(8,128)(2,1)S(1)}, u32[]{:S(2)}, u32[]{:S(2)}) collective-permute-start(bf16[96,1024]{1,0:T(8,128)(2,1)S(1)} %get-tuple-element.30.second), channel_id=1, source_target_pairs={{0,2},{2,6},{6,4},{4,0},{1,3},{3,7},{7,5},{5,1},{8,10},{10,14},{14... | collective-permute-start | bytes 589832 | tf_op jit(solution)/shard_map/ppermute | solution.py:312
  7.8 3.9 %collective-permute-start.2 = (bf16[40,128]{1,0:T(8,128)(2,1)S(1)}, bf16[40,128]{1,0:T(8,128)(2,1)S(1)}, u32[]{:S(2)}, u32[]{:S(2)}) collective-permute-start(bf16[40,128]{1,0:T(8,128)(2,1)S(1)} %get-tuple-element.32), channel_id=1, source_target_pairs={{0,1},{1,0},{2,3},{3,2},{4,5},{5,4},{6,7},{7,6},{8,9},{9,8},{10,11... | collective-permute-start | bytes 30728 | tf_op jit(solution)/shard_map/ppermute | solution.py:271
  7.8 1.9 %copy-start = (bf16[512,3072]{1,0:T(8,128)(2,1)S(1)}, bf16[512,3072]{1,0:T(8,128)(2,1)}, u32[]{:S(2)}) copy-start(bf16[512,3072]{1,0:T(8,128)(2,1)} %weight.1) | copy-start | bytes 9437188
  12.2 8.8 %collective-permute-start.5 = (bf16[808,128]{1,0:T(8,128)(2,1)S(1)}, bf16[808,128]{1,0:T(8,128)(2,1)S(1)}, u32[]{:S(2)}, u32[]{:S(2)}) collective-permute-start(bf16[808,128]{1,0:T(8,128)(2,1)S(1)} %collective-permute-done.1.arrived), channel_id=1, source_target_pairs={{0,2},{2,6},{6,4},{4,0},{1,3},{3,7},{7,5},{5,1},{8,10},{10,14},{14... | collective-permute-start | bytes 620552 | tf_op jit(solution)/shard_map/ppermute | solution.py:311
  16.8 8.5 %collective-permute-start.4 = (bf16[96,1024]{1,0:T(8,128)(2,1)S(1)}, bf16[96,1024]{1,0:T(8,128)(2,1)S(1)}, u32[]{:S(2)}, u32[]{:S(2)}) collective-permute-start(bf16[96,1024]{1,0:T(8,128)(2,1)S(1)} %collective-permute-done.second), channel_id=1, source_target_pairs={{0,2},{2,6},{6,4},{4,0},{1,3},{3,7},{7,5},{5,1},{8,10},{10,14},{14... | collective-permute-start | bytes 589832 | tf_op jit(solution)/shard_map/ppermute | solution.py:312
  20.2 2.1 %collective-permute-start.6 = (bf16[40,128]{1,0:T(8,128)(2,1)S(1)}, bf16[40,128]{1,0:T(8,128)(2,1)S(1)}, u32[]{:S(2)}, u32[]{:S(2)}) collective-permute-start(bf16[40,128]{1,0:T(8,128)(2,1)S(1)} %slice.9), channel_id=1, source_target_pairs={{0,1},{1,0},{2,3},{3,2},{4,5},{5,4},{6,7},{7,6},{8,9},{9,8},{10,11... | collective-permute-start | bytes 30728 | tf_op jit(solution)/shard_map/ppermute | solution.py:271
  21.0 8.9 %collective-permute-start.8 = (bf16[808,128]{1,0:T(8,128)(2,1)S(1)}, bf16[808,128]{1,0:T(8,128)(2,1)S(1)}, u32[]{:S(2)}, u32[]{:S(2)}) collective-permute-start(bf16[808,128]{1,0:T(8,128)(2,1)S(1)} %collective-permute-done.5.first), channel_id=1, source_target_pairs={{0,2},{2,6},{6,4},{4,0},{1,3},{3,7},{7,5},{5,1},{8,10},{10,14},{14... | collective-permute-start | bytes 620552 | tf_op jit(solution)/shard_map/ppermute | solution.py:311
  25.3 7.9 %collective-permute-start.7 = (bf16[96,1024]{1,0:T(8,128)(2,1)S(1)}, bf16[96,1024]{1,0:T(8,128)(2,1)S(1)}, u32[]{:S(2)}, u32[]{:S(2)}) collective-permute-start(bf16[96,1024]{1,0:T(8,128)(2,1)S(1)} %collective-permute-done.4.second), channel_id=1, source_target_pairs={{0,2},{2,6},{6,4},{4,0},{1,3},{3,7},{7,5},{5,1},{8,10},{10,14},{14... | collective-permute-start | bytes 589832 | tf_op jit(solution)/shard_map/ppermute | solution.py:312
  27.8 2.1 %collective-permute-start.10 = (bf16[40,128]{1,0:T(8,128)(2,1)S(1)}, bf16[40,128]{1,0:T(8,128)(2,1)S(1)}, u32[]{:S(2)}, u32[]{:S(2)}) collective-permute-start(bf16[40,128]{1,0:T(8,128)(2,1)S(1)} %slice.13), channel_id=1, source_target_pairs={{0,1},{1,0},{2,3},{3,2},{4,5},{5,4},{6,7},{7,6},{8,9},{9,8},{10,11... | collective-permute-start | bytes 30728 | tf_op jit(solution)/shard_map/ppermute | solution.py:271
  29.9 3.3 %copy-start.1 = (bf16[512,1024]{1,0:T(8,128)(2,1)S(1)}, bf16[512,1024]{1,0:T(8,128)(2,1)}, u32[]{:S(2)}) copy-start(bf16[512,1024]{1,0:T(8,128)(2,1)} %out_here.1) | copy-start | bytes 3145732
  29.9 3.3 %collective-permute-start.9 = (bf16[40,128]{1,0:T(8,128)(2,1)S(1)}, bf16[40,128]{1,0:T(8,128)(2,1)S(1)}, u32[]{:S(2)}, u32[]{:S(2)}) collective-permute-start(bf16[40,128]{1,0:T(8,128)(2,1)S(1)} %slice.12), channel_id=1, source_target_pairs={{0,1},{1,0},{2,3},{3,2},{4,5},{5,4},{6,7},{7,6},{8,9},{9,8},{10,11... | collective-permute-start | bytes 30728 | tf_op jit(solution)/shard_map/ppermute | solution.py:271

commit v6 on v5

--- a/solution.py
+++ b/solution.py
@@ -260,7 +260,7 @@
 
 def ring_pairs(size):
     order = [0] + list(range(1, size, 2)) + list(reversed(range(2, size, 2)))
-    return [(order[i], order[(i + 1) % size]) for i in range(size)]
+    return [(order[(i + 1) % size], order[i]) for i in range(size)]
 
 
 def after(*values):

time: 36.1 us -> 36 us (level)
  waiting for transfers between devices: 5.34 us -> 3.95 us
  starting transfers between devices: 14.6 us -> 15.8 us
    ppermute x3, starting transfers between devices: 5.57 us -> 10.8 us  [shards(): next_first = lax.ppermute(first, 'peak', pairs)]
    ppermute x3, starting transfers between devices: 8.55 us -> 4.5 us  [shards(): next_second = lax.ppermute(second, 'peak', pairs)]
    ppermute x3, waiting for transfers between devices: 2.1 us -> 0.3 us  [shards(): next_second = lax.ppermute(second, 'peak', pairs)]
    ppermute x3, waiting for transfers between devices: 3.22 us -> 3.63 us  [shards(): next_first = lax.ppermute(first, 'peak', pairs)]
  transfers between devices with their start and end apart: 12 -> 12, of which waited for: 5 -> 3; matrix products, arithmetic and copies ran while one was open for 0% -> 0% of each run, Pallas kernels for 31% -> 31%
where the time goes in v6:
time: 36 us; the launch traced here: 35.8 us
  starting transfers between devices  15.8 us (44%)
  Pallas kernels  14 us (39%)
  waiting for transfers between devices  3.95 us (11%)
  local copies, waits for them, and re-layouts  1.9 us (5%)
    ppermute x3, starting transfers between devices, shards(): next_first = lax.ppermute(first, 'peak', pairs)  10.8 us
    pallas_call x5, Pallas kernels, call(): pl.pallas_call(kernel, out_shape=shapes, in_specs=[spec] * len(operands),...  9.52 us
    ppermute x3, starting transfers between devices, shards(): next_second = lax.ppermute(second, 'peak', pairs)  4.5 us
    ppermute x3, waiting for transfers between devices, shards(): next_first = lax.ppermute(first, 'peak', pairs)  3.63 us
    pallas_call x1, Pallas kernels, shards(): pl.pallas_call(last_kernel, out_shape=[jax.ShapeDtypeStruct((tokens, widt...  2.85 us
    unnamed x4, local copies, waits for them, and re-layouts  1.89 us
    pallas_call x1, Pallas kernels, shards(): pl.pallas_call(embed_kernel, out_shape=[jax.ShapeDtypeStruct((cut * width...  1.64 us
  transfers between devices with their start and end apart: 12, of which 3 were waited for; matrix products, arithmetic and copies ran while one was open for 0% of the time, Pallas kernels for 31%

profile of v6, /device:TPU:0, one launch (start us, length us, event | category | flops | bytes accessed | tf_op | source)
XLA Modules:
  0.0 35.8 jit_solution(14206565005576054364)
XLA Ops:
  0.0 0.5 %collective-permute-start.3 = (bf16[512,3072]{1,0:T(8,128)(2,1)}, bf16[512,3072]{1,0:T(8,128)(2,1)S(1)}, u32[]{:S(2)}, u32[]{:S(2)}) collective-permute-start(bf16[512,3072]{1,0:T(8,128)(2,1)} %weight.1), channel_id=1, source_target_pairs={{0,1},{1,0},{2,3},{3,2},{4,5},{5,4},{6,7},{7,6},{8,9},{9,8},{10,11... | collective-permute-start | bytes 9437192 | tf_op jit(solution)/shard_map/ppermute | solution.py:271
  0.5 0.1 collective-permute-start.11
  0.5 1.6 %shard_map.82 = (bf16[808,128]{1,0:T(8,128)(2,1)S(1)}, bf16[96,1024]{1,0:T(8,128)(2,1)S(1)}, bf16[40,128]{1,0:T(8,128)(2,1)S(1)}) custom-call(bf16[192,1024]{1,0:T(8,128)(2,1)} %bitcast.4, s32[1,192]{1,0:T(1,128)} %refs_1_.1, s32[1,192]{1,0:T(1,128)} %refs_2_.1, s32[1,192]{1,0:T(1,128)} %bitcast.6, bf16[51,1024]{1,0:T(8,128)(2,1)} %bitcast.5, ...), custom_call_target="tpu_custom_call" | custom-call | flops 1048576 | bytes 1024 | tf_op jit(solution)/shard_map/pallas_call | solution.py:289
  2.2 4.1 %collective-permute-start.1 = (bf16[808,128]{1,0:T(8,128)(2,1)S(1)}, bf16[808,128]{1,0:T(8,128)(2,1)S(1)}, u32[]{:S(2)}, u32[]{:S(2)}) collective-permute-start(bf16[808,128]{1,0:T(8,128)(2,1)S(1)} %get-tuple-element.31.first), channel_id=1, source_target_pairs={{2,0},{6,2},{4,6},{0,4},{3,1},{7,3},{5,7},{1,5},{10,8},{14,10},{12... | collective-permute-start | bytes 620552 | tf_op jit(solution)/shard_map/ppermute | solution.py:311
  6.3 1.6 %collective-permute-start = (bf16[96,1024]{1,0:T(8,128)(2,1)S(1)}, bf16[96,1024]{1,0:T(8,128)(2,1)S(1)}, u32[]{:S(2)}, u32[]{:S(2)}) collective-permute-start(bf16[96,1024]{1,0:T(8,128)(2,1)S(1)} %get-tuple-element.30.second), channel_id=1, source_target_pairs={{2,0},{6,2},{4,6},{0,4},{3,1},{7,3},{5,7},{1,5},{10,8},{14,10},{12... | collective-permute-start | bytes 589832 | tf_op jit(solution)/shard_map/ppermute | solution.py:312
  7.8 0.0 collective-permute-start.2
  7.8 0.0 copy-start
  7.8 1.9 %copy-done = bf16[512,3072]{1,0:T(8,128)(2,1)S(1)} copy-done((bf16[512,3072]{1,0:T(8,128)(2,1)S(1)}, bf16[512,3072]{1,0:T(8,128)(2,1)}, u32[]{:S(2)}) %copy-start) | copy-done | bytes 3145752
  9.7 1.0 %shard_map.83.weight_here = bf16[512,3072]{1,0:T(8,128)(2,1)S(1)} custom-call(bf16[512,3072]{1,0:T(8,128)(2,1)S(1)} %copy-done), custom_call_target="tpu_custom_call" | custom-call | flops 1048576 | bytes 1024 | tf_op jit(solution)/shard_map/pallas_call | solution.py:23
  10.7 0.0 collective-permute-done.3.weight
  10.7 1.0 %shard_map.84.weight_there = bf16[512,3072]{1,0:T(8,128)(2,1)S(1)} custom-call(bf16[512,3072]{1,0:T(8,128)(2,1)S(1)} %collective-permute-done.3.weight), custom_call_target="tpu_custom_call" | custom-call | flops 1048576 | bytes 1024 | tf_op jit(solution)/shard_map/pallas_call | solution.py:23
  11.8 0.0 collective-permute-done.2.summary
  11.8 0.0 collective-permute-done.1.arrived
  11.8 3.4 %collective-permute-start.5 = (bf16[808,128]{1,0:T(8,128)(2,1)S(1)}, bf16[808,128]{1,0:T(8,128)(2,1)S(1)}, u32[]{:S(2)}, u32[]{:S(2)}) collective-permute-start(bf16[808,128]{1,0:T(8,128)(2,1)S(1)} %collective-permute-done.1.arrived), channel_id=1, source_target_pairs={{2,0},{6,2},{4,6},{0,4},{3,1},{7,3},{5,7},{1,5},{10,8},{14,10},{12... | collective-permute-start | bytes 620552 | tf_op jit(solution)/shard_map/ppermute | solution.py:311
  15.1 3.4 %shard_map.85 = (bf16[8,128,384]{2,1,0:T(8,128)(2,1)S(1)}, f32[8,384]{1,0:T(8,128)S(1)}, f32[8,384]{1,0:T(8,128)S(1)}, f32[8,64,384]{2,1,0:T(8,128)S(1)}) custom-call(bf16[808,128]{1,0:T(8,128)(2,1)S(1)} %get-tuple-element.31.first, bf16[96,1024]{1,0:T(8,128)(2,1)S(1)} %get-tuple-element.30.second, bf16[808,128]{1,0:T(8,128)(2,1)S(1)} %collective-permute-done.1.arrived, ...), custom_call_target="tpu_custom_call" | custom-call | flops 268435456 | bytes 1024 | tf_op jit(solution)/shard_map/pallas_call | solution.py:23
  18.6 0.0 collective-permute-done.second
  18.6 0.8 %collective-permute-start.4 = (bf16[96,1024]{1,0:T(8,128)(2,1)S(1)}, bf16[96,1024]{1,0:T(8,128)(2,1)S(1)}, u32[]{:S(2)}, u32[]{:S(2)}) collective-permute-start(bf16[96,1024]{1,0:T(8,128)(2,1)S(1)} %collective-permute-done.second), channel_id=1, source_target_pairs={{2,0},{6,2},{4,6},{0,4},{3,1},{7,3},{5,7},{1,5},{10,8},{14,10},{12... | collective-permute-start | bytes 589832 | tf_op jit(solution)/shard_map/ppermute | solution.py:312
  19.4 0.0 collective-permute-start.6
  19.4 1.4 %collective-permute-done.5.first = bf16[808,128]{1,0:T(8,128)(2,1)S(1)} collective-permute-done((bf16[808,128]{1,0:T(8,128)(2,1)S(1)}, bf16[808,128]{1,0:T(8,128)(2,1)S(1)}, u32[]{:S(2)}, u32[]{:S(2)}) %collective-permute-start.5) | collective-permute-done | bytes 206880 | tf_op jit(solution)/shard_map/ppermute | solution.py:311
  20.7 3.4 %collective-permute-start.8 = (bf16[808,128]{1,0:T(8,128)(2,1)S(1)}, bf16[808,128]{1,0:T(8,128)(2,1)S(1)}, u32[]{:S(2)}, u32[]{:S(2)}) collective-permute-start(bf16[808,128]{1,0:T(8,128)(2,1)S(1)} %collective-permute-done.5.first), channel_id=1, source_target_pairs={{2,0},{6,2},{4,6},{0,4},{3,1},{7,3},{5,7},{1,5},{10,8},{14,10},{12... | collective-permute-start | bytes 620552 | tf_op jit(solution)/shard_map/ppermute | solution.py:311
  24.1 0.0 collective-permute-done.6.summary
  24.1 2.0 %shard_map.86 = (f32[8,384]{1,0:T(8,128)S(1)}, f32[8,384]{1,0:T(8,128)S(1)}, f32[8,64,384]{2,1,0:T(8,128)S(1)}) custom-call(bf16[96,1024]{1,0:T(8,128)(2,1)S(1)} %collective-permute-done.second, bf16[808,128]{1,0:T(8,128)(2,1)S(1)} %collective-permute-done.5.first, bf16[40,128]{1,0:T(8,128)(2,1)S(1)} %collective-permute-done.6.summary, ...), custom_call_target="tpu_custom_call" | custom-call | flops 268435456 | bytes 1024 | tf_op jit(solution)/shard_map/pallas_call | solution.py:23
  26.1 0.0 collective-permute-done.4.second
  26.2 2.2 %collective-permute-start.7 = (bf16[96,1024]{1,0:T(8,128)(2,1)S(1)}, bf16[96,1024]{1,0:T(8,128)(2,1)S(1)}, u32[]{:S(2)}, u32[]{:S(2)}) collective-permute-start(bf16[96,1024]{1,0:T(8,128)(2,1)S(1)} %collective-permute-done.4.second), channel_id=1, source_target_pairs={{2,0},{6,2},{4,6},{0,4},{3,1},{7,3},{5,7},{1,5},{10,8},{14,10},{12... | collective-permute-start | bytes 589832 | tf_op jit(solution)/shard_map/ppermute | solution.py:312
  28.3 0.0 collective-permute-start.10
  28.3 2.3 %collective-permute-done.8.first = bf16[808,128]{1,0:T(8,128)(2,1)S(1)} collective-permute-done((bf16[808,128]{1,0:T(8,128)(2,1)S(1)}, bf16[808,128]{1,0:T(8,128)(2,1)S(1)}, u32[]{:S(2)}, u32[]{:S(2)}) %collective-permute-start.8) | collective-permute-done | bytes 206880 | tf_op jit(solution)/shard_map/ppermute | solution.py:311
  30.6 0.0 copy-start.1
  30.6 0.0 collective-permute-start.9
  30.6 0.0 collective-permute-done.10.summary
  30.6 2.0 %shard_map.87 = (f32[8,384]{1,0:T(8,128)S(1)}, f32[8,384]{1,0:T(8,128)S(1)}, f32[8,64,384]{2,1,0:T(8,128)S(1)}) custom-call(bf16[96,1024]{1,0:T(8,128)(2,1)S(1)} %collective-permute-done.4.second, bf16[808,128]{1,0:T(8,128)(2,1)S(1)} %collective-permute-done.8.first, bf16[40,128]{1,0:T(8,128)(2,1)S(1)} %collective-permute-done.10.summary, ...), custom_call_target="tpu_custom_call" | custom-call | flops 268435456 | bytes 1024 | tf_op jit(solution)/shard_map/pallas_call | solution.py:23
  32.7 0.0 collective-permute-done.11.out_there
  32.7 0.3 collective-permute-done.7.second
  33.0 0.0 collective-permute-done.9.summary
  33.0 0.0 copy-done.1
  33.0 2.9 %shard_map.88 = bf16[192,1024]{1,0:T(8,128)(2,1)} custom-call(bf16[96,1024]{1,0:T(8,128)(2,1)S(1)} %collective-permute-done.7.second, bf16[40,128]{1,0:T(8,128)(2,1)S(1)} %collective-permute-done.9.summary, bf16[512,3072]{1,0:T(8,128)(2,1)S(1)} %shard_map.83.weight_here, bf16[512,3072]{1,0:T(8,128)(2,1)S(1)} %shard_map.84.weight_there, ...), custom_call_target="tpu_custom_call" | custom-call | flops 1048576 | bytes 1024 | tf_op jit(solution)/shard_map/pallas_call | solution.py:328
  (3 shorter events, 0.0 us)
Async XLA Ops:
  0.0 10.7 %collective-permute-start.3 = (bf16[512,3072]{1,0:T(8,128)(2,1)}, bf16[512,3072]{1,0:T(8,128)(2,1)S(1)}, u32[]{:S(2)}, u32[]{:S(2)}) collective-permute-start(bf16[512,3072]{1,0:T(8,128)(2,1)} %weight.1), channel_id=1, source_target_pairs={{0,1},{1,0},{2,3},{3,2},{4,5},{5,4},{6,7},{7,6},{8,9},{9,8},{10,11... | collective-permute-start | bytes 9437192 | tf_op jit(solution)/shard_map/ppermute | solution.py:271
  0.5 32.2 %collective-permute-start.11 = (bf16[512,1024]{1,0:T(8,128)(2,1)}, bf16[512,1024]{1,0:T(8,128)(2,1)S(1)}, u32[]{:S(2)}, u32[]{:S(2)}) collective-permute-start(bf16[512,1024]{1,0:T(8,128)(2,1)} %out_here.1), channel_id=1, source_target_pairs={{0,1},{1,0},{2,3},{3,2},{4,5},{5,4},{6,7},{7,6},{8,9},{9,8},{10,11... | collective-permute-start | bytes 3145736 | tf_op jit(solution)/shard_map/ppermute | solution.py:271
  2.2 9.6 %collective-permute-start.1 = (bf16[808,128]{1,0:T(8,128)(2,1)S(1)}, bf16[808,128]{1,0:T(8,128)(2,1)S(1)}, u32[]{:S(2)}, u32[]{:S(2)}) collective-permute-start(bf16[808,128]{1,0:T(8,128)(2,1)S(1)} %get-tuple-element.31.first), channel_id=1, source_target_pairs={{2,0},{6,2},{4,6},{0,4},{3,1},{7,3},{5,7},{1,5},{10,8},{14,10},{12... | collective-permute-start | bytes 620552 | tf_op jit(solution)/shard_map/ppermute | solution.py:311
  6.3 12.3 %collective-permute-start = (bf16[96,1024]{1,0:T(8,128)(2,1)S(1)}, bf16[96,1024]{1,0:T(8,128)(2,1)S(1)}, u32[]{:S(2)}, u32[]{:S(2)}) collective-permute-start(bf16[96,1024]{1,0:T(8,128)(2,1)S(1)} %get-tuple-element.30.second), channel_id=1, source_target_pairs={{2,0},{6,2},{4,6},{0,4},{3,1},{7,3},{5,7},{1,5},{10,8},{14,10},{12... | collective-permute-start | bytes 589832 | tf_op jit(solution)/shard_map/ppermute | solution.py:312
  7.8 3.9 %collective-permute-start.2 = (bf16[40,128]{1,0:T(8,128)(2,1)S(1)}, bf16[40,128]{1,0:T(8,128)(2,1)S(1)}, u32[]{:S(2)}, u32[]{:S(2)}) collective-permute-start(bf16[40,128]{1,0:T(8,128)(2,1)S(1)} %get-tuple-element.32), channel_id=1, source_target_pairs={{0,1},{1,0},{2,3},{3,2},{4,5},{5,4},{6,7},{7,6},{8,9},{9,8},{10,11... | collective-permute-start | bytes 30728 | tf_op jit(solution)/shard_map/ppermute | solution.py:271
  7.8 1.9 %copy-start = (bf16[512,3072]{1,0:T(8,128)(2,1)S(1)}, bf16[512,3072]{1,0:T(8,128)(2,1)}, u32[]{:S(2)}) copy-start(bf16[512,3072]{1,0:T(8,128)(2,1)} %weight.1) | copy-start | bytes 9437188
  11.8 8.9 %collective-permute-start.5 = (bf16[808,128]{1,0:T(8,128)(2,1)S(1)}, bf16[808,128]{1,0:T(8,128)(2,1)S(1)}, u32[]{:S(2)}, u32[]{:S(2)}) collective-permute-start(bf16[808,128]{1,0:T(8,128)(2,1)S(1)} %collective-permute-done.1.arrived), channel_id=1, source_target_pairs={{2,0},{6,2},{4,6},{0,4},{3,1},{7,3},{5,7},{1,5},{10,8},{14,10},{12... | collective-permute-start | bytes 620552 | tf_op jit(solution)/shard_map/ppermute | solution.py:311
  18.6 7.6 %collective-permute-start.4 = (bf16[96,1024]{1,0:T(8,128)(2,1)S(1)}, bf16[96,1024]{1,0:T(8,128)(2,1)S(1)}, u32[]{:S(2)}, u32[]{:S(2)}) collective-permute-start(bf16[96,1024]{1,0:T(8,128)(2,1)S(1)} %collective-permute-done.second), channel_id=1, source_target_pairs={{2,0},{6,2},{4,6},{0,4},{3,1},{7,3},{5,7},{1,5},{10,8},{14,10},{12... | collective-permute-start | bytes 589832 | tf_op jit(solution)/shard_map/ppermute | solution.py:312
  19.4 4.7 %collective-permute-start.6 = (bf16[40,128]{1,0:T(8,128)(2,1)S(1)}, bf16[40,128]{1,0:T(8,128)(2,1)S(1)}, u32[]{:S(2)}, u32[]{:S(2)}) collective-permute-start(bf16[40,128]{1,0:T(8,128)(2,1)S(1)} %slice.9), channel_id=1, source_target_pairs={{0,1},{1,0},{2,3},{3,2},{4,5},{5,4},{6,7},{7,6},{8,9},{9,8},{10,11... | collective-permute-start | bytes 30728 | tf_op jit(solution)/shard_map/ppermute | solution.py:271
  20.7 9.9 %collective-permute-start.8 = (bf16[808,128]{1,0:T(8,128)(2,1)S(1)}, bf16[808,128]{1,0:T(8,128)(2,1)S(1)}, u32[]{:S(2)}, u32[]{:S(2)}) collective-permute-start(bf16[808,128]{1,0:T(8,128)(2,1)S(1)} %collective-permute-done.5.first), channel_id=1, source_target_pairs={{2,0},{6,2},{4,6},{0,4},{3,1},{7,3},{5,7},{1,5},{10,8},{14,10},{12... | collective-permute-start | bytes 620552 | tf_op jit(solution)/shard_map/ppermute | solution.py:311
  26.2 6.8 %collective-permute-start.7 = (bf16[96,1024]{1,0:T(8,128)(2,1)S(1)}, bf16[96,1024]{1,0:T(8,128)(2,1)S(1)}, u32[]{:S(2)}, u32[]{:S(2)}) collective-permute-start(bf16[96,1024]{1,0:T(8,128)(2,1)S(1)} %collective-permute-done.4.second), channel_id=1, source_target_pairs={{2,0},{6,2},{4,6},{0,4},{3,1},{7,3},{5,7},{1,5},{10,8},{14,10},{12... | collective-permute-start | bytes 589832 | tf_op jit(solution)/shard_map/ppermute | solution.py:312
  28.3 2.3 %collective-permute-start.10 = (bf16[40,128]{1,0:T(8,128)(2,1)S(1)}, bf16[40,128]{1,0:T(8,128)(2,1)S(1)}, u32[]{:S(2)}, u32[]{:S(2)}) collective-permute-start(bf16[40,128]{1,0:T(8,128)(2,1)S(1)} %slice.13), channel_id=1, source_target_pairs={{0,1},{1,0},{2,3},{3,2},{4,5},{5,4},{6,7},{7,6},{8,9},{9,8},{10,11... | collective-permute-start | bytes 30728 | tf_op jit(solution)/shard_map/ppermute | solution.py:271
  30.6 2.4 %copy-start.1 = (bf16[512,1024]{1,0:T(8,128)(2,1)S(1)}, bf16[512,1024]{1,0:T(8,128)(2,1)}, u32[]{:S(2)}) copy-start(bf16[512,1024]{1,0:T(8,128)(2,1)} %out_here.1) | copy-start | bytes 3145732
  30.6 2.4 %collective-permute-start.9 = (bf16[40,128]{1,0:T(8,128)(2,1)S(1)}, bf16[40,128]{1,0:T(8,128)(2,1)S(1)}, u32[]{:S(2)}, u32[]{:S(2)}) collective-permute-start(bf16[40,128]{1,0:T(8,128)(2,1)S(1)} %slice.12), channel_id=1, source_target_pairs={{0,1},{1,0},{2,3},{3,2},{4,5},{5,4},{6,7},{7,6},{8,9},{9,8},{10,11... | collective-permute-start | bytes 30728 | tf_op jit(solution)/shard_map/ppermute | solution.py:271

commit v7 on v6

--- a/solution.py
+++ b/solution.py
@@ -113,9 +113,7 @@
 def fold(rows, summary_bias, weight_here, weight_there, turned, old, new):
     width = H * HD
     count = rows.shape[0]
-    key_value = project(rows, weight_here, weight_there, width, 3 * width)
-    key = key_value[:, :width].astype(BF16)
-    value = jnp.transpose(key_value[:, width:]).astype(BF16)
+    key = project(rows, weight_here, weight_there, width, 2 * width).astype(BF16)
     low = lax.broadcasted_iota(jnp.int32, (HD, LANES), 1) < HD
     scores, folded = {}, {}
 
@@ -156,6 +154,8 @@
 
     score(0)
     score(1)
+    value = project(rows, weight_here, weight_there, 2 * width, 3 * width)
+    value = jnp.transpose(value).astype(BF16)
     for pair in range(PAIRS):
         if pair + 2 < PAIRS:
             score(pair + 2)

time: 36 us -> 35.9 us (level)
  no operation moved by 1% of the time
where the time goes in v7:
time: 35.9 us; the launch traced here: 35.8 us
  starting transfers between devices  15.9 us (44%)
  Pallas kernels  13.9 us (39%)
  waiting for transfers between devices  3.92 us (11%)
  local copies, waits for them, and re-layouts  1.9 us (5%)
    ppermute x3, starting transfers between devices, shards(): next_first = lax.ppermute(first, 'peak', pairs)  10.8 us
    pallas_call x5, Pallas kernels, call(): pl.pallas_call(kernel, out_shape=shapes, in_specs=[spec] * len(operands),...  9.47 us
    ppermute x3, starting transfers between devices, shards(): next_second = lax.ppermute(second, 'peak', pairs)  4.54 us
    ppermute x3, waiting for transfers between devices, shards(): next_first = lax.ppermute(first, 'peak', pairs)  3.57 us
    pallas_call x1, Pallas kernels, shards(): pl.pallas_call(last_kernel, out_shape=[jax.ShapeDtypeStruct((tokens, widt...  2.83 us
    unnamed x4, local copies, waits for them, and re-layouts  1.89 us
    pallas_call x1, Pallas kernels, shards(): pl.pallas_call(embed_kernel, out_shape=[jax.ShapeDtypeStruct((cut * width...  1.64 us
  transfers between devices with their start and end apart: 12, of which 3 were waited for; matrix products, arithmetic and copies ran while one was open for 0% of the time, Pallas kernels for 31%

profile of v7, /device:TPU:0, one launch (start us, length us, event | category | flops | bytes accessed | tf_op | source)
XLA Modules:
  0.0 35.8 jit_solution(2594462340531655154)
XLA Ops:
  0.0 0.5 %collective-permute-start.3 = (bf16[512,3072]{1,0:T(8,128)(2,1)}, bf16[512,3072]{1,0:T(8,128)(2,1)S(1)}, u32[]{:S(2)}, u32[]{:S(2)}) collective-permute-start(bf16[512,3072]{1,0:T(8,128)(2,1)} %weight.1), channel_id=1, source_target_pairs={{0,1},{1,0},{2,3},{3,2},{4,5},{5,4},{6,7},{7,6},{8,9},{9,8},{10,11... | collective-permute-start | bytes 9437192 | tf_op jit(solution)/shard_map/ppermute | solution.py:271
  0.5 0.1 collective-permute-start.11
  0.5 1.6 %shard_map.82 = (bf16[808,128]{1,0:T(8,128)(2,1)S(1)}, bf16[96,1024]{1,0:T(8,128)(2,1)S(1)}, bf16[40,128]{1,0:T(8,128)(2,1)S(1)}) custom-call(bf16[192,1024]{1,0:T(8,128)(2,1)} %bitcast.4, s32[1,192]{1,0:T(1,128)} %refs_1_.1, s32[1,192]{1,0:T(1,128)} %refs_2_.1, s32[1,192]{1,0:T(1,128)} %bitcast.6, bf16[51,1024]{1,0:T(8,128)(2,1)} %bitcast.5, ...), custom_call_target="tpu_custom_call" | custom-call | flops 1048576 | bytes 1024 | tf_op jit(solution)/shard_map/pallas_call | solution.py:289
  2.2 4.1 %collective-permute-start.1 = (bf16[808,128]{1,0:T(8,128)(2,1)S(1)}, bf16[808,128]{1,0:T(8,128)(2,1)S(1)}, u32[]{:S(2)}, u32[]{:S(2)}) collective-permute-start(bf16[808,128]{1,0:T(8,128)(2,1)S(1)} %get-tuple-element.31.first), channel_id=1, source_target_pairs={{2,0},{6,2},{4,6},{0,4},{3,1},{7,3},{5,7},{1,5},{10,8},{14,10},{12... | collective-permute-start | bytes 620552 | tf_op jit(solution)/shard_map/ppermute | solution.py:311
  6.3 1.6 %collective-permute-start = (bf16[96,1024]{1,0:T(8,128)(2,1)S(1)}, bf16[96,1024]{1,0:T(8,128)(2,1)S(1)}, u32[]{:S(2)}, u32[]{:S(2)}) collective-permute-start(bf16[96,1024]{1,0:T(8,128)(2,1)S(1)} %get-tuple-element.30.second), channel_id=1, source_target_pairs={{2,0},{6,2},{4,6},{0,4},{3,1},{7,3},{5,7},{1,5},{10,8},{14,10},{12... | collective-permute-start | bytes 589832 | tf_op jit(solution)/shard_map/ppermute | solution.py:312
  7.8 0.0 collective-permute-start.2
  7.8 0.0 copy-start
  7.8 1.9 %copy-done = bf16[512,3072]{1,0:T(8,128)(2,1)S(1)} copy-done((bf16[512,3072]{1,0:T(8,128)(2,1)S(1)}, bf16[512,3072]{1,0:T(8,128)(2,1)}, u32[]{:S(2)}) %copy-start) | copy-done | bytes 3145752
  9.7 1.0 %shard_map.83.weight_here = bf16[512,3072]{1,0:T(8,128)(2,1)S(1)} custom-call(bf16[512,3072]{1,0:T(8,128)(2,1)S(1)} %copy-done), custom_call_target="tpu_custom_call" | custom-call | flops 1048576 | bytes 1024 | tf_op jit(solution)/shard_map/pallas_call | solution.py:23
  10.7 0.0 collective-permute-done.3.weight
  10.7 1.0 %shard_map.84.weight_there = bf16[512,3072]{1,0:T(8,128)(2,1)S(1)} custom-call(bf16[512,3072]{1,0:T(8,128)(2,1)S(1)} %collective-permute-done.3.weight), custom_call_target="tpu_custom_call" | custom-call | flops 1048576 | bytes 1024 | tf_op jit(solution)/shard_map/pallas_call | solution.py:23
  11.8 0.0 collective-permute-done.2.summary
  11.8 0.0 collective-permute-done.1.arrived
  11.8 3.4 %collective-permute-start.5 = (bf16[808,128]{1,0:T(8,128)(2,1)S(1)}, bf16[808,128]{1,0:T(8,128)(2,1)S(1)}, u32[]{:S(2)}, u32[]{:S(2)}) collective-permute-start(bf16[808,128]{1,0:T(8,128)(2,1)S(1)} %collective-permute-done.1.arrived), channel_id=1, source_target_pairs={{2,0},{6,2},{4,6},{0,4},{3,1},{7,3},{5,7},{1,5},{10,8},{14,10},{12... | collective-permute-start | bytes 620552 | tf_op jit(solution)/shard_map/ppermute | solution.py:311
  15.1 3.4 %shard_map.85 = (bf16[8,128,384]{2,1,0:T(8,128)(2,1)S(1)}, f32[8,384]{1,0:T(8,128)S(1)}, f32[8,384]{1,0:T(8,128)S(1)}, f32[8,64,384]{2,1,0:T(8,128)S(1)}) custom-call(bf16[808,128]{1,0:T(8,128)(2,1)S(1)} %get-tuple-element.31.first, bf16[96,1024]{1,0:T(8,128)(2,1)S(1)} %get-tuple-element.30.second, bf16[808,128]{1,0:T(8,128)(2,1)S(1)} %collective-permute-done.1.arrived, ...), custom_call_target="tpu_custom_call" | custom-call | flops 268435456 | bytes 1024 | tf_op jit(solution)/shard_map/pallas_call | solution.py:23
  18.5 0.0 collective-permute-done.second
  18.6 0.8 %collective-permute-start.4 = (bf16[96,1024]{1,0:T(8,128)(2,1)S(1)}, bf16[96,1024]{1,0:T(8,128)(2,1)S(1)}, u32[]{:S(2)}, u32[]{:S(2)}) collective-permute-start(bf16[96,1024]{1,0:T(8,128)(2,1)S(1)} %collective-permute-done.second), channel_id=1, source_target_pairs={{2,0},{6,2},{4,6},{0,4},{3,1},{7,3},{5,7},{1,5},{10,8},{14,10},{12... | collective-permute-start | bytes 589832 | tf_op jit(solution)/shard_map/ppermute | solution.py:312
  19.4 0.0 collective-permute-start.6
  19.4 1.4 %collective-permute-done.5.first = bf16[808,128]{1,0:T(8,128)(2,1)S(1)} collective-permute-done((bf16[808,128]{1,0:T(8,128)(2,1)S(1)}, bf16[808,128]{1,0:T(8,128)(2,1)S(1)}, u32[]{:S(2)}, u32[]{:S(2)}) %collective-permute-start.5) | collective-permute-done | bytes 206880 | tf_op jit(solution)/shard_map/ppermute | solution.py:311
  20.7 3.4 %collective-permute-start.8 = (bf16[808,128]{1,0:T(8,128)(2,1)S(1)}, bf16[808,128]{1,0:T(8,128)(2,1)S(1)}, u32[]{:S(2)}, u32[]{:S(2)}) collective-permute-start(bf16[808,128]{1,0:T(8,128)(2,1)S(1)} %collective-permute-done.5.first), channel_id=1, source_target_pairs={{2,0},{6,2},{4,6},{0,4},{3,1},{7,3},{5,7},{1,5},{10,8},{14,10},{12... | collective-permute-start | bytes 620552 | tf_op jit(solution)/shard_map/ppermute | solution.py:311
  24.1 0.0 collective-permute-done.6.summary
  24.1 2.0 %shard_map.86 = (f32[8,384]{1,0:T(8,128)S(1)}, f32[8,384]{1,0:T(8,128)S(1)}, f32[8,64,384]{2,1,0:T(8,128)S(1)}) custom-call(bf16[96,1024]{1,0:T(8,128)(2,1)S(1)} %collective-permute-done.second, bf16[808,128]{1,0:T(8,128)(2,1)S(1)} %collective-permute-done.5.first, bf16[40,128]{1,0:T(8,128)(2,1)S(1)} %collective-permute-done.6.summary, ...), custom_call_target="tpu_custom_call" | custom-call | flops 268435456 | bytes 1024 | tf_op jit(solution)/shard_map/pallas_call | solution.py:23
  26.1 0.0 collective-permute-done.4.second
  26.1 2.2 %collective-permute-start.7 = (bf16[96,1024]{1,0:T(8,128)(2,1)S(1)}, bf16[96,1024]{1,0:T(8,128)(2,1)S(1)}, u32[]{:S(2)}, u32[]{:S(2)}) collective-permute-start(bf16[96,1024]{1,0:T(8,128)(2,1)S(1)} %collective-permute-done.4.second), channel_id=1, source_target_pairs={{2,0},{6,2},{4,6},{0,4},{3,1},{7,3},{5,7},{1,5},{10,8},{14,10},{12... | collective-permute-start | bytes 589832 | tf_op jit(solution)/shard_map/ppermute | solution.py:312
  28.3 0.0 collective-permute-start.10
  28.3 2.2 %collective-permute-done.8.first = bf16[808,128]{1,0:T(8,128)(2,1)S(1)} collective-permute-done((bf16[808,128]{1,0:T(8,128)(2,1)S(1)}, bf16[808,128]{1,0:T(8,128)(2,1)S(1)}, u32[]{:S(2)}, u32[]{:S(2)}) %collective-permute-start.8) | collective-permute-done | bytes 206880 | tf_op jit(solution)/shard_map/ppermute | solution.py:311
  30.5 0.0 copy-start.1
  30.5 0.0 collective-permute-start.9
  30.5 0.0 collective-permute-done.10.summary
  30.6 2.0 %shard_map.87 = (f32[8,384]{1,0:T(8,128)S(1)}, f32[8,384]{1,0:T(8,128)S(1)}, f32[8,64,384]{2,1,0:T(8,128)S(1)}) custom-call(bf16[96,1024]{1,0:T(8,128)(2,1)S(1)} %collective-permute-done.4.second, bf16[808,128]{1,0:T(8,128)(2,1)S(1)} %collective-permute-done.8.first, bf16[40,128]{1,0:T(8,128)(2,1)S(1)} %collective-permute-done.10.summary, ...), custom_call_target="tpu_custom_call" | custom-call | flops 268435456 | bytes 1024 | tf_op jit(solution)/shard_map/pallas_call | solution.py:23
  32.6 0.0 collective-permute-done.11.out_there
  32.6 0.3 collective-permute-done.7.second
  32.9 0.0 collective-permute-done.9.summary
  32.9 0.0 copy-done.1
  32.9 2.8 %shard_map.88 = bf16[192,1024]{1,0:T(8,128)(2,1)} custom-call(bf16[96,1024]{1,0:T(8,128)(2,1)S(1)} %collective-permute-done.7.second, bf16[40,128]{1,0:T(8,128)(2,1)S(1)} %collective-permute-done.9.summary, bf16[512,3072]{1,0:T(8,128)(2,1)S(1)} %shard_map.83.weight_here, bf16[512,3072]{1,0:T(8,128)(2,1)S(1)} %shard_map.84.weight_there, ...), custom_call_target="tpu_custom_call" | custom-call | flops 1048576 | bytes 1024 | tf_op jit(solution)/shard_map/pallas_call | solution.py:328
  (3 shorter events, 0.0 us)
Async XLA Ops:
  0.0 10.7 %collective-permute-start.3 = (bf16[512,3072]{1,0:T(8,128)(2,1)}, bf16[512,3072]{1,0:T(8,128)(2,1)S(1)}, u32[]{:S(2)}, u32[]{:S(2)}) collective-permute-start(bf16[512,3072]{1,0:T(8,128)(2,1)} %weight.1), channel_id=1, source_target_pairs={{0,1},{1,0},{2,3},{3,2},{4,5},{5,4},{6,7},{7,6},{8,9},{9,8},{10,11... | collective-permute-start | bytes 9437192 | tf_op jit(solution)/shard_map/ppermute | solution.py:271
  0.5 32.1 %collective-permute-start.11 = (bf16[512,1024]{1,0:T(8,128)(2,1)}, bf16[512,1024]{1,0:T(8,128)(2,1)S(1)}, u32[]{:S(2)}, u32[]{:S(2)}) collective-permute-start(bf16[512,1024]{1,0:T(8,128)(2,1)} %out_here.1), channel_id=1, source_target_pairs={{0,1},{1,0},{2,3},{3,2},{4,5},{5,4},{6,7},{7,6},{8,9},{9,8},{10,11... | collective-permute-start | bytes 3145736 | tf_op jit(solution)/shard_map/ppermute | solution.py:271
  2.2 9.6 %collective-permute-start.1 = (bf16[808,128]{1,0:T(8,128)(2,1)S(1)}, bf16[808,128]{1,0:T(8,128)(2,1)S(1)}, u32[]{:S(2)}, u32[]{:S(2)}) collective-permute-start(bf16[808,128]{1,0:T(8,128)(2,1)S(1)} %get-tuple-element.31.first), channel_id=1, source_target_pairs={{2,0},{6,2},{4,6},{0,4},{3,1},{7,3},{5,7},{1,5},{10,8},{14,10},{12... | collective-permute-start | bytes 620552 | tf_op jit(solution)/shard_map/ppermute | solution.py:311
  6.3 12.3 %collective-permute-start = (bf16[96,1024]{1,0:T(8,128)(2,1)S(1)}, bf16[96,1024]{1,0:T(8,128)(2,1)S(1)}, u32[]{:S(2)}, u32[]{:S(2)}) collective-permute-start(bf16[96,1024]{1,0:T(8,128)(2,1)S(1)} %get-tuple-element.30.second), channel_id=1, source_target_pairs={{2,0},{6,2},{4,6},{0,4},{3,1},{7,3},{5,7},{1,5},{10,8},{14,10},{12... | collective-permute-start | bytes 589832 | tf_op jit(solution)/shard_map/ppermute | solution.py:312
  7.8 3.9 %collective-permute-start.2 = (bf16[40,128]{1,0:T(8,128)(2,1)S(1)}, bf16[40,128]{1,0:T(8,128)(2,1)S(1)}, u32[]{:S(2)}, u32[]{:S(2)}) collective-permute-start(bf16[40,128]{1,0:T(8,128)(2,1)S(1)} %get-tuple-element.32), channel_id=1, source_target_pairs={{0,1},{1,0},{2,3},{3,2},{4,5},{5,4},{6,7},{7,6},{8,9},{9,8},{10,11... | collective-permute-start | bytes 30728 | tf_op jit(solution)/shard_map/ppermute | solution.py:271
  7.8 1.9 %copy-start = (bf16[512,3072]{1,0:T(8,128)(2,1)S(1)}, bf16[512,3072]{1,0:T(8,128)(2,1)}, u32[]{:S(2)}) copy-start(bf16[512,3072]{1,0:T(8,128)(2,1)} %weight.1) | copy-start | bytes 9437188
  11.8 8.9 %collective-permute-start.5 = (bf16[808,128]{1,0:T(8,128)(2,1)S(1)}, bf16[808,128]{1,0:T(8,128)(2,1)S(1)}, u32[]{:S(2)}, u32[]{:S(2)}) collective-permute-start(bf16[808,128]{1,0:T(8,128)(2,1)S(1)} %collective-permute-done.1.arrived), channel_id=1, source_target_pairs={{2,0},{6,2},{4,6},{0,4},{3,1},{7,3},{5,7},{1,5},{10,8},{14,10},{12... | collective-permute-start | bytes 620552 | tf_op jit(solution)/shard_map/ppermute | solution.py:311
  18.6 7.6 %collective-permute-start.4 = (bf16[96,1024]{1,0:T(8,128)(2,1)S(1)}, bf16[96,1024]{1,0:T(8,128)(2,1)S(1)}, u32[]{:S(2)}, u32[]{:S(2)}) collective-permute-start(bf16[96,1024]{1,0:T(8,128)(2,1)S(1)} %collective-permute-done.second), channel_id=1, source_target_pairs={{2,0},{6,2},{4,6},{0,4},{3,1},{7,3},{5,7},{1,5},{10,8},{14,10},{12... | collective-permute-start | bytes 589832 | tf_op jit(solution)/shard_map/ppermute | solution.py:312
  19.4 4.7 %collective-permute-start.6 = (bf16[40,128]{1,0:T(8,128)(2,1)S(1)}, bf16[40,128]{1,0:T(8,128)(2,1)S(1)}, u32[]{:S(2)}, u32[]{:S(2)}) collective-permute-start(bf16[40,128]{1,0:T(8,128)(2,1)S(1)} %slice.9), channel_id=1, source_target_pairs={{0,1},{1,0},{2,3},{3,2},{4,5},{5,4},{6,7},{7,6},{8,9},{9,8},{10,11... | collective-permute-start | bytes 30728 | tf_op jit(solution)/shard_map/ppermute | solution.py:271
  20.7 9.8 %collective-permute-start.8 = (bf16[808,128]{1,0:T(8,128)(2,1)S(1)}, bf16[808,128]{1,0:T(8,128)(2,1)S(1)}, u32[]{:S(2)}, u32[]{:S(2)}) collective-permute-start(bf16[808,128]{1,0:T(8,128)(2,1)S(1)} %collective-permute-done.5.first), channel_id=1, source_target_pairs={{2,0},{6,2},{4,6},{0,4},{3,1},{7,3},{5,7},{1,5},{10,8},{14,10},{12... | collective-permute-start | bytes 620552 | tf_op jit(solution)/shard_map/ppermute | solution.py:311
  26.1 6.8 %collective-permute-start.7 = (bf16[96,1024]{1,0:T(8,128)(2,1)S(1)}, bf16[96,1024]{1,0:T(8,128)(2,1)S(1)}, u32[]{:S(2)}, u32[]{:S(2)}) collective-permute-start(bf16[96,1024]{1,0:T(8,128)(2,1)S(1)} %collective-permute-done.4.second), channel_id=1, source_target_pairs={{2,0},{6,2},{4,6},{0,4},{3,1},{7,3},{5,7},{1,5},{10,8},{14,10},{12... | collective-permute-start | bytes 589832 | tf_op jit(solution)/shard_map/ppermute | solution.py:312
  28.3 2.2 %collective-permute-start.10 = (bf16[40,128]{1,0:T(8,128)(2,1)S(1)}, bf16[40,128]{1,0:T(8,128)(2,1)S(1)}, u32[]{:S(2)}, u32[]{:S(2)}) collective-permute-start(bf16[40,128]{1,0:T(8,128)(2,1)S(1)} %slice.13), channel_id=1, source_target_pairs={{0,1},{1,0},{2,3},{3,2},{4,5},{5,4},{6,7},{7,6},{8,9},{9,8},{10,11... | collective-permute-start | bytes 30728 | tf_op jit(solution)/shard_map/ppermute | solution.py:271
  30.5 2.4 %copy-start.1 = (bf16[512,1024]{1,0:T(8,128)(2,1)S(1)}, bf16[512,1024]{1,0:T(8,128)(2,1)}, u32[]{:S(2)}) copy-start(bf16[512,1024]{1,0:T(8,128)(2,1)} %out_here.1) | copy-start | bytes 3145732
  30.5 2.4 %collective-permute-start.9 = (bf16[40,128]{1,0:T(8,128)(2,1)S(1)}, bf16[40,128]{1,0:T(8,128)(2,1)S(1)}, u32[]{:S(2)}, u32[]{:S(2)}) collective-permute-start(bf16[40,128]{1,0:T(8,128)(2,1)S(1)} %slice.12), channel_id=1, source_target_pairs={{0,1},{1,0},{2,3},{3,2},{4,5},{5,4},{6,7},{7,6},{8,9},{9,8},{10,11... | collective-permute-start | bytes 30728 | tf_op jit(solution)/shard_map/ppermute | solution.py:271

commit v8 on v7

--- a/solution.py
+++ b/solution.py
@@ -154,11 +154,12 @@
 
     score(0)
     score(1)
+    score(2)
     value = project(rows, weight_here, weight_there, 2 * width, 3 * width)
     value = jnp.transpose(value).astype(BF16)
     for pair in range(PAIRS):
-        if pair + 2 < PAIRS:
-            score(pair + 2)
+        if pair + 3 < PAIRS:
+            score(pair + 3)
         weigh(pair)
         if pair >= 1:
             attend(pair - 1)

time: 35.9 us -> 35.9 us (level)
  no operation moved by 1% of the time
where the time goes in v8:
time: 35.9 us; the launch traced here: 35.8 us
  starting transfers between devices  15.9 us (44%)
  Pallas kernels  13.9 us (39%)
  waiting for transfers between devices  4 us (11%)
  local copies, waits for them, and re-layouts  1.9 us (5%)
    ppermute x3, starting transfers between devices, shards(): next_first = lax.ppermute(first, 'peak', pairs)  10.8 us
    pallas_call x5, Pallas kernels, call(): pl.pallas_call(kernel, out_shape=shapes, in_specs=[spec] * len(operands),...  9.44 us
    ppermute x3, starting transfers between devices, shards(): next_second = lax.ppermute(second, 'peak', pairs)  4.51 us
    ppermute x3, waiting for transfers between devices, shards(): next_first = lax.ppermute(first, 'peak', pairs)  3.62 us
    pallas_call x1, Pallas kernels, shards(): pl.pallas_call(last_kernel, out_shape=[jax.ShapeDtypeStruct((tokens, widt...  2.82 us
    unnamed x4, local copies, waits for them, and re-layouts  1.89 us
    pallas_call x1, Pallas kernels, shards(): pl.pallas_call(embed_kernel, out_shape=[jax.ShapeDtypeStruct((cut * width...  1.64 us
  transfers between devices with their start and end apart: 12, of which 3 were waited for; matrix products, arithmetic and copies ran while one was open for 0% of the time, Pallas kernels for 31%

profile of v8, /device:TPU:0, one launch (start us, length us, event | category | flops | bytes accessed | tf_op | source)
XLA Modules:
  0.0 35.8 jit_solution(6930708262229966938)
XLA Ops:
  0.0 0.5 %collective-permute-start.3 = (bf16[512,3072]{1,0:T(8,128)(2,1)}, bf16[512,3072]{1,0:T(8,128)(2,1)S(1)}, u32[]{:S(2)}, u32[]{:S(2)}) collective-permute-start(bf16[512,3072]{1,0:T(8,128)(2,1)} %weight.1), channel_id=1, source_target_pairs={{0,1},{1,0},{2,3},{3,2},{4,5},{5,4},{6,7},{7,6},{8,9},{9,8},{10,11... | collective-permute-start | bytes 9437192 | tf_op jit(solution)/shard_map/ppermute | solution.py:272
  0.5 0.1 collective-permute-start.11
  0.5 1.6 %shard_map.82 = (bf16[808,128]{1,0:T(8,128)(2,1)S(1)}, bf16[96,1024]{1,0:T(8,128)(2,1)S(1)}, bf16[40,128]{1,0:T(8,128)(2,1)S(1)}) custom-call(bf16[192,1024]{1,0:T(8,128)(2,1)} %bitcast.4, s32[1,192]{1,0:T(1,128)} %refs_1_.1, s32[1,192]{1,0:T(1,128)} %refs_2_.1, s32[1,192]{1,0:T(1,128)} %bitcast.6, bf16[51,1024]{1,0:T(8,128)(2,1)} %bitcast.5, ...), custom_call_target="tpu_custom_call" | custom-call | flops 1048576 | bytes 1024 | tf_op jit(solution)/shard_map/pallas_call | solution.py:290
  2.2 4.1 %collective-permute-start.1 = (bf16[808,128]{1,0:T(8,128)(2,1)S(1)}, bf16[808,128]{1,0:T(8,128)(2,1)S(1)}, u32[]{:S(2)}, u32[]{:S(2)}) collective-permute-start(bf16[808,128]{1,0:T(8,128)(2,1)S(1)} %get-tuple-element.31.first), channel_id=1, source_target_pairs={{2,0},{6,2},{4,6},{0,4},{3,1},{7,3},{5,7},{1,5},{10,8},{14,10},{12... | collective-permute-start | bytes 620552 | tf_op jit(solution)/shard_map/ppermute | solution.py:312
  6.3 1.6 %collective-permute-start = (bf16[96,1024]{1,0:T(8,128)(2,1)S(1)}, bf16[96,1024]{1,0:T(8,128)(2,1)S(1)}, u32[]{:S(2)}, u32[]{:S(2)}) collective-permute-start(bf16[96,1024]{1,0:T(8,128)(2,1)S(1)} %get-tuple-element.30.second), channel_id=1, source_target_pairs={{2,0},{6,2},{4,6},{0,4},{3,1},{7,3},{5,7},{1,5},{10,8},{14,10},{12... | collective-permute-start | bytes 589832 | tf_op jit(solution)/shard_map/ppermute | solution.py:313
  7.8 0.0 collective-permute-start.2
  7.8 0.0 copy-start
  7.8 1.9 %copy-done = bf16[512,3072]{1,0:T(8,128)(2,1)S(1)} copy-done((bf16[512,3072]{1,0:T(8,128)(2,1)S(1)}, bf16[512,3072]{1,0:T(8,128)(2,1)}, u32[]{:S(2)}) %copy-start) | copy-done | bytes 3145752
  9.7 1.0 %shard_map.83.weight_here = bf16[512,3072]{1,0:T(8,128)(2,1)S(1)} custom-call(bf16[512,3072]{1,0:T(8,128)(2,1)S(1)} %copy-done), custom_call_target="tpu_custom_call" | custom-call | flops 1048576 | bytes 1024 | tf_op jit(solution)/shard_map/pallas_call | solution.py:23
  10.7 0.0 collective-permute-done.3.weight
  10.7 1.0 %shard_map.84.weight_there = bf16[512,3072]{1,0:T(8,128)(2,1)S(1)} custom-call(bf16[512,3072]{1,0:T(8,128)(2,1)S(1)} %collective-permute-done.3.weight), custom_call_target="tpu_custom_call" | custom-call | flops 1048576 | bytes 1024 | tf_op jit(solution)/shard_map/pallas_call | solution.py:23
  11.8 0.0 collective-permute-done.2.summary
  11.8 0.0 collective-permute-done.1.arrived
  11.8 3.4 %collective-permute-start.5 = (bf16[808,128]{1,0:T(8,128)(2,1)S(1)}, bf16[808,128]{1,0:T(8,128)(2,1)S(1)}, u32[]{:S(2)}, u32[]{:S(2)}) collective-permute-start(bf16[808,128]{1,0:T(8,128)(2,1)S(1)} %collective-permute-done.1.arrived), channel_id=1, source_target_pairs={{2,0},{6,2},{4,6},{0,4},{3,1},{7,3},{5,7},{1,5},{10,8},{14,10},{12... | collective-permute-start | bytes 620552 | tf_op jit(solution)/shard_map/ppermute | solution.py:312
  15.1 3.4 %shard_map.85 = (bf16[8,128,384]{2,1,0:T(8,128)(2,1)S(1)}, f32[8,384]{1,0:T(8,128)S(1)}, f32[8,384]{1,0:T(8,128)S(1)}, f32[8,64,384]{2,1,0:T(8,128)S(1)}) custom-call(bf16[808,128]{1,0:T(8,128)(2,1)S(1)} %get-tuple-element.31.first, bf16[96,1024]{1,0:T(8,128)(2,1)S(1)} %get-tuple-element.30.second, bf16[808,128]{1,0:T(8,128)(2,1)S(1)} %collective-permute-done.1.arrived, ...), custom_call_target="tpu_custom_call" | custom-call | flops 268435456 | bytes 1024 | tf_op jit(solution)/shard_map/pallas_call | solution.py:23
  18.6 0.0 collective-permute-done.second
  18.6 0.8 %collective-permute-start.4 = (bf16[96,1024]{1,0:T(8,128)(2,1)S(1)}, bf16[96,1024]{1,0:T(8,128)(2,1)S(1)}, u32[]{:S(2)}, u32[]{:S(2)}) collective-permute-start(bf16[96,1024]{1,0:T(8,128)(2,1)S(1)} %collective-permute-done.second), channel_id=1, source_target_pairs={{2,0},{6,2},{4,6},{0,4},{3,1},{7,3},{5,7},{1,5},{10,8},{14,10},{12... | collective-permute-start | bytes 589832 | tf_op jit(solution)/shard_map/ppermute | solution.py:313
  19.4 0.0 collective-permute-start.6
  19.4 1.4 %collective-permute-done.5.first = bf16[808,128]{1,0:T(8,128)(2,1)S(1)} collective-permute-done((bf16[808,128]{1,0:T(8,128)(2,1)S(1)}, bf16[808,128]{1,0:T(8,128)(2,1)S(1)}, u32[]{:S(2)}, u32[]{:S(2)}) %collective-permute-start.5) | collective-permute-done | bytes 206880 | tf_op jit(solution)/shard_map/ppermute | solution.py:312
  20.7 3.4 %collective-permute-start.8 = (bf16[808,128]{1,0:T(8,128)(2,1)S(1)}, bf16[808,128]{1,0:T(8,128)(2,1)S(1)}, u32[]{:S(2)}, u32[]{:S(2)}) collective-permute-start(bf16[808,128]{1,0:T(8,128)(2,1)S(1)} %collective-permute-done.5.first), channel_id=1, source_target_pairs={{2,0},{6,2},{4,6},{0,4},{3,1},{7,3},{5,7},{1,5},{10,8},{14,10},{12... | collective-permute-start | bytes 620552 | tf_op jit(solution)/shard_map/ppermute | solution.py:312
  24.1 0.0 collective-permute-done.6.summary
  24.1 2.0 %shard_map.86 = (f32[8,384]{1,0:T(8,128)S(1)}, f32[8,384]{1,0:T(8,128)S(1)}, f32[8,64,384]{2,1,0:T(8,128)S(1)}) custom-call(bf16[96,1024]{1,0:T(8,128)(2,1)S(1)} %collective-permute-done.second, bf16[808,128]{1,0:T(8,128)(2,1)S(1)} %collective-permute-done.5.first, bf16[40,128]{1,0:T(8,128)(2,1)S(1)} %collective-permute-done.6.summary, ...), custom_call_target="tpu_custom_call" | custom-call | flops 268435456 | bytes 1024 | tf_op jit(solution)/shard_map/pallas_call | solution.py:23
  26.1 0.0 collective-permute-done.4.second
  26.1 2.2 %collective-permute-start.7 = (bf16[96,1024]{1,0:T(8,128)(2,1)S(1)}, bf16[96,1024]{1,0:T(8,128)(2,1)S(1)}, u32[]{:S(2)}, u32[]{:S(2)}) collective-permute-start(bf16[96,1024]{1,0:T(8,128)(2,1)S(1)} %collective-permute-done.4.second), channel_id=1, source_target_pairs={{2,0},{6,2},{4,6},{0,4},{3,1},{7,3},{5,7},{1,5},{10,8},{14,10},{12... | collective-permute-start | bytes 589832 | tf_op jit(solution)/shard_map/ppermute | solution.py:313
  28.3 0.0 collective-permute-start.10
  28.3 2.3 %collective-permute-done.8.first = bf16[808,128]{1,0:T(8,128)(2,1)S(1)} collective-permute-done((bf16[808,128]{1,0:T(8,128)(2,1)S(1)}, bf16[808,128]{1,0:T(8,128)(2,1)S(1)}, u32[]{:S(2)}, u32[]{:S(2)}) %collective-permute-start.8) | collective-permute-done | bytes 206880 | tf_op jit(solution)/shard_map/ppermute | solution.py:312
  30.6 0.0 copy-start.1
  30.6 0.0 collective-permute-start.9
  30.6 0.0 collective-permute-done.10.summary
  30.6 2.0 %shard_map.87 = (f32[8,384]{1,0:T(8,128)S(1)}, f32[8,384]{1,0:T(8,128)S(1)}, f32[8,64,384]{2,1,0:T(8,128)S(1)}) custom-call(bf16[96,1024]{1,0:T(8,128)(2,1)S(1)} %collective-permute-done.4.second, bf16[808,128]{1,0:T(8,128)(2,1)S(1)} %collective-permute-done.8.first, bf16[40,128]{1,0:T(8,128)(2,1)S(1)} %collective-permute-done.10.summary, ...), custom_call_target="tpu_custom_call" | custom-call | flops 268435456 | bytes 1024 | tf_op jit(solution)/shard_map/pallas_call | solution.py:23
  32.6 0.0 collective-permute-done.11.out_there
  32.6 0.3 collective-permute-done.7.second
  33.0 0.0 collective-permute-done.9.summary
  33.0 0.0 copy-done.1
  33.0 2.8 %shard_map.88 = bf16[192,1024]{1,0:T(8,128)(2,1)} custom-call(bf16[96,1024]{1,0:T(8,128)(2,1)S(1)} %collective-permute-done.7.second, bf16[40,128]{1,0:T(8,128)(2,1)S(1)} %collective-permute-done.9.summary, bf16[512,3072]{1,0:T(8,128)(2,1)S(1)} %shard_map.83.weight_here, bf16[512,3072]{1,0:T(8,128)(2,1)S(1)} %shard_map.84.weight_there, ...), custom_call_target="tpu_custom_call" | custom-call | flops 1048576 | bytes 1024 | tf_op jit(solution)/shard_map/pallas_call | solution.py:329
  (3 shorter events, 0.0 us)
Async XLA Ops:
  0.0 10.7 %collective-permute-start.3 = (bf16[512,3072]{1,0:T(8,128)(2,1)}, bf16[512,3072]{1,0:T(8,128)(2,1)S(1)}, u32[]{:S(2)}, u32[]{:S(2)}) collective-permute-start(bf16[512,3072]{1,0:T(8,128)(2,1)} %weight.1), channel_id=1, source_target_pairs={{0,1},{1,0},{2,3},{3,2},{4,5},{5,4},{6,7},{7,6},{8,9},{9,8},{10,11... | collective-permute-start | bytes 9437192 | tf_op jit(solution)/shard_map/ppermute | solution.py:272
  0.5 32.2 %collective-permute-start.11 = (bf16[512,1024]{1,0:T(8,128)(2,1)}, bf16[512,1024]{1,0:T(8,128)(2,1)S(1)}, u32[]{:S(2)}, u32[]{:S(2)}) collective-permute-start(bf16[512,1024]{1,0:T(8,128)(2,1)} %out_here.1), channel_id=1, source_target_pairs={{0,1},{1,0},{2,3},{3,2},{4,5},{5,4},{6,7},{7,6},{8,9},{9,8},{10,11... | collective-permute-start | bytes 3145736 | tf_op jit(solution)/shard_map/ppermute | solution.py:272
  2.2 9.6 %collective-permute-start.1 = (bf16[808,128]{1,0:T(8,128)(2,1)S(1)}, bf16[808,128]{1,0:T(8,128)(2,1)S(1)}, u32[]{:S(2)}, u32[]{:S(2)}) collective-permute-start(bf16[808,128]{1,0:T(8,128)(2,1)S(1)} %get-tuple-element.31.first), channel_id=1, source_target_pairs={{2,0},{6,2},{4,6},{0,4},{3,1},{7,3},{5,7},{1,5},{10,8},{14,10},{12... | collective-permute-start | bytes 620552 | tf_op jit(solution)/shard_map/ppermute | solution.py:312
  6.3 12.3 %collective-permute-start = (bf16[96,1024]{1,0:T(8,128)(2,1)S(1)}, bf16[96,1024]{1,0:T(8,128)(2,1)S(1)}, u32[]{:S(2)}, u32[]{:S(2)}) collective-permute-start(bf16[96,1024]{1,0:T(8,128)(2,1)S(1)} %get-tuple-element.30.second), channel_id=1, source_target_pairs={{2,0},{6,2},{4,6},{0,4},{3,1},{7,3},{5,7},{1,5},{10,8},{14,10},{12... | collective-permute-start | bytes 589832 | tf_op jit(solution)/shard_map/ppermute | solution.py:313
  7.8 3.9 %collective-permute-start.2 = (bf16[40,128]{1,0:T(8,128)(2,1)S(1)}, bf16[40,128]{1,0:T(8,128)(2,1)S(1)}, u32[]{:S(2)}, u32[]{:S(2)}) collective-permute-start(bf16[40,128]{1,0:T(8,128)(2,1)S(1)} %get-tuple-element.32), channel_id=1, source_target_pairs={{0,1},{1,0},{2,3},{3,2},{4,5},{5,4},{6,7},{7,6},{8,9},{9,8},{10,11... | collective-permute-start | bytes 30728 | tf_op jit(solution)/shard_map/ppermute | solution.py:272
  7.8 1.9 %copy-start = (bf16[512,3072]{1,0:T(8,128)(2,1)S(1)}, bf16[512,3072]{1,0:T(8,128)(2,1)}, u32[]{:S(2)}) copy-start(bf16[512,3072]{1,0:T(8,128)(2,1)} %weight.1) | copy-start | bytes 9437188
  11.8 8.9 %collective-permute-start.5 = (bf16[808,128]{1,0:T(8,128)(2,1)S(1)}, bf16[808,128]{1,0:T(8,128)(2,1)S(1)}, u32[]{:S(2)}, u32[]{:S(2)}) collective-permute-start(bf16[808,128]{1,0:T(8,128)(2,1)S(1)} %collective-permute-done.1.arrived), channel_id=1, source_target_pairs={{2,0},{6,2},{4,6},{0,4},{3,1},{7,3},{5,7},{1,5},{10,8},{14,10},{12... | collective-permute-start | bytes 620552 | tf_op jit(solution)/shard_map/ppermute | solution.py:312
  18.6 7.6 %collective-permute-start.4 = (bf16[96,1024]{1,0:T(8,128)(2,1)S(1)}, bf16[96,1024]{1,0:T(8,128)(2,1)S(1)}, u32[]{:S(2)}, u32[]{:S(2)}) collective-permute-start(bf16[96,1024]{1,0:T(8,128)(2,1)S(1)} %collective-permute-done.second), channel_id=1, source_target_pairs={{2,0},{6,2},{4,6},{0,4},{3,1},{7,3},{5,7},{1,5},{10,8},{14,10},{12... | collective-permute-start | bytes 589832 | tf_op jit(solution)/shard_map/ppermute | solution.py:313
  19.4 4.7 %collective-permute-start.6 = (bf16[40,128]{1,0:T(8,128)(2,1)S(1)}, bf16[40,128]{1,0:T(8,128)(2,1)S(1)}, u32[]{:S(2)}, u32[]{:S(2)}) collective-permute-start(bf16[40,128]{1,0:T(8,128)(2,1)S(1)} %slice.9), channel_id=1, source_target_pairs={{0,1},{1,0},{2,3},{3,2},{4,5},{5,4},{6,7},{7,6},{8,9},{9,8},{10,11... | collective-permute-start | bytes 30728 | tf_op jit(solution)/shard_map/ppermute | solution.py:272
  20.7 9.9 %collective-permute-start.8 = (bf16[808,128]{1,0:T(8,128)(2,1)S(1)}, bf16[808,128]{1,0:T(8,128)(2,1)S(1)}, u32[]{:S(2)}, u32[]{:S(2)}) collective-permute-start(bf16[808,128]{1,0:T(8,128)(2,1)S(1)} %collective-permute-done.5.first), channel_id=1, source_target_pairs={{2,0},{6,2},{4,6},{0,4},{3,1},{7,3},{5,7},{1,5},{10,8},{14,10},{12... | collective-permute-start | bytes 620552 | tf_op jit(solution)/shard_map/ppermute | solution.py:312
  26.1 6.8 %collective-permute-start.7 = (bf16[96,1024]{1,0:T(8,128)(2,1)S(1)}, bf16[96,1024]{1,0:T(8,128)(2,1)S(1)}, u32[]{:S(2)}, u32[]{:S(2)}) collective-permute-start(bf16[96,1024]{1,0:T(8,128)(2,1)S(1)} %collective-permute-done.4.second), channel_id=1, source_target_pairs={{2,0},{6,2},{4,6},{0,4},{3,1},{7,3},{5,7},{1,5},{10,8},{14,10},{12... | collective-permute-start | bytes 589832 | tf_op jit(solution)/shard_map/ppermute | solution.py:313
  28.3 2.3 %collective-permute-start.10 = (bf16[40,128]{1,0:T(8,128)(2,1)S(1)}, bf16[40,128]{1,0:T(8,128)(2,1)S(1)}, u32[]{:S(2)}, u32[]{:S(2)}) collective-permute-start(bf16[40,128]{1,0:T(8,128)(2,1)S(1)} %slice.13), channel_id=1, source_target_pairs={{0,1},{1,0},{2,3},{3,2},{4,5},{5,4},{6,7},{7,6},{8,9},{9,8},{10,11... | collective-permute-start | bytes 30728 | tf_op jit(solution)/shard_map/ppermute | solution.py:272
  30.6 2.4 %copy-start.1 = (bf16[512,1024]{1,0:T(8,128)(2,1)S(1)}, bf16[512,1024]{1,0:T(8,128)(2,1)}, u32[]{:S(2)}) copy-start(bf16[512,1024]{1,0:T(8,128)(2,1)} %out_here.1) | copy-start | bytes 3145732
  30.6 2.4 %collective-permute-start.9 = (bf16[40,128]{1,0:T(8,128)(2,1)S(1)}, bf16[40,128]{1,0:T(8,128)(2,1)S(1)}, u32[]{:S(2)}, u32[]{:S(2)}) collective-permute-start(bf16[40,128]{1,0:T(8,128)(2,1)S(1)} %slice.12), channel_id=1, source_target_pairs={{0,1},{1,0},{2,3},{3,2},{4,5},{5,4},{6,7},{7,6},{8,9},{9,8},{10,11... | collective-permute-start | bytes 30728 | tf_op jit(solution)/shard_map/ppermute | solution.py:272

commit v9 on v7

--- a/solution.py
+++ b/solution.py
@@ -159,9 +159,9 @@
     for pair in range(PAIRS):
         if pair + 2 < PAIRS:
             score(pair + 2)
-        weigh(pair)
         if pair >= 1:
             attend(pair - 1)
+        weigh(pair)
     attend(PAIRS - 1)
 
 

time: 35.9 us -> 35.9 us (level)
  no operation moved by 1% of the time
where the time goes in v9:
time: 35.9 us; the launch traced here: 35.8 us
  starting transfers between devices  15.9 us (44%)
  Pallas kernels  13.9 us (39%)
  waiting for transfers between devices  3.92 us (11%)
  local copies, waits for them, and re-layouts  1.9 us (5%)
    ppermute x3, starting transfers between devices, shards(): next_first = lax.ppermute(first, 'peak', pairs)  10.8 us
    pallas_call x5, Pallas kernels, call(): pl.pallas_call(kernel, out_shape=shapes, in_specs=[spec] * len(operands),...  9.47 us
    ppermute x3, starting transfers between devices, shards(): next_second = lax.ppermute(second, 'peak', pairs)  4.54 us
    ppermute x3, waiting for transfers between devices, shards(): next_first = lax.ppermute(first, 'peak', pairs)  3.57 us
    pallas_call x1, Pallas kernels, shards(): pl.pallas_call(last_kernel, out_shape=[jax.ShapeDtypeStruct((tokens, widt...  2.83 us
    unnamed x4, local copies, waits for them, and re-layouts  1.89 us
    pallas_call x1, Pallas kernels, shards(): pl.pallas_call(embed_kernel, out_shape=[jax.ShapeDtypeStruct((cut * width...  1.64 us
  transfers between devices with their start and end apart: 12, of which 3 were waited for; matrix products, arithmetic and copies ran while one was open for 0% of the time, Pallas kernels for 31%

profile of v9, /device:TPU:0, one launch (start us, length us, event | category | flops | bytes accessed | tf_op | source)
XLA Modules:
  0.0 35.8 jit_solution(2594462340531655154)
XLA Ops:
  0.0 0.5 %collective-permute-start.3 = (bf16[512,3072]{1,0:T(8,128)(2,1)}, bf16[512,3072]{1,0:T(8,128)(2,1)S(1)}, u32[]{:S(2)}, u32[]{:S(2)}) collective-permute-start(bf16[512,3072]{1,0:T(8,128)(2,1)} %weight.1), channel_id=1, source_target_pairs={{0,1},{1,0},{2,3},{3,2},{4,5},{5,4},{6,7},{7,6},{8,9},{9,8},{10,11... | collective-permute-start | bytes 9437192 | tf_op jit(solution)/shard_map/ppermute | solution.py:271
  0.5 0.1 collective-permute-start.11
  0.5 1.6 %shard_map.82 = (bf16[808,128]{1,0:T(8,128)(2,1)S(1)}, bf16[96,1024]{1,0:T(8,128)(2,1)S(1)}, bf16[40,128]{1,0:T(8,128)(2,1)S(1)}) custom-call(bf16[192,1024]{1,0:T(8,128)(2,1)} %bitcast.4, s32[1,192]{1,0:T(1,128)} %refs_1_.1, s32[1,192]{1,0:T(1,128)} %refs_2_.1, s32[1,192]{1,0:T(1,128)} %bitcast.6, bf16[51,1024]{1,0:T(8,128)(2,1)} %bitcast.5, ...), custom_call_target="tpu_custom_call" | custom-call | flops 1048576 | bytes 1024 | tf_op jit(solution)/shard_map/pallas_call | solution.py:289
  2.2 4.1 %collective-permute-start.1 = (bf16[808,128]{1,0:T(8,128)(2,1)S(1)}, bf16[808,128]{1,0:T(8,128)(2,1)S(1)}, u32[]{:S(2)}, u32[]{:S(2)}) collective-permute-start(bf16[808,128]{1,0:T(8,128)(2,1)S(1)} %get-tuple-element.31.first), channel_id=1, source_target_pairs={{2,0},{6,2},{4,6},{0,4},{3,1},{7,3},{5,7},{1,5},{10,8},{14,10},{12... | collective-permute-start | bytes 620552 | tf_op jit(solution)/shard_map/ppermute | solution.py:311
  6.3 1.6 %collective-permute-start = (bf16[96,1024]{1,0:T(8,128)(2,1)S(1)}, bf16[96,1024]{1,0:T(8,128)(2,1)S(1)}, u32[]{:S(2)}, u32[]{:S(2)}) collective-permute-start(bf16[96,1024]{1,0:T(8,128)(2,1)S(1)} %get-tuple-element.30.second), channel_id=1, source_target_pairs={{2,0},{6,2},{4,6},{0,4},{3,1},{7,3},{5,7},{1,5},{10,8},{14,10},{12... | collective-permute-start | bytes 589832 | tf_op jit(solution)/shard_map/ppermute | solution.py:312
  7.8 0.0 collective-permute-start.2
  7.8 0.0 copy-start
  7.8 1.9 %copy-done = bf16[512,3072]{1,0:T(8,128)(2,1)S(1)} copy-done((bf16[512,3072]{1,0:T(8,128)(2,1)S(1)}, bf16[512,3072]{1,0:T(8,128)(2,1)}, u32[]{:S(2)}) %copy-start) | copy-done | bytes 3145752
  9.7 1.0 %shard_map.83.weight_here = bf16[512,3072]{1,0:T(8,128)(2,1)S(1)} custom-call(bf16[512,3072]{1,0:T(8,128)(2,1)S(1)} %copy-done), custom_call_target="tpu_custom_call" | custom-call | flops 1048576 | bytes 1024 | tf_op jit(solution)/shard_map/pallas_call | solution.py:23
  10.7 0.0 collective-permute-done.3.weight
  10.7 1.0 %shard_map.84.weight_there = bf16[512,3072]{1,0:T(8,128)(2,1)S(1)} custom-call(bf16[512,3072]{1,0:T(8,128)(2,1)S(1)} %collective-permute-done.3.weight), custom_call_target="tpu_custom_call" | custom-call | flops 1048576 | bytes 1024 | tf_op jit(solution)/shard_map/pallas_call | solution.py:23
  11.8 0.0 collective-permute-done.2.summary
  11.8 0.0 collective-permute-done.1.arrived
  11.8 3.4 %collective-permute-start.5 = (bf16[808,128]{1,0:T(8,128)(2,1)S(1)}, bf16[808,128]{1,0:T(8,128)(2,1)S(1)}, u32[]{:S(2)}, u32[]{:S(2)}) collective-permute-start(bf16[808,128]{1,0:T(8,128)(2,1)S(1)} %collective-permute-done.1.arrived), channel_id=1, source_target_pairs={{2,0},{6,2},{4,6},{0,4},{3,1},{7,3},{5,7},{1,5},{10,8},{14,10},{12... | collective-permute-start | bytes 620552 | tf_op jit(solution)/shard_map/ppermute | solution.py:311
  15.1 3.4 %shard_map.85 = (bf16[8,128,384]{2,1,0:T(8,128)(2,1)S(1)}, f32[8,384]{1,0:T(8,128)S(1)}, f32[8,384]{1,0:T(8,128)S(1)}, f32[8,64,384]{2,1,0:T(8,128)S(1)}) custom-call(bf16[808,128]{1,0:T(8,128)(2,1)S(1)} %get-tuple-element.31.first, bf16[96,1024]{1,0:T(8,128)(2,1)S(1)} %get-tuple-element.30.second, bf16[808,128]{1,0:T(8,128)(2,1)S(1)} %collective-permute-done.1.arrived, ...), custom_call_target="tpu_custom_call" | custom-call | flops 268435456 | bytes 1024 | tf_op jit(solution)/shard_map/pallas_call | solution.py:23
  18.5 0.0 collective-permute-done.second
  18.6 0.8 %collective-permute-start.4 = (bf16[96,1024]{1,0:T(8,128)(2,1)S(1)}, bf16[96,1024]{1,0:T(8,128)(2,1)S(1)}, u32[]{:S(2)}, u32[]{:S(2)}) collective-permute-start(bf16[96,1024]{1,0:T(8,128)(2,1)S(1)} %collective-permute-done.second), channel_id=1, source_target_pairs={{2,0},{6,2},{4,6},{0,4},{3,1},{7,3},{5,7},{1,5},{10,8},{14,10},{12... | collective-permute-start | bytes 589832 | tf_op jit(solution)/shard_map/ppermute | solution.py:312
  19.4 0.0 collective-permute-start.6
  19.4 1.4 %collective-permute-done.5.first = bf16[808,128]{1,0:T(8,128)(2,1)S(1)} collective-permute-done((bf16[808,128]{1,0:T(8,128)(2,1)S(1)}, bf16[808,128]{1,0:T(8,128)(2,1)S(1)}, u32[]{:S(2)}, u32[]{:S(2)}) %collective-permute-start.5) | collective-permute-done | bytes 206880 | tf_op jit(solution)/shard_map/ppermute | solution.py:311
  20.7 3.4 %collective-permute-start.8 = (bf16[808,128]{1,0:T(8,128)(2,1)S(1)}, bf16[808,128]{1,0:T(8,128)(2,1)S(1)}, u32[]{:S(2)}, u32[]{:S(2)}) collective-permute-start(bf16[808,128]{1,0:T(8,128)(2,1)S(1)} %collective-permute-done.5.first), channel_id=1, source_target_pairs={{2,0},{6,2},{4,6},{0,4},{3,1},{7,3},{5,7},{1,5},{10,8},{14,10},{12... | collective-permute-start | bytes 620552 | tf_op jit(solution)/shard_map/ppermute | solution.py:311
  24.1 0.0 collective-permute-done.6.summary
  24.1 2.0 %shard_map.86 = (f32[8,384]{1,0:T(8,128)S(1)}, f32[8,384]{1,0:T(8,128)S(1)}, f32[8,64,384]{2,1,0:T(8,128)S(1)}) custom-call(bf16[96,1024]{1,0:T(8,128)(2,1)S(1)} %collective-permute-done.second, bf16[808,128]{1,0:T(8,128)(2,1)S(1)} %collective-permute-done.5.first, bf16[40,128]{1,0:T(8,128)(2,1)S(1)} %collective-permute-done.6.summary, ...), custom_call_target="tpu_custom_call" | custom-call | flops 268435456 | bytes 1024 | tf_op jit(solution)/shard_map/pallas_call | solution.py:23
  26.1 0.0 collective-permute-done.4.second
  26.1 2.2 %collective-permute-start.7 = (bf16[96,1024]{1,0:T(8,128)(2,1)S(1)}, bf16[96,1024]{1,0:T(8,128)(2,1)S(1)}, u32[]{:S(2)}, u32[]{:S(2)}) collective-permute-start(bf16[96,1024]{1,0:T(8,128)(2,1)S(1)} %collective-permute-done.4.second), channel_id=1, source_target_pairs={{2,0},{6,2},{4,6},{0,4},{3,1},{7,3},{5,7},{1,5},{10,8},{14,10},{12... | collective-permute-start | bytes 589832 | tf_op jit(solution)/shard_map/ppermute | solution.py:312
  28.3 0.0 collective-permute-start.10
  28.3 2.2 %collective-permute-done.8.first = bf16[808,128]{1,0:T(8,128)(2,1)S(1)} collective-permute-done((bf16[808,128]{1,0:T(8,128)(2,1)S(1)}, bf16[808,128]{1,0:T(8,128)(2,1)S(1)}, u32[]{:S(2)}, u32[]{:S(2)}) %collective-permute-start.8) | collective-permute-done | bytes 206880 | tf_op jit(solution)/shard_map/ppermute | solution.py:311
  30.5 0.0 copy-start.1
  30.5 0.0 collective-permute-start.9
  30.5 0.0 collective-permute-done.10.summary
  30.6 2.0 %shard_map.87 = (f32[8,384]{1,0:T(8,128)S(1)}, f32[8,384]{1,0:T(8,128)S(1)}, f32[8,64,384]{2,1,0:T(8,128)S(1)}) custom-call(bf16[96,1024]{1,0:T(8,128)(2,1)S(1)} %collective-permute-done.4.second, bf16[808,128]{1,0:T(8,128)(2,1)S(1)} %collective-permute-done.8.first, bf16[40,128]{1,0:T(8,128)(2,1)S(1)} %collective-permute-done.10.summary, ...), custom_call_target="tpu_custom_call" | custom-call | flops 268435456 | bytes 1024 | tf_op jit(solution)/shard_map/pallas_call | solution.py:23
  32.6 0.0 collective-permute-done.11.out_there
  32.6 0.3 collective-permute-done.7.second
  32.9 0.0 collective-permute-done.9.summary
  32.9 0.0 copy-done.1
  32.9 2.8 %shard_map.88 = bf16[192,1024]{1,0:T(8,128)(2,1)} custom-call(bf16[96,1024]{1,0:T(8,128)(2,1)S(1)} %collective-permute-done.7.second, bf16[40,128]{1,0:T(8,128)(2,1)S(1)} %collective-permute-done.9.summary, bf16[512,3072]{1,0:T(8,128)(2,1)S(1)} %shard_map.83.weight_here, bf16[512,3072]{1,0:T(8,128)(2,1)S(1)} %shard_map.84.weight_there, ...), custom_call_target="tpu_custom_call" | custom-call | flops 1048576 | bytes 1024 | tf_op jit(solution)/shard_map/pallas_call | solution.py:328
  (3 shorter events, 0.0 us)
Async XLA Ops:
  0.0 10.7 %collective-permute-start.3 = (bf16[512,3072]{1,0:T(8,128)(2,1)}, bf16[512,3072]{1,0:T(8,128)(2,1)S(1)}, u32[]{:S(2)}, u32[]{:S(2)}) collective-permute-start(bf16[512,3072]{1,0:T(8,128)(2,1)} %weight.1), channel_id=1, source_target_pairs={{0,1},{1,0},{2,3},{3,2},{4,5},{5,4},{6,7},{7,6},{8,9},{9,8},{10,11... | collective-permute-start | bytes 9437192 | tf_op jit(solution)/shard_map/ppermute | solution.py:271
  0.5 32.1 %collective-permute-start.11 = (bf16[512,1024]{1,0:T(8,128)(2,1)}, bf16[512,1024]{1,0:T(8,128)(2,1)S(1)}, u32[]{:S(2)}, u32[]{:S(2)}) collective-permute-start(bf16[512,1024]{1,0:T(8,128)(2,1)} %out_here.1), channel_id=1, source_target_pairs={{0,1},{1,0},{2,3},{3,2},{4,5},{5,4},{6,7},{7,6},{8,9},{9,8},{10,11... | collective-permute-start | bytes 3145736 | tf_op jit(solution)/shard_map/ppermute | solution.py:271
  2.2 9.6 %collective-permute-start.1 = (bf16[808,128]{1,0:T(8,128)(2,1)S(1)}, bf16[808,128]{1,0:T(8,128)(2,1)S(1)}, u32[]{:S(2)}, u32[]{:S(2)}) collective-permute-start(bf16[808,128]{1,0:T(8,128)(2,1)S(1)} %get-tuple-element.31.first), channel_id=1, source_target_pairs={{2,0},{6,2},{4,6},{0,4},{3,1},{7,3},{5,7},{1,5},{10,8},{14,10},{12... | collective-permute-start | bytes 620552 | tf_op jit(solution)/shard_map/ppermute | solution.py:311
  6.3 12.3 %collective-permute-start = (bf16[96,1024]{1,0:T(8,128)(2,1)S(1)}, bf16[96,1024]{1,0:T(8,128)(2,1)S(1)}, u32[]{:S(2)}, u32[]{:S(2)}) collective-permute-start(bf16[96,1024]{1,0:T(8,128)(2,1)S(1)} %get-tuple-element.30.second), channel_id=1, source_target_pairs={{2,0},{6,2},{4,6},{0,4},{3,1},{7,3},{5,7},{1,5},{10,8},{14,10},{12... | collective-permute-start | bytes 589832 | tf_op jit(solution)/shard_map/ppermute | solution.py:312
  7.8 3.9 %collective-permute-start.2 = (bf16[40,128]{1,0:T(8,128)(2,1)S(1)}, bf16[40,128]{1,0:T(8,128)(2,1)S(1)}, u32[]{:S(2)}, u32[]{:S(2)}) collective-permute-start(bf16[40,128]{1,0:T(8,128)(2,1)S(1)} %get-tuple-element.32), channel_id=1, source_target_pairs={{0,1},{1,0},{2,3},{3,2},{4,5},{5,4},{6,7},{7,6},{8,9},{9,8},{10,11... | collective-permute-start | bytes 30728 | tf_op jit(solution)/shard_map/ppermute | solution.py:271
  7.8 1.9 %copy-start = (bf16[512,3072]{1,0:T(8,128)(2,1)S(1)}, bf16[512,3072]{1,0:T(8,128)(2,1)}, u32[]{:S(2)}) copy-start(bf16[512,3072]{1,0:T(8,128)(2,1)} %weight.1) | copy-start | bytes 9437188
  11.8 8.9 %collective-permute-start.5 = (bf16[808,128]{1,0:T(8,128)(2,1)S(1)}, bf16[808,128]{1,0:T(8,128)(2,1)S(1)}, u32[]{:S(2)}, u32[]{:S(2)}) collective-permute-start(bf16[808,128]{1,0:T(8,128)(2,1)S(1)} %collective-permute-done.1.arrived), channel_id=1, source_target_pairs={{2,0},{6,2},{4,6},{0,4},{3,1},{7,3},{5,7},{1,5},{10,8},{14,10},{12... | collective-permute-start | bytes 620552 | tf_op jit(solution)/shard_map/ppermute | solution.py:311
  18.6 7.6 %collective-permute-start.4 = (bf16[96,1024]{1,0:T(8,128)(2,1)S(1)}, bf16[96,1024]{1,0:T(8,128)(2,1)S(1)}, u32[]{:S(2)}, u32[]{:S(2)}) collective-permute-start(bf16[96,1024]{1,0:T(8,128)(2,1)S(1)} %collective-permute-done.second), channel_id=1, source_target_pairs={{2,0},{6,2},{4,6},{0,4},{3,1},{7,3},{5,7},{1,5},{10,8},{14,10},{12... | collective-permute-start | bytes 589832 | tf_op jit(solution)/shard_map/ppermute | solution.py:312
  19.4 4.7 %collective-permute-start.6 = (bf16[40,128]{1,0:T(8,128)(2,1)S(1)}, bf16[40,128]{1,0:T(8,128)(2,1)S(1)}, u32[]{:S(2)}, u32[]{:S(2)}) collective-permute-start(bf16[40,128]{1,0:T(8,128)(2,1)S(1)} %slice.9), channel_id=1, source_target_pairs={{0,1},{1,0},{2,3},{3,2},{4,5},{5,4},{6,7},{7,6},{8,9},{9,8},{10,11... | collective-permute-start | bytes 30728 | tf_op jit(solution)/shard_map/ppermute | solution.py:271
  20.7 9.8 %collective-permute-start.8 = (bf16[808,128]{1,0:T(8,128)(2,1)S(1)}, bf16[808,128]{1,0:T(8,128)(2,1)S(1)}, u32[]{:S(2)}, u32[]{:S(2)}) collective-permute-start(bf16[808,128]{1,0:T(8,128)(2,1)S(1)} %collective-permute-done.5.first), channel_id=1, source_target_pairs={{2,0},{6,2},{4,6},{0,4},{3,1},{7,3},{5,7},{1,5},{10,8},{14,10},{12... | collective-permute-start | bytes 620552 | tf_op jit(solution)/shard_map/ppermute | solution.py:311
  26.1 6.8 %collective-permute-start.7 = (bf16[96,1024]{1,0:T(8,128)(2,1)S(1)}, bf16[96,1024]{1,0:T(8,128)(2,1)S(1)}, u32[]{:S(2)}, u32[]{:S(2)}) collective-permute-start(bf16[96,1024]{1,0:T(8,128)(2,1)S(1)} %collective-permute-done.4.second), channel_id=1, source_target_pairs={{2,0},{6,2},{4,6},{0,4},{3,1},{7,3},{5,7},{1,5},{10,8},{14,10},{12... | collective-permute-start | bytes 589832 | tf_op jit(solution)/shard_map/ppermute | solution.py:312
  28.3 2.2 %collective-permute-start.10 = (bf16[40,128]{1,0:T(8,128)(2,1)S(1)}, bf16[40,128]{1,0:T(8,128)(2,1)S(1)}, u32[]{:S(2)}, u32[]{:S(2)}) collective-permute-start(bf16[40,128]{1,0:T(8,128)(2,1)S(1)} %slice.13), channel_id=1, source_target_pairs={{0,1},{1,0},{2,3},{3,2},{4,5},{5,4},{6,7},{7,6},{8,9},{9,8},{10,11... | collective-permute-start | bytes 30728 | tf_op jit(solution)/shard_map/ppermute | solution.py:271
  30.5 2.4 %copy-start.1 = (bf16[512,1024]{1,0:T(8,128)(2,1)S(1)}, bf16[512,1024]{1,0:T(8,128)(2,1)}, u32[]{:S(2)}) copy-start(bf16[512,1024]{1,0:T(8,128)(2,1)} %out_here.1) | copy-start | bytes 3145732
  30.5 2.4 %collective-permute-start.9 = (bf16[40,128]{1,0:T(8,128)(2,1)S(1)}, bf16[40,128]{1,0:T(8,128)(2,1)S(1)}, u32[]{:S(2)}, u32[]{:S(2)}) collective-permute-start(bf16[40,128]{1,0:T(8,128)(2,1)S(1)} %slice.12), channel_id=1, source_target_pairs={{0,1},{1,0},{2,3},{3,2},{4,5},{5,4},{6,7},{7,6},{8,9},{9,8},{10,11... | collective-permute-start | bytes 30728 | tf_op jit(solution)/shard_map/ppermute | solution.py:271
